TPU v7x, 32 devices: a whole 2x2x4 slice. The times are simulated.
32 devices in a mesh: fsdp: 16 (over z, y, core), seq: 2 (over x).
Axes of the slice: x: 2, y: 2, z: 4, core: 2. Of those that a mesh axis runs over, the one named last changes fastest.
Arguments:
- inputs: bfloat16 [16, 1024, 1280], P('fsdp', 'seq'), may hold values from -6 to 6
- row_ids: int32 [16, 1024], P('fsdp', 'seq'), may hold values from 0 to 31
- col_ids: int32 [16, 1024], P('fsdp', 'seq'), may hold values from 0 to 31
- norm1_gain: bfloat16 [1280], P('fsdp'), may hold values from 0.5 to 1.5
- norm1_bias: bfloat16 [1280], P('fsdp'), may hold values from -3 to 3
- qkv_weight: bfloat16 [1280, 3840], P('fsdp'), may hold values from -0.15625 to 0.15625
- qkv_bias: bfloat16 [3840], P('fsdp'), may hold values from -3 to 3
- proj_weight: bfloat16 [1280, 1280], P('fsdp'), may hold values from -0.625 to 0.625
- proj_bias: bfloat16 [1280], P('fsdp'), may hold values from -3 to 3
- norm2_gain: bfloat16 [1280], P('fsdp'), may hold values from 0.5 to 1.5
- norm2_bias: bfloat16 [1280], P('fsdp'), may hold values from -3 to 3
- fc1_weight: bfloat16 [1280, 5120], P('fsdp'), may hold values from -0.15625 to 0.15625
- fc1_bias: bfloat16 [5120], P('fsdp'), may hold values from -3 to 3
- fc2_weight: bfloat16 [5120, 1280], P('fsdp'), may hold values from -0.078125 to 0.078125
- fc2_bias: bfloat16 [1280], P('fsdp'), may hold values from -3 to 3
- cotangent: bfloat16 [16, 1024, 1280], P('fsdp', 'seq'), may hold values from -6 to 6
Outputs:
- block_out: bfloat16 [16, 1024, 1280], P('fsdp', 'seq')
- grad_inputs: float32 [16, 1024, 1280], P('fsdp', 'seq')
- grad_norm1_gain: float32 [1280], P('fsdp')
- grad_norm1_bias: float32 [1280], P('fsdp')
- grad_qkv_weight: float32 [1280, 3840], P('fsdp')
- grad_qkv_bias: float32 [2560], P('fsdp')
- grad_value_bias: float32 [1280], P('fsdp')
- grad_proj_weight: float32 [1280, 1280], P('fsdp')
- grad_proj_bias: float32 [1280], P('fsdp')
- grad_norm2_gain: float32 [1280], P('fsdp')
- grad_norm2_bias: float32 [1280], P('fsdp')
- grad_fc1_weight: float32 [1280, 5120], P('fsdp')
- grad_fc1_bias: float32 [5120], P('fsdp')
- grad_fc2_weight: float32 [5120, 1280], P('fsdp')
- grad_fc2_bias: float32 [1280], P('fsdp')
All inputs are finite; a program needn't handle non-finite values.
Results may differ from a plain program's by a relative error of at most 0.015.
Values may be sent and summed in bfloat16 or wider, within the bound.
A program may use at most 320 MiB of HBM per device.

v0:
```python
import jax
import jax.numpy as jnp
from jax import lax
from jax.sharding import PartitionSpec as P

HEADS = 16
HEAD = 80


EPSILON = 1e-06


def normalize(values):
    centered = values - jnp.mean(values, axis=-1, keepdims=True)
    inv_scale = lax.rsqrt(jnp.mean(centered * centered, axis=-1, keepdims=True) + EPSILON)
    return (centered * inv_scale, inv_scale)


def norm_back(grad_norm, normed, inv_scale):
    return inv_scale * (
        grad_norm
        - jnp.mean(grad_norm, axis=-1, keepdims=True)
        - normed * jnp.mean(grad_norm * normed, axis=-1, keepdims=True)
    )


def rotary(row_ids, col_ids, head_size):
    quarter = head_size // 4
    frequency = jnp.power(10000.0, -2.0 * jnp.arange(quarter, dtype=jnp.float32) / (head_size // 2))
    angles = jnp.concatenate(
        [
            row_ids.astype(jnp.float32)[..., None] * frequency,
            col_ids.astype(jnp.float32)[..., None] * frequency,
        ],
        axis=-1,
    )
    angles = jnp.concatenate([angles, angles], axis=-1)
    return (jnp.cos(angles), jnp.sin(angles))


def turned(values):
    half_size = values.shape[-1] // 2
    return jnp.concatenate([-values[..., half_size:], values[..., :half_size]], axis=-1)


def turned_back(values):
    half_size = values.shape[-1] // 2
    return jnp.concatenate([values[..., half_size:], -values[..., :half_size]], axis=-1)


def outer_sum(left_side, right_side):
    return lax.dot_general(
        left_side, right_side, (((0,), (0,)), ((), ())), preferred_element_type=jnp.float32
    )


def against(left_side, right_side):
    return lax.dot_general(
        left_side, right_side, (((1,), (1,)), ((), ())), preferred_element_type=jnp.float32
    )


def patches_last(values):
    return jnp.transpose(values, (1, 2, 0))


def split_blocks(values, query_block):
    heads_here, head_size, image_len = values.shape
    return jnp.transpose(
        values.reshape(heads_here, head_size, image_len // query_block, query_block), (2, 0, 1, 3)
    )


def join_blocks(values):
    block_count, heads_here, head_size, query_block = values.shape
    return jnp.transpose(values, (0, 3, 1, 2)).reshape(
        block_count * query_block, heads_here, head_size
    )


def attend_image(queries, key_rot, values, score_scale, query_block):
    keys_last = patches_last(key_rot)
    values_last = patches_last(values)
    blocks = split_blocks(patches_last(queries), query_block)

    def per_block(block_query):
        scores = (
            jnp.einsum("hdq,hdk->hqk", block_query, keys_last, preferred_element_type=jnp.float32)
            * score_scale
        )
        highest = jnp.max(scores, axis=-1, keepdims=True)
        exponent = jnp.exp(scores - highest)
        totals = jnp.sum(exponent, axis=-1, keepdims=True)
        weights = (exponent / totals).astype(jnp.bfloat16)
        attended = jnp.einsum(
            "hqk,hdk->hdq", weights, values_last, preferred_element_type=jnp.float32
        )
        return (attended, (highest + jnp.log(totals))[..., 0])

    attended, log_total = lax.map(per_block, blocks)
    return (join_blocks(attended), log_total)


def attend_back(queries, key_rot, values, grad_out, log_total, score_scale, query_block):
    keys_last = patches_last(key_rot)
    values_last = patches_last(values)
    blocks = split_blocks(patches_last(queries), query_block)
    grad_blocks = split_blocks(patches_last(grad_out), query_block)

    def per_block(carry, block_entry):
        grad_keys, grad_values = carry
        block_query, block_grad, block_log = block_entry
        scores = (
            jnp.einsum("hdq,hdk->hqk", block_query, keys_last, preferred_element_type=jnp.float32)
            * score_scale
        )
        probs = jnp.exp(scores - block_log[..., None])
        probs_low = probs.astype(jnp.bfloat16)
        grad_probs = jnp.einsum(
            "hdq,hdk->hqk", block_grad, values_last, preferred_element_type=jnp.float32
        )
        inner = jnp.sum(grad_probs * probs, axis=-1, keepdims=True)
        grad_scores = (probs * (grad_probs - inner)).astype(jnp.bfloat16)
        grad_query = (
            jnp.einsum("hqk,hdk->hdq", grad_scores, keys_last, preferred_element_type=jnp.float32)
            * score_scale
        )
        grad_keys = (
            grad_keys
            + jnp.einsum(
                "hqk,hdq->hdk", grad_scores, block_query, preferred_element_type=jnp.float32
            )
            * score_scale
        )
        grad_values = grad_values + jnp.einsum(
            "hqk,hdq->hdk", probs_low, block_grad, preferred_element_type=jnp.float32
        )
        return ((grad_keys, grad_values), grad_query)

    zero_keys = jnp.zeros(keys_last.shape, jnp.float32)
    (grad_keys, grad_values), grad_query = lax.scan(
        per_block, (zero_keys, zero_keys), (blocks, grad_blocks, log_total)
    )
    return (
        join_blocks(grad_query),
        jnp.transpose(grad_keys, (2, 0, 1)),
        jnp.transpose(grad_values, (2, 0, 1)),
    )


def body(
    inputs,
    row_ids,
    col_ids,
    norm1_gain,
    norm1_bias,
    qkv_weight,
    qkv_bias,
    proj_weight,
    proj_bias,
    norm2_gain,
    norm2_bias,
    fc1_weight,
    fc1_bias,
    fc2_weight,
    fc2_bias,
    cotangent,
):
    images, local_len, model_width = inputs.shape
    seq_parts = lax.axis_size("seq")
    image_len = local_len * seq_parts
    heads_here = HEADS // seq_parts
    head_size = model_width // HEADS
    score_scale = HEAD ** (-0.5)
    query_block = min(512, image_len)
    row_count = images * local_len
    cos_table, sin_table = rotary(row_ids, col_ids, head_size)
    cos_table = cos_table[:, :, None, :]
    sin_table = sin_table[:, :, None, :]
    flat_inputs = inputs.astype(jnp.float32).reshape(row_count, model_width)
    shard_set = (
        norm1_gain,
        norm1_bias,
        qkv_weight,
        qkv_bias,
        proj_weight,
        proj_bias,
        norm2_gain,
        norm2_bias,
        fc1_weight,
        fc1_bias,
        fc2_weight,
        fc2_bias,
    )

    def attend_all(image_item):
        return attend_image(
            image_item[:, 0], image_item[:, 1], image_item[:, 2], score_scale, query_block
        )

    def back_all(image_entry):
        spread_now, grad_now, log_now = image_entry
        return attend_back(
            spread_now[:, 0],
            spread_now[:, 1],
            spread_now[:, 2],
            grad_now,
            log_now,
            score_scale,
            query_block,
        )

    def forward(shard_now, flat_now):
        (
            gain_one,
            bias_one,
            w_qkv,
            b_qkv,
            w_proj,
            b_proj,
            gain_two,
            bias_two,
            w_up,
            b_up,
            w_down,
            b_down,
        ) = shard_now
        gathered = (
            lax.all_gather(gain_one, "fsdp", axis=0, tiled=True),
            lax.all_gather(bias_one, "fsdp", axis=0, tiled=True),
            lax.all_gather(w_qkv, "fsdp", axis=0, tiled=True),
            lax.all_gather(b_qkv, "fsdp", axis=0, tiled=True),
            lax.all_gather(w_proj, "fsdp", axis=0, tiled=True),
            lax.all_gather(b_proj, "fsdp", axis=0, tiled=True),
            lax.all_gather(gain_two, "fsdp", axis=0, tiled=True),
            lax.all_gather(bias_two, "fsdp", axis=0, tiled=True),
            lax.all_gather(w_up, "fsdp", axis=0, tiled=True),
            lax.all_gather(b_up, "fsdp", axis=0, tiled=True),
            lax.all_gather(w_down, "fsdp", axis=0, tiled=True),
            lax.all_gather(b_down, "fsdp", axis=0, tiled=True),
        )
        (
            gain_one,
            bias_one,
            w_qkv,
            b_qkv,
            w_proj,
            b_proj,
            gain_two,
            bias_two,
            w_up,
            b_up,
            w_down,
            b_down,
        ) = gathered
        normed_one, inv_one = normalize(flat_now)
        ln_one = (normed_one * gain_one.astype(jnp.float32) + bias_one.astype(jnp.float32)).astype(
            jnp.bfloat16
        )
        qkv_mixed = (
            jnp.dot(ln_one, w_qkv, preferred_element_type=jnp.float32) + b_qkv.astype(jnp.float32)
        ).reshape(images, local_len, 3, HEADS, head_size)
        query_rot = qkv_mixed[:, :, 0] * cos_table + turned(qkv_mixed[:, :, 0]) * sin_table
        key_rot = qkv_mixed[:, :, 1] * cos_table + turned(qkv_mixed[:, :, 1]) * sin_table
        packed = (
            jnp.stack([query_rot, key_rot, qkv_mixed[:, :, 2]], axis=2)
            .astype(jnp.bfloat16)
            .reshape(images, local_len, 3, model_width)
        )
        spread = lax.all_to_all(packed, "seq", split_axis=3, concat_axis=1, tiled=True).reshape(
            images, image_len, 3, heads_here, head_size
        )
        attended, log_total = lax.map(attend_all, spread)
        attn_low = attended.astype(jnp.bfloat16).reshape(images, image_len, heads_here * head_size)
        token_out = lax.all_to_all(
            attn_low, "seq", split_axis=1, concat_axis=2, tiled=True
        ).reshape(row_count, model_width)
        after_attn = flat_now + (
            jnp.dot(token_out, w_proj, preferred_element_type=jnp.float32)
            + b_proj.astype(jnp.float32)
        )
        normed_two, inv_two = normalize(after_attn)
        ln_two = (normed_two * gain_two.astype(jnp.float32) + bias_two.astype(jnp.float32)).astype(
            jnp.bfloat16
        )
        pre_act = jnp.dot(ln_two, w_up, preferred_element_type=jnp.float32) + b_up.astype(
            jnp.float32
        )
        gating = jax.nn.sigmoid(1.702 * pre_act)
        activated = (pre_act * gating).astype(jnp.bfloat16)
        block_out = after_attn + (
            jnp.dot(activated, w_down, preferred_element_type=jnp.float32)
            + b_down.astype(jnp.float32)
        )
        return (
            gathered,
            normed_one,
            inv_one,
            ln_one,
            spread,
            log_total,
            token_out,
            normed_two,
            inv_two,
            ln_two,
            pre_act,
            gating,
            activated,
            block_out,
        )

    saved = forward(shard_set, flat_inputs)
    block_result = saved[13].astype(jnp.bfloat16).reshape(images, local_len, model_width)
    barrier = lax.optimization_barrier((block_result, shard_set, flat_inputs))
    saved = forward(barrier[1], barrier[2])
    (
        gathered,
        normed_one,
        inv_one,
        ln_one,
        spread,
        log_total,
        token_out,
        normed_two,
        inv_two,
        ln_two,
        pre_act,
        gating,
        activated,
        block_out,
    ) = saved
    (
        gain_one,
        bias_one,
        w_qkv,
        b_qkv,
        w_proj,
        b_proj,
        gain_two,
        bias_two,
        w_up,
        b_up,
        w_down,
        b_down,
    ) = gathered
    grad_out = cotangent.astype(jnp.float32).reshape(row_count, model_width)
    grad_down_in = grad_out.astype(jnp.bfloat16)
    grad_fc2_w = outer_sum(activated, grad_down_in)
    grad_fc2_b = jnp.sum(grad_down_in.astype(jnp.float32), axis=0)
    grad_act = against(grad_down_in, w_down)
    grad_pre = (grad_act * (gating + 1.702 * pre_act * gating * (1.0 - gating))).astype(
        jnp.bfloat16
    )
    grad_fc1_w = outer_sum(ln_two, grad_pre)
    grad_fc1_b = jnp.sum(grad_pre.astype(jnp.float32), axis=0)
    grad_ln_two = against(grad_pre, w_up)
    grad_gain_two = jnp.sum(grad_ln_two * normed_two, axis=0)
    grad_bias_two = jnp.sum(grad_ln_two, axis=0)
    grad_after = grad_out + norm_back(
        grad_ln_two * gain_two.astype(jnp.float32), normed_two, inv_two
    )
    grad_proj_in = grad_after.astype(jnp.bfloat16)
    grad_proj_w = outer_sum(token_out, grad_proj_in)
    grad_proj_b = jnp.sum(grad_proj_in.astype(jnp.float32), axis=0)
    grad_attn = (
        against(grad_proj_in, w_proj).astype(jnp.bfloat16).reshape(images, local_len, model_width)
    )
    heads_grad = lax.all_to_all(grad_attn, "seq", split_axis=2, concat_axis=1, tiled=True).reshape(
        images, image_len, heads_here, head_size
    )
    grad_query, grad_key, grad_value = lax.map(back_all, (spread, heads_grad, log_total))
    grad_packed = (
        jnp.stack([grad_query, grad_key, grad_value], axis=2)
        .astype(jnp.bfloat16)
        .reshape(images, image_len, 3, heads_here * head_size)
    )
    tokens_grad = (
        lax.all_to_all(grad_packed, "seq", split_axis=1, concat_axis=3, tiled=True)
        .reshape(images, local_len, 3, HEADS, head_size)
        .astype(jnp.float32)
    )
    grad_q_rot = tokens_grad[:, :, 0]
    grad_k_rot = tokens_grad[:, :, 1]
    grad_q_pre = grad_q_rot * cos_table + turned_back(grad_q_rot * sin_table)
    grad_k_pre = grad_k_rot * cos_table + turned_back(grad_k_rot * sin_table)
    grad_qkv_in = (
        jnp.stack([grad_q_pre, grad_k_pre, tokens_grad[:, :, 2]], axis=2)
        .reshape(row_count, 3 * model_width)
        .astype(jnp.bfloat16)
    )
    grad_qkv_w = outer_sum(ln_one, grad_qkv_in)
    grad_qkv_b = jnp.sum(grad_qkv_in.astype(jnp.float32), axis=0)
    grad_qk_b = grad_qkv_b[: 2 * model_width]
    grad_val_b = grad_qkv_b[2 * model_width :]
    grad_ln_one = against(grad_qkv_in, w_qkv)
    grad_gain_one = jnp.sum(grad_ln_one * normed_one, axis=0)
    grad_bias_one = jnp.sum(grad_ln_one, axis=0)
    grad_inputs = grad_after + norm_back(
        grad_ln_one * gain_one.astype(jnp.float32), normed_one, inv_one
    )
    owned = (
        lax.psum_scatter(grad_gain_one, "fsdp", scatter_dimension=0, tiled=True),
        lax.psum_scatter(grad_bias_one, "fsdp", scatter_dimension=0, tiled=True),
        lax.psum_scatter(grad_qkv_w, "fsdp", scatter_dimension=0, tiled=True),
        lax.psum_scatter(grad_qk_b, "fsdp", scatter_dimension=0, tiled=True),
        lax.psum_scatter(grad_val_b, "fsdp", scatter_dimension=0, tiled=True),
        lax.psum_scatter(grad_proj_w, "fsdp", scatter_dimension=0, tiled=True),
        lax.psum_scatter(grad_proj_b, "fsdp", scatter_dimension=0, tiled=True),
        lax.psum_scatter(grad_gain_two, "fsdp", scatter_dimension=0, tiled=True),
        lax.psum_scatter(grad_bias_two, "fsdp", scatter_dimension=0, tiled=True),
        lax.psum_scatter(grad_fc1_w, "fsdp", scatter_dimension=0, tiled=True),
        lax.psum_scatter(grad_fc1_b, "fsdp", scatter_dimension=0, tiled=True),
        lax.psum_scatter(grad_fc2_w, "fsdp", scatter_dimension=0, tiled=True),
        lax.psum_scatter(grad_fc2_b, "fsdp", scatter_dimension=0, tiled=True),
    )
    sum_a, sum_b, sum_c, sum_d, sum_e, sum_f, sum_g, sum_h, sum_i, sum_j, sum_k, sum_l, sum_m = (
        owned
    )
    summed = lax.psum(
        (sum_a, sum_b, sum_c, sum_d, sum_e, sum_f, sum_g, sum_h, sum_i, sum_j, sum_k, sum_l, sum_m),
        "seq",
    )
    return (
        block_result,
        grad_inputs.reshape(images, local_len, model_width),
        summed[0],
        summed[1],
        summed[2],
        summed[3],
        summed[4],
        summed[5],
        summed[6],
        summed[7],
        summed[8],
        summed[9],
        summed[10],
        summed[11],
        summed[12],
    )


def solution(mesh):
    in_specs = (
        P("fsdp", "seq", None),
        P("fsdp", "seq"),
        P("fsdp", "seq"),
        P("fsdp"),
        P("fsdp"),
        P("fsdp", None),
        P("fsdp"),
        P("fsdp", None),
        P("fsdp"),
        P("fsdp"),
        P("fsdp"),
        P("fsdp", None),
        P("fsdp"),
        P("fsdp", None),
        P("fsdp"),
        P("fsdp", "seq", None),
    )
    out_specs = (
        P("fsdp", "seq", None),
        P("fsdp", "seq", None),
        P("fsdp"),
        P("fsdp"),
        P("fsdp", None),
        P("fsdp"),
        P("fsdp"),
        P("fsdp", None),
        P("fsdp"),
        P("fsdp"),
        P("fsdp"),
        P("fsdp", None),
        P("fsdp"),
        P("fsdp", None),
        P("fsdp"),
    )
    return jax.shard_map(body, mesh=mesh, in_specs=in_specs, out_specs=out_specs, check_vma=False)
```

profile of v0, /device:TPU:0, one launch (start us, length us, event | category | flops | bytes accessed | tf_op | source)
XLA Modules:
  0.0 1964.9 jit_solution(3167938996482446068)
XLA Ops:
  20.1 65.6 %all-reduce.28 = (bf16[3840]{0:T(1024)(128)(2,1)S(1)}, bf16[1280]{0:T(1024)(128)(2,1)S(1)}, bf16[1280]{0:T(1024)(128)(2,1)S(1)}, bf16[1280]{0:T(1024)(128)(2,1)}...) all-reduce(bf16[3840]{0:T(1024)(128)(2,1)S(1)} %dynamic-update-slic, ...), channel_id=1, replica_groups=mesh['fsdp'=16,'seq'=2] {'fsdp'}, use_global_device_ids=true, to_apply=%add.2 | all-reduce | flops 16640 | bytes 66560
  128.2 17.5 copy.84
  151.8 59.4 %all-to-all-done = bf16[1,512,3,1280]{1,2,0,3:T(4,128)(2,1)} async-done(((bf16[1,512,3,1280]{1,2,0,3:T(4,128)(2,1)}), bf16[1,512,3,1280]{1,2,0,3:T(4,128)(2,1)}, u32[]{:S(2)}, u32[]{:S(2)}) %all-to-all-start) | async-done | bytes 3932192 | tf_op jit(solution)/shard_map/all_to_all | solution.py:270
  235.0 35.1 %while.64 = (s32[]{:T(128)}, bf16[2,8,80,512]{3,2,1,0:T(8,128)(2,1)S(1)}, bf16[2,8,80,512]{3,2,1,0:T(8,128)(2,1)S(1)}, bf16[8,80,1024]{2,1,0:T(8,128)(2,1)}, bf16[8,80,1024]{2,1,0:T(8,128)(2,1)}, /*index=5*/s32[]{:T(128)}) while((s32[]{:T(128)}, bf16[2,8,80,512]{3,2,1,0:T(8,128)(2,1)S(1)}, bf16[2,8,80,512]{3,2,1,0:T(8,128)(2,1)S(1)}, ...), condition=%wide.region_5.0_spmd, body=%wide.region_2.5_spmd.sunk | while | flops 1363149824 | bytes 38174796 | solution.py:100
  331.4 22.3 %all-gather.15.cloned.1.call-done = bf16[5120,1280]{1,0:T(8,128)(2,1)} async-done(((bf16[320,1280]{1,0:T(8,128)(2,1)}), bf16[5120,1280]{1,0:T(8,128)(2,1)}) %all-gather.15.cloned.1.call-update) | async-done | bytes 13107216 | tf_op jit(solution)/shard_map/all_gather | solution.py:239
  353.8 25.8 %fusion.74 = bf16[1,512,1280]{2,1,0:T(8,128)(2,1)} fusion(f32[512,1280]{1,0:T(8,128)} %copy-done.13, bf16[5120,1280]{1,0:T(8,128)(2,1)} %all-gather.15.cloned.1.call-done, bf16[1280,5120]{1,0:T(8,128)(2,1)} %all-gather.13.cloned.1.call-done, f32[5120]{0:T(1024)S(1)} %convert_element_type.230, f32[1280]{0:T(1024)S(1)} %convert_element_type.232, ...), kind=kOutput, calls=%fused_computation.94 | convolution fusion | flops 13445365760 | bytes 30186496 | tf_op jit(solution)/shard_map/dot_general | solution.py:292
  383.4 61.7 %all-reduce.27 = (bf16[3840]{0:T(1024)(128)(2,1)S(1)}, bf16[1280]{0:T(1024)(128)(2,1)S(1)}, bf16[1280]{0:T(1024)(128)(2,1)S(1)}, bf16[1280]{0:T(1024)(128)(2,1)}...) all-reduce(bf16[3840]{0:T(1024)(128)(2,1)S(1)} %dynamic-update-slic, ...), channel_id=1, replica_groups=mesh['fsdp'=16,'seq'=2] {'fsdp'}, use_global_device_ids=true, to_apply=%add.10 | all-reduce | flops 15360 | bytes 61440
  445.8 16.7 all-gather.17.cloned.1.call-done
  492.9 17.5 copy.92
  516.6 59.3 %all-to-all-done.2 = bf16[1,512,3,1280]{1,2,0,3:T(4,128)(2,1)} async-done(((bf16[1,512,3,1280]{1,2,0,3:T(4,128)(2,1)}), bf16[1,512,3,1280]{1,2,0,3:T(4,128)(2,1)}, u32[]{:S(2)}, u32[]{:S(2)}) %all-to-all-start.2) | async-done | bytes 3932192 | tf_op jit(solution)/shard_map/all_to_all | solution.py:270
  600.7 25.1 %while.65 = (s32[]{:T(128)}, bf16[2,8,80,512]{3,2,1,0:T(8,128)(2,1)S(1)}, f32[2,8,512]{2,1,0:T(8,128)}, bf16[2,8,80,512]{3,2,1,0:T(8,128)(2,1)}, bf16[8,80,1024]...) while((s32[]{:T(128)}, bf16[2,8,80,512]{3,2,1,0:T(8,128)(2,1)S(1)}, ...), condition=%wide.region_13.14_spmd, body=%wide.region_10.13_spmd.sunk | while | flops 1379921920 | bytes 55051344 | solution.py:100
  649.5 16.2 all-to-all-done.3
  695.0 23.4 %all-gather.21.cloned.1.call-done = bf16[5120,1280]{1,0:T(8,128)(2,1)} async-done(((bf16[320,1280]{1,0:T(8,128)(2,1)}), bf16[5120,1280]{1,0:T(8,128)(2,1)}) %all-gather.21.cloned.1.call-update) | async-done | bytes 13107216 | tf_op jit(solution)/shard_map/all_gather | solution.py:239
  718.4 16.5 convert_reduce_fusion
  734.9 15.2 multiply_reduce_fusion.3
  807.0 96.6 %while.66 = (s32[]{:T(128)}, f32[8,80,1024]{2,1,0:T(8,128)}, f32[8,80,1024]{2,1,0:T(8,128)}, bf16[2,8,80,512]{3,2,1,0:T(8,128)(2,1)}, bf16[2,8,80,512]{3,2,1,0:T...) while((s32[]{:T(128)}, f32[8,80,1024]{2,1,0:T(8,128)}, ...), condition=%wide.region_20.21_spmd.clone, body=%wide.region_18.20_spmd.clone.sunk | while | flops 3409375232 | bytes 282708832 | solution.py:141
  925.0 62.9 %all_to_all.84 = bf16[1,1024,3,640]{3,2,0,1:T(4,128)(2,1)S(1)} all-to-all(bf16[1,1024,3,640]{3,2,0,1:T(4,128)(2,1)} %copy.103), channel_id=1, replica_groups=mesh['fsdp'=16,'seq'=2] {'seq'}, dimensions={1} | all-to-all | bytes 7864320 | tf_op jit(solution)/shard_map/all_to_all | solution.py:378
  1021.4 21.9 %fusion.113 = f32[1280,5120]{1,0:T(8,128)} fusion(bf16[512,5120]{1,0:T(8,128)(2,1)} %get-tuple-element.402, f32[512,1280]{1,0:T(8,128)} %copy-done.10, f32[1280]{0:T(1024)S(1)} %copy-done.47, f32[1280]{0:T(1024)S(1)} %copy-done.31, f32[512]{0:T(512)S(1)} %copy-done.43, f32[512]{0:T(512)S(1)} %copy-done.37), kind=kOutput, calls=%fused_computation.198 | convolution fusion | flops 6714163200 | bytes 34093056 | tf_op jit(solution)/shard_map/dot_general | solution.py:52
  1044.0 16.5 fusion.61
  1074.4 144.2 %reduce-scatter.5.cloned.1.call-done = f32[80,3840]{1,0:T(8,128)} async-done(((f32[1280,3840]{1,0:T(8,128)}), f32[80,3840]{1,0:T(8,128)}) %reduce-scatter.5.cloned.1.call-update) | async-done | bytes 1228816 | tf_op jit(solution)/shard_map/reduce_scatter | solution.py:404
  1218.6 256.2 %reduce-scatter.9.cloned.1.call-done = f32[80,5120]{1,0:T(8,128)} async-done(((f32[1280,5120]{1,0:T(8,128)}), f32[80,5120]{1,0:T(8,128)}) %reduce-scatter.9.cloned.1.call-update) | async-done | bytes 1638416 | tf_op jit(solution)/shard_map/reduce_scatter | solution.py:411
  1474.8 256.1 %reduce-scatter.11.cloned.1.call-done = f32[320,1280]{1,0:T(8,128)} async-done(((f32[5120,1280]{1,0:T(8,128)}), f32[320,1280]{1,0:T(8,128)}) %reduce-scatter.11.cloned.1.call-update) | async-done | bytes 1638416 | tf_op jit(solution)/shard_map/reduce_scatter | solution.py:413
  1737.7 87.6 %all-reduce.32.cloned.1.call-done = (f32[1280]{0:T(1024)}, f32[1280]{0:T(1024)}, f32[2560]{0:T(1024)}, f32[1280]{0:T(1024)}, f32[1280]{0:T(1024)}, /*index=5*/f3...) async-done(((f32[1280]{0:T(1024)}, f32[1280]{0:T(1024)}, f32[2560]{0:T(1024)}, f32[1280]{0:T(1024)}, f32[1280]{0:T(1024)}, /*index=5*/f32[1280]{0:T(1024)}, ...) | async-done | bytes 66576
  1837.9 114.7 %all-reduce.34.cloned.1.call-done = (f32[80,3840]{1,0:T(8,128)}, f32[80,1280]{1,0:T(8,128)}, f32[80,5120]{1,0:T(8,128)}, f32[320,1280]{1,0:T(8,128)}) async-done(((f32[80,3840]{1,0:T(8,128)}, f32[80,1280]{1,0:T(8,128)}, f32[80,5120]{1,0:T(8,128)}, f32[320,1280]{1,0:T(8,128)}), (f32[80,3840]{1,0:T(8,128)}, f32[80,1280]{1,0:T(8,128)}, f32[80,5120]{1,0:T(8,128)}, ...) | async-done | bytes 4915216 | tf_op jit(solution)/shard_map/psum | solution.py:419
  (400 shorter events, 568.0 us)
Async XLA Ops:
  7.2 78.5 %copy-start.56 = (s32[1,512]{1,0:T(1,128)S(1)}, s32[1,512]{1,0:T(1,128)}, u32[]{:S(2)}) copy-start(s32[1,512]{1,0:T(1,128)} %param.23) | copy-start | bytes 6148
  7.2 78.5 %copy-start.57 = (s32[1,512]{1,0:T(1,128)S(1)}, s32[1,512]{1,0:T(1,128)}, u32[]{:S(2)}) copy-start(s32[1,512]{1,0:T(1,128)} %param.24) | copy-start | bytes 6148
  7.2 79.2 %copy-start.12 = (bf16[1,512,1280]{2,1,0:T(8,128)(2,1)S(1)}, bf16[1,512,1280]{2,1,0:T(8,128)(2,1)}, u32[]{:S(2)}) copy-start(bf16[1,512,1280]{2,1,0:T(8,128)(2,1)} %param.22) | copy-start | bytes 3932164
  7.2 90.6 %all-gather.9.cloned.1.call-start = ((), (), s32[]{:S(2)}) async-start(), calls=%async_computation.10 | async-start | bytes 10444800 | tf_op jit(solution)/shard_map/all_gather | solution.py:231
  7.9 316.6 %all-gather.11.cloned.1.call-start = ((), (), s32[]{:S(2)}) async-start(), calls=%async_computation.11 | async-start | bytes 3481600 | tf_op jit(solution)/shard_map/all_gather | solution.py:233
  8.7 322.7 %all-gather.13.cloned.1.call-start = ((), (), s32[]{:S(2)}) async-start(), calls=%async_computation.12 | async-start | bytes 13926400 | tf_op jit(solution)/shard_map/all_gather | solution.py:237
  9.4 344.3 %all-gather.15.cloned.1.call-start = ((), (), s32[]{:S(2)}) async-start(), calls=%async_computation.13 | async-start | bytes 13926400 | tf_op jit(solution)/shard_map/all_gather | solution.py:239
  145.7 65.5 %all-to-all-start = ((bf16[1,512,3,1280]{1,2,0,3:T(4,128)(2,1)}), bf16[1,512,3,1280]{1,2,0,3:T(4,128)(2,1)}, u32[]{:S(2)}, u32[]{:S(2)}) async-start(bf16[1,512,3,1280]{1,2,0,3:T(4,128)(2,1)} %copy.84), calls=%async_computation | async-start | bytes 10485760 | tf_op jit(solution)/shard_map/all_to_all | solution.py:270
  294.2 21.2 %all-to-all-start.1 = ((bf16[2,2,163840]{2,1,0:T(2,128)(2,1)}), bf16[2,2,163840]{2,1,0:T(2,128)(2,1)}, u32[]{:S(2)}, u32[]{:S(2)}) async-start(bf16[2,2,163840]{2,1,0:T(2,128)(2,1)} %reshape.1032), calls=%async_computation.1 | async-start | bytes 2621440 | tf_op jit(solution)/shard_map/all_to_all | solution.py:275
  298.8 163.6 %all-gather.17.cloned.1.call-start = ((), (), s32[]{:S(2)}) async-start(), calls=%async_computation.14 | async-start | bytes 10444800 | tf_op jit(solution)/shard_map/all_gather | solution.py:231
  300.5 161.9 %copy-start.5 = (f32[512,1280]{1,0:T(8,128)}, f32[512,1280]{1,0:T(8,128)S(1)}, u32[]{:S(2)}) copy-start(f32[512,1280]{1,0:T(8,128)S(1)} %convert_bitcast_fusion.1) | copy-start | bytes 7864324
  379.6 294.1 %all-gather.19.cloned.1.call-start = ((), (), s32[]{:S(2)}) async-start(), calls=%async_computation.15 | async-start | bytes 3481600 | tf_op jit(solution)/shard_map/all_gather | solution.py:233
  380.1 299.9 %all-gather.23.cloned.1.call-start = ((), (), s32[]{:S(2)}) async-start(), calls=%async_computation.17 | async-start | bytes 13926400 | tf_op jit(solution)/shard_map/all_gather | solution.py:237
  380.9 337.5 %all-gather.21.cloned.1.call-start = ((), (), s32[]{:S(2)}) async-start(), calls=%async_computation.16 | async-start | bytes 13926400 | tf_op jit(solution)/shard_map/all_gather | solution.py:239
  510.4 65.5 %all-to-all-start.2 = ((bf16[1,512,3,1280]{1,2,0,3:T(4,128)(2,1)}), bf16[1,512,3,1280]{1,2,0,3:T(4,128)(2,1)}, u32[]{:S(2)}, u32[]{:S(2)}) async-start(bf16[1,512,3,1280]{1,2,0,3:T(4,128)(2,1)} %copy.92), calls=%async_computation.2 | async-start | bytes 10485760 | tf_op jit(solution)/shard_map/all_to_all | solution.py:270
  645.8 19.9 %all-to-all-start.3 = ((bf16[2,2,163840]{2,1,0:T(2,128)(2,1)}), bf16[2,2,163840]{2,1,0:T(2,128)(2,1)S(1)}, u32[]{:S(2)}, u32[]{:S(2)}) async-start(bf16[2,2,163840]{2,1,0:T(2,128)(2,1)} %reshape.1034), calls=%async_computation.3 | async-start | bytes 2621440 | tf_op jit(solution)/shard_map/all_to_all | solution.py:275
  649.5 100.7 %copy-start.30 = (f32[1280]{0:T(1024)}, f32[1280]{0:T(1024)S(1)}, u32[]{:S(2)}) copy-start(f32[1280]{0:T(1024)S(1)} %convert_element_type.242) | copy-start | bytes 15364
  776.8 21.7 %all-to-all-start.4 = ((bf16[2,2,163840]{2,1,0:T(2,128)(2,1)}), bf16[2,2,163840]{2,1,0:T(2,128)(2,1)}, u32[]{:S(2)}, u32[]{:S(2)}) async-start(bf16[2,2,163840]{2,1,0:T(2,128)(2,1)} %reshape.1036), calls=%async_computation.4 | async-start | bytes 2621440 | tf_op jit(solution)/shard_map/all_to_all | solution.py:368
  781.3 293.1 %reduce-scatter.7.cloned.1.call-start = ((), (), s32[]{:S(2)}) async-start(), calls=%async_computation.19 | async-start | bytes 6963200 | tf_op jit(solution)/shard_map/reduce_scatter | solution.py:407
  787.4 431.2 %reduce-scatter.5.cloned.1.call-start = ((), (), s32[]{:S(2)}) async-start(), calls=%async_computation.18 | async-start | bytes 20889600 | tf_op jit(solution)/shard_map/reduce_scatter | solution.py:404
  1020.7 454.1 %reduce-scatter.9.cloned.1.call-start = ((), (), s32[]{:S(2)}) async-start(), calls=%async_computation.20 | async-start | bytes 27852800 | tf_op jit(solution)/shard_map/reduce_scatter | solution.py:411
  1043.3 687.6 %reduce-scatter.11.cloned.1.call-start = ((), (), s32[]{:S(2)}) async-start(), calls=%async_computation.21 | async-start | bytes 27852800 | tf_op jit(solution)/shard_map/reduce_scatter | solution.py:413
  1060.6 764.7 %all-reduce.32.cloned.1.call-start = ((), (), s32[]{:S(2)}) async-start(), calls=%async_computation.22 | async-start | bytes 180224
  1074.3 878.2 %all-reduce.34.cloned.1.call-start = ((), (), s32[]{:S(2)}) async-start(), calls=%async_computation.23 | async-start | bytes 9830400 | tf_op jit(solution)/shard_map/psum | solution.py:419
  (76 other events, 1151.5 us)
Sparse Core Ops, SparseCore 0:
  10.3 87.4 all-gather.8
  100.1 44.1 all-gather.10
  146.5 102.8 all-gather.12
  251.6 102.1 all-gather.14
  379.7 82.6 all-gather.16
  464.6 44.0 all-gather.18
  511.0 102.8 all-gather.22
  616.2 102.1 all-gather.20
  787.5 85.5 reduce-scatter.6
  1020.8 197.7 reduce-scatter.4
  1223.3 251.4 reduce-scatter.8
  1479.4 251.4 reduce-scatter.10
  1737.4 87.8 all-reduce.31
  1827.8 124.7 all-reduce.33
where the time goes:
time: 1980 us; the launch traced here: 1960 us
  waiting for transfers between devices  1100 us (56%)
  matrix products  296 us (15%)
  local copies, waits for them, and re-layouts  240 us (12%)
  blocking collectives  196 us (10%)
  other arithmetic  90.9 us (5%)
  starting transfers between devices  25.5 us (1%)
    reduce_scatter x1, waiting for transfers between devices, body(): lax.psum_scatter(grad_fc1_w, 'fsdp', scatter_dimension=0, tiled=True)  256 us
    reduce_scatter x1, waiting for transfers between devices, body(): lax.psum_scatter(grad_fc2_w, 'fsdp', scatter_dimension=0, tiled=True)  256 us
    reduce_scatter x1, waiting for transfers between devices, body(): lax.psum_scatter(grad_qkv_w, 'fsdp', scatter_dimension=0, tiled=True)  144 us
    unnamed x2, blocking collectives  127 us
    all_to_all x2, waiting for transfers between devices, forward(): lax.all_to_all(packed, 'seq', split_axis=3, concat_axis=1, tiled=True)  119 us
    psum x1, waiting for transfers between devices, body(): lax.psum((sum_a, sum_b, sum_c, sum_d, sum_e, sum_f, sum_g, sum_h, sum_i,...  115 us
    unnamed x15, waiting for transfers between devices  92.2 us
    all_to_all x1, blocking collectives, body(): lax.all_to_all(grad_packed, 'seq', split_axis=1, concat_axis=3, tiled=True)  62.9 us
  transfers between devices with their start and end apart: 19, of which 14 were waited for; matrix products, arithmetic and copies ran while one was open for 26% of the time, Pallas kernels for 0%

commit v1 on v0

v1 whole, which is shorter than its diff:
```python
import functools

import jax
import jax.numpy as jnp
from jax import lax
from jax.experimental import pallas as pl
from jax.experimental.pallas import tpu as pltpu
from jax.sharding import PartitionSpec as P

HEADS = 16
HEAD = 80
EPSILON = 1e-06
LOG2E = 1.4426950408889634

bf16 = jnp.bfloat16
f32 = jnp.float32


def contract(left, right, left_dim, right_dim):
    return lax.dot_general(
        left, right, (((left_dim,), (right_dim,)), ((), ())), preferred_element_type=f32
    )


def attend_kernel(qkv_ref, cos_ref, sin_ref, rot_ref, probs_ref, out_ref):
    half = HEAD // 2
    scale = HEAD**-0.5 * LOG2E

    def rotate(values):
        turned = jnp.concatenate([-values[half:], values[:half]], axis=0)
        return (values * cos_ref[...] + turned * sin_ref[...]).astype(bf16)

    queries = rotate(qkv_ref[0])
    keys = rotate(qkv_ref[1])
    values = qkv_ref[2].astype(bf16)
    rot_ref[0] = queries
    rot_ref[1] = keys
    rot_ref[2] = values
    scores = contract(keys, queries, 0, 0)
    highest = jnp.max(scores, axis=0, keepdims=True)
    exponent = jnp.exp2(scores * scale - highest * scale)
    totals = jnp.sum(exponent, axis=0, keepdims=True)
    probs = (exponent * (1.0 / totals)).astype(bf16)
    probs_ref[0] = probs
    out_ref[...] = contract(values, probs, 1, 0).astype(bf16)


def attend(qkv_t, cos_t, sin_t):
    _, width, length = qkv_t.shape
    heads = width // HEAD
    part = pl.BlockSpec((3, HEAD, length), lambda h: (0, h, 0))
    table = pl.BlockSpec((HEAD, length), lambda h: (0, 0))
    return pl.pallas_call(
        attend_kernel,
        grid=(heads,),
        in_specs=[part, table, table],
        out_specs=[
            part,
            pl.BlockSpec((1, length, length), lambda h: (h, 0, 0)),
            pl.BlockSpec((HEAD, length), lambda h: (h, 0)),
        ],
        out_shape=[
            jax.ShapeDtypeStruct((3, width, length), bf16),
            jax.ShapeDtypeStruct((heads, length, length), bf16),
            jax.ShapeDtypeStruct((width, length), bf16),
        ],
        compiler_params=pltpu.CompilerParams(vmem_limit_bytes=50 * 2**20),
        cost_estimate=pl.CostEstimate(
            flops=heads * length * length * HEAD * 4 * 5,
            bytes_accessed=heads * length * length * 2 + width * length * 20,
            transcendentals=heads * length * length,
        ),
    )(qkv_t, cos_t, sin_t)


def attend_back_kernel(rot_ref, grad_ref, probs_ref, cos_ref, sin_ref, out_ref, scores_ref):
    half = HEAD // 2
    scale = HEAD**-0.5
    length = probs_ref.shape[1]
    chunk = min(512, length)
    for start in range(0, length, chunk):
        part = slice(start, start + chunk)
        grad_probs = contract(rot_ref[2], grad_ref[:, part], 0, 0)
        probs = probs_ref[0, :, part].astype(f32)
        inner = jnp.sum(grad_probs * probs, axis=0, keepdims=True) / jnp.sum(
            probs, axis=0, keepdims=True
        )
        scores_ref[:, part] = (probs * (grad_probs - inner)).astype(bf16)

    def turn_back(values):
        values = (values * scale).astype(bf16).astype(f32)
        sined = values * sin_ref[...]
        return (
            values * cos_ref[...] + jnp.concatenate([sined[half:], -sined[:half]], axis=0)
        ).astype(bf16)

    grad_scores = scores_ref[...]
    out_ref[0] = turn_back(contract(rot_ref[1], grad_scores, 1, 0))
    out_ref[1] = turn_back(contract(rot_ref[0], grad_scores, 1, 1))
    out_ref[2] = contract(grad_ref[...], probs_ref[0], 1, 1).astype(bf16)


def attend_back(rotated, grad_t, probs, cos_t, sin_t):
    _, width, length = rotated.shape
    heads = width // HEAD
    part = pl.BlockSpec((3, HEAD, length), lambda h: (0, h, 0))
    table = pl.BlockSpec((HEAD, length), lambda h: (0, 0))
    return pl.pallas_call(
        attend_back_kernel,
        grid=(heads,),
        in_specs=[
            part,
            pl.BlockSpec((HEAD, length), lambda h: (h, 0)),
            pl.BlockSpec((1, length, length), lambda h: (h, 0, 0)),
            table,
            table,
        ],
        out_specs=part,
        out_shape=jax.ShapeDtypeStruct((3, width, length), bf16),
        scratch_shapes=[pltpu.VMEM((length, length), bf16)],
        compiler_params=pltpu.CompilerParams(vmem_limit_bytes=50 * 2**20),
        cost_estimate=pl.CostEstimate(
            flops=heads * length * length * HEAD * 8 * 4,
            bytes_accessed=heads * length * length * 2 + width * length * 16,
            transcendentals=0,
        ),
    )(rotated, grad_t, probs, cos_t, sin_t)


class Chain:
    def __init__(self):
        position = lax.axis_index("fsdp")
        self.core = position % 2
        self.y = (position // 2) % 2
        self.z = position // 4
        self.x = lax.axis_index("seq")

    @staticmethod
    def _fsdp(values, move):
        pairs = []
        for z in range(4):
            for y in range(2):
                for core in range(2):
                    to_z, to_y, to_core = move(z, y, core)
                    pairs.append(((z * 2 + y) * 2 + core, (to_z * 2 + to_y) * 2 + to_core))
        return lax.ppermute(values, "fsdp", pairs)

    def swap_x(self, values):
        return lax.ppermute(values, "seq", [(0, 1), (1, 0)])

    def swap_y(self, values):
        return self._fsdp(values, lambda z, y, core: (z, 1 - y, core))

    def swap_core(self, values):
        return self._fsdp(values, lambda z, y, core: (z, y, 1 - core))

    def ring_z(self, values):
        return self._fsdp(values, lambda z, y, core: ((z + 1) % 4, y, core))

    def gather(self, block):
        rows, columns = block.shape
        line = jnp.zeros((4, rows, columns), block.dtype)
        line = lax.dynamic_update_index_in_dim(line, block, self.z, 0)
        moving = block
        for step in range(1, 4):
            moving = self.ring_z(moving)
            line = lax.dynamic_update_index_in_dim(line, moving, (self.z + 4 - step) % 4, 0)
        other = self.swap_y(line)
        line_far = self.swap_core(line)
        other_far = self.swap_core(other)
        full = jnp.zeros((4, 2, 2, rows, columns), block.dtype)
        for part, y, core in (
            (line, self.y, self.core),
            (other, 1 - self.y, self.core),
            (line_far, self.y, 1 - self.core),
            (other_far, 1 - self.y, 1 - self.core),
        ):
            full = lax.dynamic_update_slice(full, part[:, None, None], (0, y, core, 0, 0))
        return full.reshape(16 * rows, columns)

    def scatter(self, whole):
        rows = whole.shape[0] // 16
        columns = whole.shape[1]
        add = lambda a, b: (a.astype(f32) + b.astype(f32)).astype(bf16)
        cut = whole.reshape(8, 2, rows, columns)
        pick = lambda a, index, dim: lax.dynamic_index_in_dim(a, index, dim, keepdims=False)
        half = add(pick(cut, self.core, 1), self.swap_core(pick(cut, 1 - self.core, 1)))
        cut = half.reshape(4, 2, rows, columns)
        line = add(pick(cut, self.y, 1), self.swap_y(pick(cut, 1 - self.y, 1)))
        moving = pick(line, (self.z + 3) % 4, 0)
        for step in range(2, 5):
            moving = add(self.ring_z(moving), pick(line, (self.z + 4 - step) % 4, 0))
        return moving

    def tokens_to_all(self, values):
        return jnp.concatenate([values, self.swap_x(values)], axis=0)

    def ids_to_all(self, ids):
        return jnp.concatenate([ids, self.swap_x(ids)], axis=1)

    def tokens_sum(self, product):
        away = self.swap_x(product(1).astype(bf16))
        return product(0) + away.astype(f32)

    def heads_to_all(self, attended):
        other = self.swap_x(attended)
        length = other.shape[1] // 2
        other = jnp.concatenate([other[:, length:], other[:, :length]], axis=1)
        first = self.x == 0
        return jnp.concatenate(
            [jnp.where(first, attended, other), jnp.where(first, other, attended)], axis=0
        )

    def features_to_heads(self, grad_t):
        cut = grad_t.reshape(2, grad_t.shape[0] // 2, grad_t.shape[1])
        own = lax.dynamic_index_in_dim(cut, self.x, 0, keepdims=False)
        away = lax.dynamic_index_in_dim(cut, 1 - self.x, 0, keepdims=False)
        return jnp.concatenate([own, self.swap_x(away)], axis=1)

    def seq_parts(self, values):
        other = self.swap_x(values)
        first = self.x == 0
        return jnp.stack([jnp.where(first, values, other), jnp.where(first, other, values)])

    def seq_sum(self, values):
        return values.astype(f32) + self.swap_x(values).astype(f32)

    def sum_all(self, vector):
        vector = vector + self.swap_core(vector)
        vector = vector + self._fsdp(vector, lambda z, y, core: (z, 1 - y, core))
        vector = vector + self._fsdp(vector, lambda z, y, core: (z ^ 1, y, core))
        vector = vector + self._fsdp(vector, lambda z, y, core: (z ^ 2, y, core))
        return vector + self.swap_x(vector)


class Plain:
    def __init__(self):
        self.x = lax.axis_index("seq")

    def gather(self, block):
        return lax.all_gather(block, "fsdp", axis=0, tiled=True)

    def scatter(self, whole):
        return lax.psum_scatter(whole, "fsdp", scatter_dimension=0, tiled=True)

    def tokens_to_all(self, values):
        return lax.all_gather(values, "seq", axis=0, tiled=True)

    def ids_to_all(self, ids):
        return lax.all_gather(ids, "seq", axis=1, tiled=True)

    def tokens_sum(self, product):
        return lax.psum_scatter(product(None), "seq", scatter_dimension=0, tiled=True)

    def heads_to_all(self, attended):
        return lax.all_gather(attended, "seq", axis=0, tiled=True)

    def features_to_heads(self, grad_t):
        return lax.all_to_all(grad_t, "seq", split_axis=0, concat_axis=1, tiled=True)

    def seq_parts(self, values):
        return lax.all_gather(values, "seq", axis=0)

    def seq_sum(self, values):
        return lax.psum(values.astype(f32), "seq")

    def sum_all(self, vector):
        return lax.psum(vector, ("fsdp", "seq"))


def normalize(values):
    centered = values - jnp.mean(values, axis=-1, keepdims=True)
    inv_scale = lax.rsqrt(jnp.mean(centered * centered, axis=-1, keepdims=True) + EPSILON)
    return (centered * inv_scale, inv_scale)


def norm_back(grad_norm, normed, inv_scale):
    return inv_scale * (
        grad_norm
        - jnp.mean(grad_norm, axis=-1, keepdims=True)
        - normed * jnp.mean(grad_norm * normed, axis=-1, keepdims=True)
    )


def rotary(ids, head_size):
    quarter = head_size // 4
    frequency = jnp.power(10000.0, -2.0 * jnp.arange(quarter, dtype=f32) / (head_size // 2))
    angles = (ids.astype(f32)[:, None, :] * frequency[None, :, None]).reshape(
        2 * quarter, ids.shape[1]
    )
    angles = jnp.concatenate([angles, angles], axis=0)
    return (jnp.cos(angles), jnp.sin(angles))


def body(
    inputs,
    row_ids,
    col_ids,
    norm1_gain,
    norm1_bias,
    qkv_weight,
    qkv_bias,
    proj_weight,
    proj_bias,
    norm2_gain,
    norm2_bias,
    fc1_weight,
    fc1_bias,
    fc2_weight,
    fc2_bias,
    cotangent,
):
    fsdp, seq = lax.axis_size("fsdp"), lax.axis_size("seq")
    move = Chain() if (fsdp, seq) == (16, 2) else Plain()
    x = move.x
    _, local, width = inputs.shape
    heads = HEADS // seq
    head_size = width // HEADS
    inner = heads * head_size
    rows = width // fsdp
    hidden = fc1_weight.shape[1]
    deep = hidden // fsdp
    cut = deep // seq

    own_in = inputs[0]
    own_grad = cotangent[0]
    all_in = move.tokens_to_all(own_in)
    ids = move.ids_to_all(jnp.concatenate([row_ids, col_ids], axis=0))

    own_part = lambda a, dim: lax.dynamic_index_in_dim(a, x, dim, keepdims=False)
    qkv_block = own_part(qkv_weight.reshape(rows, 3, seq, inner), 2).reshape(rows, 3 * inner)
    fc1_block = own_part(fc1_weight.reshape(rows, fsdp, seq, cut), 2).reshape(rows, fsdp * cut)
    fc2_block = own_part(fc2_weight.reshape(seq, cut, width), 0)

    vectors = (
        norm1_gain,
        norm1_bias,
        proj_bias,
        norm2_gain,
        norm2_bias,
        fc2_bias,
        qkv_bias,
        fc1_bias,
    )
    packed = lax.all_gather(jnp.concatenate(vectors), "fsdp", axis=0).astype(f32)
    whole_vectors = []
    start = 0
    for vector in vectors:
        whole_vectors.append(packed[:, start : start + vector.shape[0]].reshape(-1))
        start += vector.shape[0]
    gain_one, bias_one, b_proj, gain_two, bias_two, b_down, b_qkv, b_up = whole_vectors
    b_qkv = own_part(b_qkv.reshape(3, seq, inner), 1).reshape(-1)
    b_up = own_part(b_up.reshape(fsdp, seq, cut), 1).reshape(-1)

    w_qkv = move.gather(qkv_block)
    w_proj = move.gather(proj_weight)
    w_up = move.gather(fc1_block)
    w_down = move.gather(fc2_block)
    all_grad = move.tokens_to_all(own_grad)

    cos_t, sin_t = rotary(ids, head_size)
    normed_all, _ = normalize(all_in.astype(f32))
    ln_one = (normed_all * gain_one + bias_one).astype(bf16)
    qkv_t = contract(w_qkv, ln_one, 0, 1) + b_qkv[:, None]
    length = qkv_t.shape[1]
    rotated, probs, attended = attend(qkv_t.reshape(3, inner, length), cos_t, sin_t)
    attended = move.heads_to_all(attended)
    after_all = all_in.astype(f32) + (contract(attended, w_proj, 0, 0) + b_proj)
    own_tokens = (
        (lambda a, dim: lax.slice_in_dim(a, 0, local, axis=dim))
        if isinstance(move, Chain)
        else (lambda a, dim: lax.dynamic_slice_in_dim(a, x * local, local, axis=dim))
    )
    after_attn = own_tokens(after_all, 0)
    normed_two_all, _ = normalize(after_all)
    ln_two = (normed_two_all * gain_two + bias_two).astype(bf16)
    pre_act = contract(ln_two, w_up, 1, 0) + b_up
    gating = jax.nn.sigmoid(1.702 * pre_act)
    activated = (pre_act * gating).astype(bf16)
    slope = (gating + 1.702 * pre_act * gating * (1.0 - gating)).astype(bf16)

    def half(values, part):
        return values if part is None else lax.slice_in_dim(values, part * local, (part + 1) * local, axis=0)

    mlp_out = move.tokens_sum(lambda part: contract(half(activated, part), w_down, 1, 0))
    block_out = after_attn + (mlp_out + b_down)

    grad_fc2 = move.scatter(contract(activated, all_grad, 0, 0).astype(bf16))
    grad_pre = (contract(all_grad, w_down, 1, 1) * slope.astype(f32)).astype(bf16)
    grad_ln_two = move.tokens_sum(lambda part: contract(half(grad_pre, part), w_up, 1, 1))
    grad_fc1 = move.scatter(contract(ln_two, grad_pre, 0, 0).astype(bf16))
    normed_two, inv_two = normalize(after_attn)
    grad_out = own_grad.astype(f32)
    grad_after = grad_out + norm_back(grad_ln_two * gain_two, normed_two, inv_two)
    grad_proj_in = grad_after.astype(bf16)

    grad_att = contract(w_proj, grad_proj_in, 1, 1).astype(bf16)
    grad_att = move.features_to_heads(grad_att)
    grad_proj = move.scatter(contract(own_tokens(attended, 1), grad_proj_in, 1, 0).astype(bf16))
    grad_qkv_t = attend_back(rotated, grad_att, probs, cos_t, sin_t).reshape(3 * inner, length)

    def half_t(values, part):
        return values if part is None else lax.slice_in_dim(values, part * local, (part + 1) * local, axis=1)

    grad_ln_one = move.tokens_sum(lambda part: contract(half_t(grad_qkv_t, part), w_qkv, 0, 1))
    grad_qkv = move.scatter(contract(ln_one, grad_qkv_t, 0, 1).astype(bf16))
    normed_one, inv_one = normalize(own_in.astype(f32))
    grad_inputs = grad_after + norm_back(grad_ln_one * gain_one, normed_one, inv_one)

    spread = lambda vector, shape, dim: lax.dynamic_update_index_in_dim(
        jnp.zeros(shape, f32), vector, x, dim
    ).reshape(-1)
    grad_vectors = (
        jnp.sum(grad_ln_one * normed_one, axis=0),
        jnp.sum(grad_ln_one, axis=0),
        jnp.sum(grad_proj_in.astype(f32), axis=0),
        jnp.sum(grad_ln_two * normed_two, axis=0),
        jnp.sum(grad_ln_two, axis=0),
        jnp.sum(grad_out, axis=0),
        spread(
            jnp.sum(grad_qkv_t.astype(f32), axis=1).reshape(3, inner), (3, seq, inner), 1
        ),
        spread(
            jnp.sum(grad_pre.astype(f32), axis=0).reshape(fsdp, cut), (fsdp, seq, cut), 1
        ),
    )
    summed = move.sum_all(jnp.concatenate(grad_vectors))
    position = lax.axis_index("fsdp")
    pieces = []
    start = 0
    for size in (width,) * 6 + (2 * width, width, hidden):
        share = size // fsdp
        pieces.append(lax.dynamic_slice_in_dim(summed, start + position * share, share))
        start += size
    g_gain_one, g_bias_one, g_b_proj, g_gain_two, g_bias_two, g_b_down, g_b_qk, g_b_v, g_b_up = pieces

    g_qkv = jnp.transpose(
        move.seq_parts(grad_qkv.reshape(rows, 3, inner)), (1, 2, 0, 3)
    ).reshape(rows, 3 * width)
    g_fc1 = jnp.transpose(
        move.seq_parts(grad_fc1.reshape(rows, fsdp, cut)), (1, 2, 0, 3)
    ).reshape(rows, hidden)
    g_fc2 = move.seq_parts(grad_fc2).reshape(deep, width)
    g_proj = move.seq_sum(grad_proj)

    return (
        block_out.astype(bf16)[None],
        grad_inputs[None],
        g_gain_one,
        g_bias_one,
        g_qkv.astype(f32),
        g_b_qk,
        g_b_v,
        g_proj,
        g_b_proj,
        g_gain_two,
        g_bias_two,
        g_fc1.astype(f32),
        g_b_up,
        g_fc2.astype(f32),
        g_b_down,
    )


def solution(mesh):
    rows = P("fsdp", None)
    vector = P("fsdp")
    tokens = P("fsdp", "seq", None)
    ids = P("fsdp", "seq")
    in_specs = (
        tokens,
        ids,
        ids,
        vector,
        vector,
        rows,
        vector,
        rows,
        vector,
        vector,
        vector,
        rows,
        vector,
        rows,
        vector,
        tokens,
    )
    out_specs = (
        tokens,
        tokens,
        vector,
        vector,
        rows,
        vector,
        vector,
        rows,
        vector,
        vector,
        vector,
        rows,
        vector,
        rows,
        vector,
    )
    return jax.shard_map(body, mesh=mesh, in_specs=in_specs, out_specs=out_specs, check_vma=False)
```

time: 1980 us -> 749 us (0.38)
  waiting for transfers between devices: 1100 us -> 366 us
  matrix products: 296 us -> 115 us
  local copies, waits for them, and re-layouts: 240 us -> 80.9 us
  blocking collectives: 196 us -> 61.3 us
  other arithmetic: 90.9 us -> 28.2 us
  Pallas kernels: 0 us -> 45.2 us
    reduce_scatter x4 -> x0, waiting for transfers between devices: 657 us -> none  [the longest x1 256 us: body(): lax.psum_scatter(grad_fc1_w, 'fsdp', scatter_dimension=0, tiled=True)]
    ppermute x0 -> x61, waiting for transfers between devices: none -> 366 us  [the longest x48 270 us: _fsdp(): return lax.ppermute(values, 'fsdp', pairs)]
    dot_general x30 -> x15, matrix products: 276 us -> 115 us  [contract(): lax.dot_general(left, right, (((left_dim,), (right_dim,)), ((), ())), pre...]
    all_to_all x5 -> x0, waiting for transfers between devices: 161 us -> none  [the longest x2 119 us: forward(): lax.all_to_all(packed, 'seq', split_axis=3, concat_axis=1, tiled=True)]
    psum x1 -> x0, waiting for transfers between devices: 115 us -> none  [body(): lax.psum((sum_a, sum_b, sum_c, sum_d, sum_e, sum_f, sum_g, sum_h, sum_i,...]
    unnamed x15 -> x0, waiting for transfers between devices: 92.2 us -> none
    all_gather x8 -> x0, waiting for transfers between devices: 73.1 us -> none  [the longest x2 45.8 us: forward(): lax.all_gather(w_down, 'fsdp', axis=0, tiled=True)]
    unnamed x2 -> x1, blocking collectives: 127 us -> 61.3 us
  transfers between devices with their start and end apart: 19 -> 61, of which waited for: 14 -> 31; matrix products, arithmetic and copies ran while one was open for 26% -> 23% of each run, Pallas kernels for 0% -> 6%
where the time goes in v1:
time: 749 us; the launch traced here: 740 us
  waiting for transfers between devices  366 us (49%)
  matrix products  115 us (15%)
  local copies, waits for them, and re-layouts  80.9 us (11%)
  blocking collectives  61.3 us (8%)
  Pallas kernels  45.2 us (6%)
  starting transfers between devices  39.4 us (5%)
  other arithmetic  28.2 us (4%)
    ppermute x48, waiting for transfers between devices, _fsdp(): return lax.ppermute(values, 'fsdp', pairs)  270 us
    dot_general x15, matrix products, contract(): lax.dot_general(left, right, (((left_dim,), (right_dim,)), ((), ())), pre...  115 us
    ppermute x13, waiting for transfers between devices, swap_x(): return lax.ppermute(values, 'seq', [(0, 1), (1, 0)])  96.4 us
    unnamed x1, blocking collectives  61.3 us
    pallas_call x1, Pallas kernels, attend_back(): pl.pallas_call(attend_back_kernel, grid=(heads,), in_specs=[part, pl.Bloc...  26.3 us
    ppermute x48, starting transfers between devices, _fsdp(): return lax.ppermute(values, 'fsdp', pairs)  20.9 us
    pallas_call x1, Pallas kernels, attend(): pl.pallas_call(attend_kernel, grid=(heads,), in_specs=[part, table, table...  18.8 us
    ppermute x13, starting transfers between devices, swap_x(): return lax.ppermute(values, 'seq', [(0, 1), (1, 0)])  18.5 us
  transfers between devices with their start and end apart: 61, of which 31 were waited for; matrix products, arithmetic and copies ran while one was open for 23% of the time, Pallas kernels for 6%

profile of v1, /device:TPU:0, one launch (start us, length us, event | category | flops | bytes accessed | tf_op | source)
XLA Modules:
  0.0 740.1 jit_solution(11953404796680133508)
XLA Ops:
  20.0 61.3 %all-reduce = bf16[16640]{0:T(1024)(128)(2,1)S(1)} all-reduce(bf16[16640]{0:T(1024)(128)(2,1)S(1)} %dynamic-update-slice), channel_id=2, replica_groups=mesh['fsdp'=16,'seq'=2] {'fsdp'}, use_global_device_ids=true, to_apply=%add | all-reduce | flops 16640 | bytes 66560
  100.7 13.7 %collective-permute-done.10 = bf16[80,1280]{1,0:T(8,128)(2,1)S(1)} collective-permute-done((bf16[80,1280]{1,0:T(8,128)(2,1)}, bf16[80,1280]{1,0:T(8,128)(2,1)S(1)}, u32[]{:S(2)}, u32[]{:S(2)}) %collective-permute-start.10) | collective-permute-done | bytes 204832 | tf_op jit(solution)/shard_map/ppermute | solution.py:146
  115.8 13.7 %collective-permute-done.11 = bf16[80,1280]{1,0:T(8,128)(2,1)S(1)} collective-permute-done((bf16[80,1280]{1,0:T(8,128)(2,1)S(1)}, bf16[80,1280]{1,0:T(8,128)(2,1)S(1)}, u32[]{:S(2)}, u32[]{:S(2)}) %collective-permute-start.11) | collective-permute-done | bytes 204832 | tf_op jit(solution)/shard_map/ppermute | solution.py:146
  140.8 9.4 %collective-permute-done.3 = bf16[80,1920]{1,0:T(8,128)(2,1)S(1)} collective-permute-done((bf16[80,1920]{1,0:T(8,128)(2,1)S(1)}, bf16[80,1920]{1,0:T(8,128)(2,1)S(1)}, u32[]{:S(2)}, u32[]{:S(2)}) %collective-permute-start.3) | collective-permute-done | bytes 307232 | tf_op jit(solution)/shard_map/ppermute | solution.py:146
  153.1 10.1 %collective-permute-done.23 = bf16[160,1280]{1,0:T(8,128)(2,1)S(1)} collective-permute-done((bf16[160,1280]{1,0:T(8,128)(2,1)S(1)}, bf16[160,1280]{1,0:T(8,128)(2,1)S(1)}, u32[]{:S(2)}, u32[]{:S(2)}) %collective-permute-start.23) | collective-permute-done | bytes 409632 | tf_op jit(solution)/shard_map/ppermute | solution.py:146
  164.0 9.0 %collective-permute-done.17 = bf16[80,2560]{1,0:T(8,128)(2,1)S(1)} collective-permute-done((bf16[80,2560]{1,0:T(8,128)(2,1)S(1)}, bf16[80,2560]{1,0:T(8,128)(2,1)S(1)}, u32[]{:S(2)}, u32[]{:S(2)}) %collective-permute-start.17) | collective-permute-done | bytes 409632 | tf_op jit(solution)/shard_map/ppermute | solution.py:146
  185.7 26.4 %collective-permute-done.4 = bf16[4,80,1920]{2,1,0:T(8,128)(2,1)S(1)} collective-permute-done((bf16[4,80,1920]{2,1,0:T(8,128)(2,1)}, bf16[4,80,1920]{2,1,0:T(8,128)(2,1)S(1)}, u32[]{:S(2)}, u32[]{:S(2)}) %collective-permute-start.4) | collective-permute-done | bytes 1228832 | tf_op jit(solution)/shard_map/ppermute | solution.py:146
  214.7 32.6 %collective-permute-done.18 = bf16[4,80,2560]{2,1,0:T(8,128)(2,1)S(1)} collective-permute-done((bf16[4,80,2560]{2,1,0:T(8,128)(2,1)}, bf16[4,80,2560]{2,1,0:T(8,128)(2,1)S(1)}, u32[]{:S(2)}, u32[]{:S(2)}) %collective-permute-start.18) | collective-permute-done | bytes 1638432 | tf_op jit(solution)/shard_map/ppermute | solution.py:146
  247.2 34.9 %collective-permute-done.24 = bf16[4,160,1280]{2,1,0:T(8,128)(2,1)} collective-permute-done((bf16[4,160,1280]{2,1,0:T(8,128)(2,1)}, bf16[4,160,1280]{2,1,0:T(8,128)(2,1)}, u32[]{:S(2)}, u32[]{:S(2)}) %collective-permute-start.24) | collective-permute-done | bytes 1638432 | tf_op jit(solution)/shard_map/ppermute | solution.py:146
  287.3 10.0 %broadcast_add_fusion = f32[1920,1024]{1,0:T(8,128)} fusion(f32[1920]{0:T(1024)S(1)} %add.481, bf16[1280,1920]{1,0:T(8,128)(2,1)S(1)} %bitcast.289, f32[1280]{0:T(1024)S(1)} %add.478, f32[1280]{0:T(1024)S(1)} %mul.176, f32[1024]{0:T(1024)S(1)} %add_rsqrt_fusion.1, f32[1024]{0:T(1024)S(1)} %broadcast_multiply_fusion.2, ...), kind=kOutput, calls=%fused_computation.27 | convolution fusion | flops 5046927360 | bytes 15427072 | tf_op jit(solution)/shard_map/dot_general | solution.py:20
  297.2 18.8 %shard_map.271 = (bf16[3,640,1024]{2,1,0:T(8,128)(2,1)}, bf16[8,1024,1024]{2,1,0:T(8,128)(2,1)}, bf16[640,1024]{1,0:T(8,128)(2,1)S(1)}) custom-call(f32[3,640,1024]{2,1,0:T(8,128)} %bitcast.311, f32[80,1024]{1,0:T(8,128)S(1)} %get-tuple-element.47.cos_ref, f32[80,1024]{1,0:T(8,128)S(1)} %get-tuple-element.46.sin_ref), custom_call_target="tpu_custom_call" | custom-call | flops 13421772800 | bytes 29884416 | tf_op jit(solution)/shard_map/pallas_call | solution.py:53
  321.9 24.9 %collective-permute-done.8 = bf16[640,1024]{1,0:T(8,128)(2,1)S(1)} collective-permute-done((bf16[640,1024]{1,0:T(8,128)(2,1)S(1)}, bf16[640,1024]{1,0:T(8,128)(2,1)S(1)}, u32[]{:S(2)}, u32[]{:S(2)}) %collective-permute-start.8) | collective-permute-done | bytes 1310752 | tf_op jit(solution)/shard_map/ppermute | solution.py:149
  354.7 11.6 %multiply_convert_fusion.1 = (bf16[1024,2560]{1,0:T(8,128)(2,1)}, f32[1024,2560]{1,0:T(8,128)}) fusion(f32[2560]{0:T(1024)S(1)} %add.492, bf16[1280,2560]{1,0:T(8,128)(2,1)S(1)} %bitcast.284, f32[1024,1280]{1,0:T(8,128)S(1)} %get-tuple-element.62, f32[1280]{0:T(1024)S(1)} %add.489, f32[1280]{0:T(1024)S(1)} %mul.188, f32[1024]{0:T(1024)S(1)} %add_rsqrt_fusion, ...), kind=kOutput, calls=%fused_computation.5 | convolution fusion | flops 6735790080 | bytes 27553792 | tf_op jit(solution)/shard_map/dot_general | solution.py:20
  366.2 15.9 %convert_reduce_fusion = (f32[2560]{0:T(1024)S(1)}, bf16[1024,2560]{1,0:T(8,128)(2,1)}) fusion(f32[1024,2560]{1,0:T(8,128)} %get-tuple-element.64, f32[2560]{0:T(1024)S(1)} %add.492, bf16[2560,1280]{1,0:T(8,128)(2,1)} %bitcast.49, bf16[512,1280]{1,0:T(8,128)(2,1)} %collective-permute-done.28, bf16[512,1280]{1,0:T(8,128)(2,1)S(1)} %bitcast.307), kind=kOutput, calls=%fused_computation.2 | convolution fusion | flops 6755448320 | bytes 24924160 | tf_op jit(solution)/shard_map/dot_general | solution.py:20
  388.7 9.4 %convolution_convert_fusion.1 = bf16[1280,2560]{1,0:T(8,128)(2,1)} fusion(bf16[1024,2560]{1,0:T(8,128)(2,1)S(1)} %copy-done.53, f32[1024,1280]{1,0:T(8,128)S(1)} %get-tuple-element.62, f32[1280]{0:T(1024)S(1)} %add.489, f32[1280]{0:T(1024)S(1)} %mul.188, f32[1024]{0:T(1024)S(1)} %add_rsqrt_fusion, f32[1024]{0:T(1024)S(1)} %broadcast_multiply_fusion.1), kind=kOutput, calls=%fused_computation.1 | convolution fusion | flops 6720716800 | bytes 17057792 | tf_op jit(solution)/shard_map/dot_general | solution.py:20
  409.2 9.4 %convolution_convert_fusion = bf16[2560,1280]{1,0:T(8,128)(2,1)S(1)} fusion(bf16[1024,2560]{1,0:T(8,128)(2,1)} %get-tuple-element.63, bf16[512,1280]{1,0:T(8,128)(2,1)} %collective-permute-done.28, bf16[512,1280]{1,0:T(8,128)(2,1)S(1)} %bitcast.308), kind=kOutput, calls=%fused_computation | convolution fusion | flops 6719406080 | bytes 14417920 | tf_op jit(solution)/shard_map/dot_general | solution.py:20
  425.4 40.0 %collective-permute-done.29 = bf16[512,1280]{1,0:T(8,128)(2,1)} collective-permute-done((bf16[512,1280]{1,0:T(8,128)(2,1)S(1)}, bf16[512,1280]{1,0:T(8,128)(2,1)}, u32[]{:S(2)}, u32[]{:S(2)}) %collective-permute-start.29) | collective-permute-done | bytes 1310752 | tf_op jit(solution)/shard_map/ppermute | solution.py:149
  490.9 26.3 %shard_map.272 = bf16[3,640,1024]{2,1,0:T(8,128)(2,1)} custom-call(bf16[3,640,1024]{2,1,0:T(8,128)(2,1)} %get-tuple-element.19.rot_ref, bf16[640,1024]{1,0:T(8,128)(2,1)S(1)} %pad_maximum_fusion.7.grad_ref, bf16[8,1024,1024]{2,1,0:T(8,128)(2,1)} %get-tuple-element.20.probs_ref, f32[80,1024]{1,0:T(8,128)S(1)} %get-tuple-element.47.cos_ref, ...), custom_call_target="tpu_custom_call" | custom-call | flops 21474836480 | bytes 27262976 | tf_op jit(solution)/shard_map/pallas_call | solution.py:108
  538.3 14.3 %collective-permute-done.31 = bf16[512,1280]{1,0:T(8,128)(2,1)} collective-permute-done((bf16[512,1280]{1,0:T(8,128)(2,1)}, bf16[512,1280]{1,0:T(8,128)(2,1)}, u32[]{:S(2)}, u32[]{:S(2)}) %collective-permute-start.31) | collective-permute-done | bytes 1310752 | tf_op jit(solution)/shard_map/ppermute | solution.py:149
  568.7 34.7 %collective-permute-done.33 = f32[16640]{0:T(1024)S(1)} collective-permute-done((f32[16640]{0:T(1024)S(1)}, f32[16640]{0:T(1024)S(1)}, u32[]{:S(2)}, u32[]{:S(2)}) %collective-permute-start.33) | collective-permute-done | bytes 66592 | tf_op jit(solution)/shard_map/ppermute | solution.py:146
  635.7 16.5 %collective-permute-done.50 = bf16[4,80,2560]{2,1,0:T(8,128)(2,1)S(1)} collective-permute-done((bf16[4,80,2560]{2,1,0:T(8,128)(2,1)S(1)}, bf16[4,80,2560]{2,1,0:T(8,128)(2,1)S(1)}, u32[]{:S(2)}, u32[]{:S(2)}) %collective-permute-start.50) | collective-permute-done | bytes 1638432 | tf_op jit(solution)/shard_map/ppermute | solution.py:146
  653.7 13.2 %collective-permute-done.51 = bf16[80,2560]{1,0:T(8,128)(2,1)S(1)} collective-permute-done((bf16[80,2560]{1,0:T(8,128)(2,1)S(1)}, bf16[80,2560]{1,0:T(8,128)(2,1)S(1)}, u32[]{:S(2)}, u32[]{:S(2)}) %collective-permute-start.51) | collective-permute-done | bytes 409632 | tf_op jit(solution)/shard_map/ppermute | solution.py:146
  688.3 8.6 %collective-permute-done.59 = bf16[160,1280]{1,0:T(8,128)(2,1)S(1)} collective-permute-done((bf16[160,1280]{1,0:T(8,128)(2,1)S(1)}, bf16[160,1280]{1,0:T(8,128)(2,1)S(1)}, u32[]{:S(2)}, u32[]{:S(2)}) %collective-permute-start.59) | collective-permute-done | bytes 409632 | tf_op jit(solution)/shard_map/ppermute | solution.py:146
  710.2 8.9 %collective-permute-done.54 = bf16[80,16,160]{2,1,0:T(8,128)(2,1)S(1)} collective-permute-done((bf16[80,16,160]{2,1,0:T(8,128)(2,1)S(1)}, bf16[80,16,160]{2,1,0:T(8,128)(2,1)S(1)}, u32[]{:S(2)}, u32[]{:S(2)}) %collective-permute-start.54) | collective-permute-done | bytes 409632 | tf_op jit(solution)/shard_map/ppermute | solution.py:149
  (439 shorter events, 263.2 us)
Async XLA Ops:
  1.4 92.1 %collective-permute-start.7 = (s32[2,512]{1,0:T(2,128)S(1)}, s32[2,512]{1,0:T(2,128)S(1)}, u32[]{:S(2)}, u32[]{:S(2)}) collective-permute-start(s32[2,512]{1,0:T(2,128)S(1)} %pad_add_fusion), channel_id=1, source_target_pairs={{0,1},{1,0},{2,3},{3,2},{4,5},{5,4},{6,7},{7,6},{8,9},{9,8},{10,11... | collective-permute-start | bytes 12296 | tf_op jit(solution)/shard_map/ppermute | solution.py:149
  4.4 91.1 %collective-permute-start.9 = (bf16[80,1280]{1,0:T(8,128)(2,1)}, bf16[80,1280]{1,0:T(8,128)(2,1)}, u32[]{:S(2)}, u32[]{:S(2)}) collective-permute-start(bf16[80,1280]{1,0:T(8,128)(2,1)} %param.23), channel_id=1, source_target_pairs={{0,8},{2,10},{4,12},{6,14},{8,16},{10,18},{12,20},{14,22},{16,24},... | collective-permute-start | bytes 614408 | tf_op jit(solution)/shard_map/ppermute | solution.py:146
  9.4 87.8 %collective-permute-start.1 = (bf16[80,1920]{1,0:T(8,128)(2,1)}, bf16[80,1920]{1,0:T(8,128)(2,1)}, u32[]{:S(2)}, u32[]{:S(2)}) collective-permute-start(bf16[80,1920]{1,0:T(8,128)(2,1)} %bitcast.151), channel_id=1, source_target_pairs={{0,8},{2,10},{4,12},{6,14},{8,16},{10,18},{12,20},{14,22},{16,24},... | collective-permute-start | bytes 921608 | tf_op jit(solution)/shard_map/ppermute | solution.py:146
  16.1 82.8 %collective-permute-start.15 = (bf16[80,2560]{1,0:T(8,128)(2,1)}, bf16[80,2560]{1,0:T(8,128)(2,1)}, u32[]{:S(2)}, u32[]{:S(2)}) collective-permute-start(bf16[80,2560]{1,0:T(8,128)(2,1)} %reshape.264), channel_id=1, source_target_pairs={{0,8},{2,10},{4,12},{6,14},{8,16},{10,18},{12,20},{14,22},{16,24},... | collective-permute-start | bytes 1228808 | tf_op jit(solution)/shard_map/ppermute | solution.py:146
  17.7 348.5 %collective-permute-start.28 = (bf16[512,1280]{1,0:T(8,128)(2,1)}, bf16[512,1280]{1,0:T(8,128)(2,1)}, u32[]{:S(2)}, u32[]{:S(2)}) collective-permute-start(bf16[512,1280]{1,0:T(8,128)(2,1)} %bitcast.306), channel_id=1, source_target_pairs={{0,1},{1,0},{2,3},{3,2},{4,5},{5,4},{6,7},{7,6},{8,9},{9,8},{10,11... | collective-permute-start | bytes 3932168 | tf_op jit(solution)/shard_map/ppermute | solution.py:149
  93.5 88.5 %collective-permute-start = (bf16[512,1280]{1,0:T(8,128)(2,1)S(1)}, bf16[512,1280]{1,0:T(8,128)(2,1)S(1)}, u32[]{:S(2)}, u32[]{:S(2)}) collective-permute-start(bf16[512,1280]{1,0:T(8,128)(2,1)S(1)} %bitcast.260), channel_id=1, source_target_pairs={{0,1},{1,0},{2,3},{3,2},{4,5},{5,4},{6,7},{7,6},{8,9},{9,8},{10,11... | collective-permute-start | bytes 3932168 | tf_op jit(solution)/shard_map/ppermute | solution.py:149
  131.7 53.9 %collective-permute-start.13 = (bf16[4,80,1280]{2,1,0:T(8,128)(2,1)}, bf16[4,80,1280]{2,1,0:T(8,128)(2,1)S(1)}, u32[]{:S(2)}, u32[]{:S(2)}) collective-permute-start(bf16[4,80,1280]{2,1,0:T(8,128)(2,1)} %bitcast_dynamic-update-slice_fusion.25), channel_id=1, source_target_pairs={{0,2},{2,0},{4,6},{6,4},{8,10},{10,8},{12,14},{14,12},{16,18},{18,... | collective-permute-start | bytes 2457608 | tf_op jit(solution)/shard_map/ppermute | solution.py:146
  132.5 50.9 %collective-permute-start.12 = (bf16[4,80,1280]{2,1,0:T(8,128)(2,1)}, bf16[4,80,1280]{2,1,0:T(8,128)(2,1)S(1)}, u32[]{:S(2)}, u32[]{:S(2)}) collective-permute-start(bf16[4,80,1280]{2,1,0:T(8,128)(2,1)} %bitcast_dynamic-update-slice_fusion.25), channel_id=1, source_target_pairs={{0,4},{2,6},{4,0},{6,2},{8,12},{10,14},{12,8},{14,10},{16,20},{18,... | collective-permute-start | bytes 2457608 | tf_op jit(solution)/shard_map/ppermute | solution.py:146
  172.9 39.4 %collective-permute-start.5 = (bf16[4,80,1920]{2,1,0:T(8,128)(2,1)}, bf16[4,80,1920]{2,1,0:T(8,128)(2,1)S(1)}, u32[]{:S(2)}, u32[]{:S(2)}) collective-permute-start(bf16[4,80,1920]{2,1,0:T(8,128)(2,1)} %bitcast_dynamic-update-slice_fusion.22), channel_id=1, source_target_pairs={{0,2},{2,0},{4,6},{6,4},{8,10},{10,8},{12,14},{14,12},{16,18},{18,... | collective-permute-start | bytes 3686408 | tf_op jit(solution)/shard_map/ppermute | solution.py:146
  183.4 63.8 %collective-permute-start.18 = (bf16[4,80,2560]{2,1,0:T(8,128)(2,1)}, bf16[4,80,2560]{2,1,0:T(8,128)(2,1)S(1)}, u32[]{:S(2)}, u32[]{:S(2)}) collective-permute-start(bf16[4,80,2560]{2,1,0:T(8,128)(2,1)} %bitcast_dynamic-update-slice_fusion.19), channel_id=1, source_target_pairs={{0,4},{2,6},{4,0},{6,2},{8,12},{10,14},{12,8},{14,10},{16,20},{18,... | collective-permute-start | bytes 4915208 | tf_op jit(solution)/shard_map/ppermute | solution.py:146
  185.6 96.6 %collective-permute-start.24 = (bf16[4,160,1280]{2,1,0:T(8,128)(2,1)}, bf16[4,160,1280]{2,1,0:T(8,128)(2,1)}, u32[]{:S(2)}, u32[]{:S(2)}) collective-permute-start(bf16[4,160,1280]{2,1,0:T(8,128)(2,1)} %bitcast_dynamic-update-slice_fusion.16), channel_id=1, source_target_pairs={{0,4},{2,6},{4,0},{6,2},{8,12},{10,14},{12,8},{14,10},{16,20},{18,... | collective-permute-start | bytes 4915208 | tf_op jit(solution)/shard_map/ppermute | solution.py:146
  212.3 74.6 %collective-permute-start.19 = (bf16[4,80,2560]{2,1,0:T(8,128)(2,1)}, bf16[4,80,2560]{2,1,0:T(8,128)(2,1)S(1)}, u32[]{:S(2)}, u32[]{:S(2)}) collective-permute-start(bf16[4,80,2560]{2,1,0:T(8,128)(2,1)} %bitcast_dynamic-update-slice_fusion.19), channel_id=1, source_target_pairs={{0,2},{2,0},{4,6},{6,4},{8,10},{10,8},{12,14},{14,12},{16,18},{18,... | collective-permute-start | bytes 4915208 | tf_op jit(solution)/shard_map/ppermute | solution.py:146
  214.4 70.6 %collective-permute-start.25 = (bf16[4,160,1280]{2,1,0:T(8,128)(2,1)}, bf16[4,160,1280]{2,1,0:T(8,128)(2,1)S(1)}, u32[]{:S(2)}, u32[]{:S(2)}) collective-permute-start(bf16[4,160,1280]{2,1,0:T(8,128)(2,1)} %bitcast_dynamic-update-slice_fusion.16), channel_id=1, source_target_pairs={{0,2},{2,0},{4,6},{6,4},{8,10},{10,8},{12,14},{14,12},{16,18},{18,... | collective-permute-start | bytes 4915208 | tf_op jit(solution)/shard_map/ppermute | solution.py:146
  247.2 39.8 %collective-permute-start.6 = (bf16[4,80,1920]{2,1,0:T(8,128)(2,1)S(1)}, bf16[4,80,1920]{2,1,0:T(8,128)(2,1)S(1)}, u32[]{:S(2)}, u32[]{:S(2)}) collective-permute-start(bf16[4,80,1920]{2,1,0:T(8,128)(2,1)S(1)} %collective-permute-done.4), channel_id=1, source_target_pairs={{0,2},{2,0},{4,6},{6,4},{8,10},{10,8},{12,14},{14,12},{16,18},{18,... | collective-permute-start | bytes 3686408 | tf_op jit(solution)/shard_map/ppermute | solution.py:146
  407.2 73.5 %collective-permute-start.27 = (bf16[512,1280]{1,0:T(8,128)(2,1)}, bf16[512,1280]{1,0:T(8,128)(2,1)}, u32[]{:S(2)}, u32[]{:S(2)}) collective-permute-start(bf16[512,1280]{1,0:T(8,128)(2,1)} %convolution_convert_fusion.6), channel_id=1, source_target_pairs={{0,1},{1,0},{2,3},{3,2},{4,5},{5,4},{6,7},{7,6},{8,9},{9,8},{10,11... | collective-permute-start | bytes 3932168 | tf_op jit(solution)/shard_map/ppermute | solution.py:149
  408.7 56.7 %collective-permute-start.29 = (bf16[512,1280]{1,0:T(8,128)(2,1)S(1)}, bf16[512,1280]{1,0:T(8,128)(2,1)}, u32[]{:S(2)}, u32[]{:S(2)}) collective-permute-start(bf16[512,1280]{1,0:T(8,128)(2,1)S(1)} %copy-done.51), channel_id=1, source_target_pairs={{0,1},{1,0},{2,3},{3,2},{4,5},{5,4},{6,7},{7,6},{8,9},{9,8},{10,11... | collective-permute-start | bytes 3932168 | tf_op jit(solution)/shard_map/ppermute | solution.py:149
  422.4 138.3 %collective-permute-start.55 = (bf16[8,160,1280]{2,1,0:T(8,128)(2,1)}, bf16[8,160,1280]{2,1,0:T(8,128)(2,1)}, u32[]{:S(2)}, u32[]{:S(2)}) collective-permute-start(bf16[8,160,1280]{2,1,0:T(8,128)(2,1)} %dynamic-slice_bitcast_fusion), channel_id=1, source_target_pairs={{0,2},{2,0},{4,6},{6,4},{8,10},{10,8},{12,14},{14,12},{16,18},{18,... | collective-permute-start | bytes 9830408 | tf_op jit(solution)/shard_map/ppermute | solution.py:146
  424.3 139.8 %collective-permute-start.49 = (bf16[8,80,2560]{2,1,0:T(8,128)(2,1)}, bf16[8,80,2560]{2,1,0:T(8,128)(2,1)}, u32[]{:S(2)}, u32[]{:S(2)}) collective-permute-start(bf16[8,80,2560]{2,1,0:T(8,128)(2,1)} %dynamic-slice_bitcast_fusion.1), channel_id=1, source_target_pairs={{0,2},{2,0},{4,6},{6,4},{8,10},{10,8},{12,14},{14,12},{16,18},{18,... | collective-permute-start | bytes 9830408 | tf_op jit(solution)/shard_map/ppermute | solution.py:146
  480.7 56.5 %collective-permute-start.43 = (bf16[8,80,1280]{2,1,0:T(8,128)(2,1)}, bf16[8,80,1280]{2,1,0:T(8,128)(2,1)S(1)}, u32[]{:S(2)}, u32[]{:S(2)}) collective-permute-start(bf16[8,80,1280]{2,1,0:T(8,128)(2,1)} %dynamic-slice_bitcast_fusion.5), channel_id=1, source_target_pairs={{0,2},{2,0},{4,6},{6,4},{8,10},{10,8},{12,14},{14,12},{16,18},{18,... | collective-permute-start | bytes 4915208 | tf_op jit(solution)/shard_map/ppermute | solution.py:146
  537.2 92.9 %collective-permute-start.37 = (bf16[8,80,1920]{2,1,0:T(8,128)(2,1)}, bf16[8,80,1920]{2,1,0:T(8,128)(2,1)}, u32[]{:S(2)}, u32[]{:S(2)}) collective-permute-start(bf16[8,80,1920]{2,1,0:T(8,128)(2,1)} %dynamic-slice_bitcast_fusion.2), channel_id=1, source_target_pairs={{0,2},{2,0},{4,6},{6,4},{8,10},{10,8},{12,14},{14,12},{16,18},{18,... | collective-permute-start | bytes 7372808 | tf_op jit(solution)/shard_map/ppermute | solution.py:146
  537.7 65.7 %collective-permute-start.44 = (bf16[4,80,1280]{2,1,0:T(8,128)(2,1)S(1)}, bf16[4,80,1280]{2,1,0:T(8,128)(2,1)S(1)}, u32[]{:S(2)}, u32[]{:S(2)}) collective-permute-start(bf16[4,80,1280]{2,1,0:T(8,128)(2,1)S(1)} %dynamic-slice_bitcast_fusion.7), channel_id=1, source_target_pairs={{0,4},{2,6},{4,0},{6,2},{8,12},{10,14},{12,8},{14,10},{16,20},{18,... | collective-permute-start | bytes 2457608 | tf_op jit(solution)/shard_map/ppermute | solution.py:146
  563.6 71.5 %collective-permute-start.56 = (bf16[4,160,1280]{2,1,0:T(8,128)(2,1)S(1)}, bf16[4,160,1280]{2,1,0:T(8,128)(2,1)S(1)}, u32[]{:S(2)}, u32[]{:S(2)}) collective-permute-start(bf16[4,160,1280]{2,1,0:T(8,128)(2,1)S(1)} %dynamic-slice_bitcast_fusion.3), channel_id=1, source_target_pairs={{0,4},{2,6},{4,0},{6,2},{8,12},{10,14},{12,8},{14,10},{16,20},{18,... | collective-permute-start | bytes 4915208 | tf_op jit(solution)/shard_map/ppermute | solution.py:146
  613.4 38.8 %collective-permute-start.50 = (bf16[4,80,2560]{2,1,0:T(8,128)(2,1)S(1)}, bf16[4,80,2560]{2,1,0:T(8,128)(2,1)S(1)}, u32[]{:S(2)}, u32[]{:S(2)}) collective-permute-start(bf16[4,80,2560]{2,1,0:T(8,128)(2,1)S(1)} %dynamic-slice_bitcast_fusion.4), channel_id=1, source_target_pairs={{0,4},{2,6},{4,0},{6,2},{8,12},{10,14},{12,8},{14,10},{16,20},{18,... | collective-permute-start | bytes 4915208 | tf_op jit(solution)/shard_map/ppermute | solution.py:146
  632.5 42.9 %collective-permute-start.38 = (bf16[4,80,1920]{2,1,0:T(8,128)(2,1)S(1)}, bf16[4,80,1920]{2,1,0:T(8,128)(2,1)S(1)}, u32[]{:S(2)}, u32[]{:S(2)}) collective-permute-start(bf16[4,80,1920]{2,1,0:T(8,128)(2,1)S(1)} %dynamic-slice_bitcast_fusion.6), channel_id=1, source_target_pairs={{0,4},{2,6},{4,0},{6,2},{8,12},{10,14},{12,8},{14,10},{16,20},{18,... | collective-permute-start | bytes 3686408 | tf_op jit(solution)/shard_map/ppermute | solution.py:146
  (107 other events, 2400.8 us)

commit v2 on v1

v2 whole, which is shorter than its diff:
```python
import functools

import jax
import jax.numpy as jnp
from jax import lax
from jax.experimental import pallas as pl
from jax.experimental.pallas import tpu as pltpu
from jax.sharding import PartitionSpec as P

HEADS = 16
HEAD = 80
EPSILON = 1e-06
LOG2E = 1.4426950408889634

bf16 = jnp.bfloat16
f32 = jnp.float32


def contract(left, right, left_dim, right_dim):
    return lax.dot_general(
        left, right, (((left_dim,), (right_dim,)), ((), ())), preferred_element_type=f32
    )


def attend_head(qkv_ref, cos_ref, sin_ref, rot_ref, probs_ref):
    half = HEAD // 2
    scale = HEAD**-0.5 * LOG2E

    def rotate(values):
        turned = jnp.concatenate([-values[half:], values[:half]], axis=0)
        return (values * cos_ref[...] + turned * sin_ref[...]).astype(bf16)

    queries = rotate(qkv_ref[0])
    keys = rotate(qkv_ref[1])
    values = qkv_ref[2].astype(bf16)
    rot_ref[0] = queries
    rot_ref[1] = keys
    rot_ref[2] = values
    scores = contract(keys, queries, 0, 0)
    highest = jnp.max(scores, axis=0, keepdims=True)
    exponent = jnp.exp2(scores * scale - highest * scale)
    totals = jnp.sum(exponent, axis=0, keepdims=True)
    probs = (exponent * (1.0 / totals)).astype(bf16)
    probs_ref[0] = probs
    return contract(values, probs, 1, 0).astype(bf16)


def attend_kernel(qkv_ref, cos_ref, sin_ref, rot_ref, probs_ref, out_ref):
    out_ref[...] = attend_head(qkv_ref, cos_ref, sin_ref, rot_ref, probs_ref)


def attend_send_kernel(
    qkv_ref, cos_ref, sin_ref, proj_ref, fc1_ref, fc2_ref, grad_ref, rot_ref, probs_ref, all_ref,
    w_proj_ref, w_up_ref, w_down_ref, all_grad_ref, held, local, send, recv, *scratch
):
    z, y, core, x = place()
    to_x = device_at(z, y, core, 1 - x)
    head, heads = pl.program_id(0), pl.num_programs(0)
    local_len = held.shape[2] // 2
    proj_held, fc1_held, fc2_held, grad_held, fetched, g_local, g_send, g_recv = scratch[:8]
    proj = SpreadAcross(proj_held, w_proj_ref, *scratch[8:11])
    fc1 = Spread(fc1_held, w_up_ref, *scratch[11:14])
    fc2 = Spread(fc2_held, w_down_ref, *scratch[14:17])
    spreads = (proj, fc1, fc2)
    sources = (proj_ref, fc1_ref, fc2_ref, grad_ref)
    fetches = [
        pltpu.make_async_copy(source, target, fetched.at[i])
        for i, (source, target) in enumerate(zip(sources, scratch))
    ]
    grads = (
        pltpu.make_async_copy(grad_held, all_grad_ref.at[0], g_local.at[0]),
        remote(grad_held, all_grad_ref.at[1], g_send.at[0], g_recv.at[0], to_x),
    )

    def parts(h):
        copies = [pltpu.make_async_copy(held.at[h], all_ref.at[x, h], local.at[h])]
        for p in range(2):
            copies.append(
                remote(
                    held.at[h, :, pl.ds(p * local_len, local_len)],
                    all_ref.at[x, h, :, pl.ds((1 - p) * local_len, local_len)],
                    send.at[h, p],
                    recv.at[h, p],
                    to_x,
                )
            )
        return copies

    @pl.when(head == 0)
    def _():
        for fetch in fetches:
            fetch.start()
        greet_all()
        for fetch in fetches:
            fetch.wait()
        for each in spreads:
            each.begin()

    @pl.when(head == 3)
    def _():
        proj.pass_on(0)
        proj.step(1)

    @pl.when(head == 6)
    def _():
        fc1.step(1)
        fc1.pass_on(0)

    held[head] = attend_head(qkv_ref, cos_ref, sin_ref, rot_ref, probs_ref)
    for copy in parts(head):
        copy.start()

    @pl.when(head == heads - 1)
    def _():
        for copy in grads:
            copy.start()
        fc2.step(1)
        fc2.pass_on(0)
        for k in range(2, 4):
            for each in spreads:
                each.step(k)
            for each in spreads:
                each.pass_on(k - 1)
        for each in spreads:
            each.pass_on(3)
        for h in range(held.shape[0]):
            for copy in parts(h):
                copy.wait()
        for copy in grads:
            copy.wait()
        for each in spreads:
            each.finish()


def attend(qkv_t, cos_t, sin_t, blocks=(), tokens=None):
    anywhere = pl.BlockSpec(memory_space=pl.ANY)
    _, width, length = qkv_t.shape
    heads = width // HEAD
    part = pl.BlockSpec((3, HEAD, length), lambda h: (0, h, 0))
    table = pl.BlockSpec((HEAD, length), lambda h: (0, 0))
    if blocks:
        out_spec = anywhere
        out_shape = jax.ShapeDtypeStruct((2, heads, HEAD, length), bf16)
        scratch = [
            pltpu.VMEM((heads, HEAD, length), bf16),
            pltpu.SemaphoreType.DMA((heads,)),
            pltpu.SemaphoreType.DMA((heads, 2)),
            pltpu.SemaphoreType.DMA((heads, 2)),
        ]
        scratch += [pltpu.VMEM(a.shape, a.dtype) for a in (*blocks, tokens)]
        scratch += [pltpu.SemaphoreType.DMA((4,))] + [pltpu.SemaphoreType.DMA((1,))] * 3
        scratch += Spread.scratch() * len(blocks)
        extra = dict(collective_id=5, has_side_effects=True)
    else:
        out_spec = pl.BlockSpec((HEAD, length), lambda h: (h, 0))
        out_shape = jax.ShapeDtypeStruct((width, length), bf16)
        scratch, extra = [], {}
    more = [] if tokens is None else [*blocks, tokens]
    gives = [jax.ShapeDtypeStruct((4, 2, 2) + block.shape, block.dtype) for block in blocks]
    if more:
        gives.append(jax.ShapeDtypeStruct((2,) + tokens.shape, tokens.dtype))
    rotated, probs, out, *whole = pl.pallas_call(
        attend_send_kernel if blocks else attend_kernel,
        grid=(heads,),
        in_specs=[part, table, table] + [anywhere] * len(more),
        out_specs=[part, pl.BlockSpec((1, length, length), lambda h: (h, 0, 0)), out_spec]
        + [anywhere] * len(more),
        out_shape=[
            jax.ShapeDtypeStruct((3, width, length), bf16),
            jax.ShapeDtypeStruct((heads, length, length), bf16),
            out_shape,
        ]
        + gives,
        scratch_shapes=scratch,
        compiler_params=pltpu.CompilerParams(vmem_limit_bytes=56 * 2**20, **extra),
        cost_estimate=pl.CostEstimate(
            flops=heads * length * length * HEAD * 4 * 5,
            bytes_accessed=heads * length * length * 2 + width * length * 20,
            transcendentals=heads * length * length,
        ),
    )(qkv_t, cos_t, sin_t, *more)
    whole = [each.reshape(-1, each.shape[-1]) for each in whole]
    return (rotated, probs, out.reshape(-1, length), *whole)


def attend_back_scatter_kernel(
    rot_ref, probs_ref, cos_ref, sin_ref, grad_ref, terms_ref, away_ref, far_ref, out_ref, sum_ref, here_ref, near_ref,
    scores_ref, held, local, send, recv, x_send, x_recv, *scratch
):
    owners = [
        Owner(terms_ref, sum_ref, columns, False, *scratch[7 * i : 7 * i + 7])
        for i, columns in enumerate(Owner.pieces(terms_ref))
    ]
    owner = owners[0]
    swaps = (
        remote(away_ref, here_ref, x_send.at[0], x_recv.at[0], owner.to_x),
        remote(far_ref, near_ref, x_send.at[1], x_recv.at[1], owner.to_x),
    )
    head, last = pl.program_id(0), pl.num_programs(0) - 1
    heads, _, length = held.shape
    local_len = length // 2

    def parts(h):
        rows = pl.ds(pl.multiple_of(h * HEAD, 16), HEAD)
        return (
            pltpu.make_async_copy(
                grad_ref.at[owner.x, rows], held.at[h, :, pl.ds(0, local_len)], local.at[h]
            ),
            remote(
                grad_ref.at[1 - owner.x, rows],
                held.at[h, :, pl.ds(local_len, local_len)],
                send.at[h],
                recv.at[h],
                owner.to_x,
            ),
        )

    @pl.when(head == 0)
    def _():
        greet_all()
        for h in range(heads):
            for copy in parts(h):
                copy.start()
        for swap in swaps:
            swap.start()
        for each in owners:
            each.begin()

    for copy in parts(head):
        copy.wait()
    attend_back_head(
        rot_ref, held.at[head], probs_ref, cos_ref, sin_ref, out_ref, scores_ref
    )

    @pl.when(head == 0)
    def _():
        for k in range(4):
            for each in owners:
                each.core_add(k)

    for k in range(2):

        @pl.when(head == 3 + 3 * k)
        def _(k=k):
            for each in owners:
                each.y_add(k)

    @pl.when(head == last)
    def _():
        for k in range(2, 4):
            for each in owners:
                each.y_add(k)
        for each in owners:
            each.finish()
        for swap in swaps:
            swap.wait()


def attend_back_kernel(rot_ref, probs_ref, cos_ref, sin_ref, grad_ref, out_ref, scores_ref):
    attend_back_head(rot_ref, grad_ref, probs_ref, cos_ref, sin_ref, out_ref, scores_ref)


def attend_back_head(rot_ref, grad_ref, probs_ref, cos_ref, sin_ref, out_ref, scores_ref):
    half = HEAD // 2
    scale = HEAD**-0.5
    length = probs_ref.shape[1]
    chunk = min(512, length)
    for start in range(0, length, chunk):
        part = slice(start, start + chunk)
        grad_probs = contract(rot_ref[2], grad_ref[:, part], 0, 0)
        probs = probs_ref[0, :, part].astype(f32)
        inner = jnp.sum(grad_probs * probs, axis=0, keepdims=True) / jnp.sum(
            probs, axis=0, keepdims=True
        )
        scores_ref[:, part] = (probs * (grad_probs - inner)).astype(bf16)

    def turn_back(values):
        values = (values * scale).astype(bf16).astype(f32)
        sined = values * sin_ref[...]
        return (
            values * cos_ref[...] + jnp.concatenate([sined[half:], -sined[:half]], axis=0)
        ).astype(bf16)

    grad_scores = scores_ref[...]
    out_ref[0] = turn_back(contract(rot_ref[1], grad_scores, 1, 0))
    out_ref[1] = turn_back(contract(rot_ref[0], grad_scores, 1, 1))
    out_ref[2] = contract(grad_ref[...], probs_ref[0], 1, 1).astype(bf16)


def attend_back(rotated, grad_t, probs, cos_t, sin_t, terms=None, away=()):
    anywhere = pl.BlockSpec(memory_space=pl.ANY)
    _, width, length = rotated.shape
    heads = width // HEAD
    part = pl.BlockSpec((3, HEAD, length), lambda h: (0, h, 0))
    table = pl.BlockSpec((HEAD, length), lambda h: (0, 0))
    in_specs = [part, pl.BlockSpec((1, length, length), lambda h: (h, 0, 0)), table, table]
    out_specs, out_shape = [part], [jax.ShapeDtypeStruct((3, width, length), bf16)]
    scratch = [pltpu.VMEM((length, length), bf16)]
    arguments = [rotated, probs, cos_t, sin_t, grad_t]
    if terms is None:
        kernel, extra = attend_back_kernel, {}
        in_specs.append(pl.BlockSpec((HEAD, length), lambda h: (h, 0)))
    else:
        kernel, extra = attend_back_scatter_kernel, dict(collective_id=2, has_side_effects=True)
        terms = terms.reshape(4, 2, 2, terms.shape[0] // 16, terms.shape[1])
        arguments += [terms, *away]
        in_specs += [anywhere] * 4
        out_specs += [anywhere] * 3
        out_shape.append(owner_shape(terms, False))
        out_shape += [jax.ShapeDtypeStruct(a.shape, a.dtype) for a in away]
        scratch += [
            pltpu.VMEM((heads, HEAD, length), bf16),
            pltpu.SemaphoreType.DMA((heads,)),
            pltpu.SemaphoreType.DMA((heads,)),
            pltpu.SemaphoreType.DMA((heads,)),
            pltpu.SemaphoreType.DMA((2,)),
            pltpu.SemaphoreType.DMA((2,)),
        ]
        for columns in Owner.pieces(terms):
            scratch += Owner.scratch(terms, columns)
    return pl.pallas_call(
        kernel,
        grid=(heads,),
        in_specs=in_specs,
        out_specs=out_specs,
        out_shape=out_shape,
        scratch_shapes=scratch,
        compiler_params=pltpu.CompilerParams(vmem_limit_bytes=56 * 2**20, **extra),
        cost_estimate=pl.CostEstimate(
            flops=heads * length * length * HEAD * 8 * 4,
            bytes_accessed=heads * length * length * 2 + width * length * 16,
            transcendentals=0,
        ),
    )(*arguments)


def place():
    position = lax.axis_index("fsdp")
    return position // 4, (position // 2) % 2, position % 2, lax.axis_index("seq")


def device_at(z, y, core, x):
    return ((z * 2 + y) * 2 + core, x)


def greet(peers):
    barrier = pltpu.get_barrier_semaphore()
    for peer in peers:
        pl.semaphore_signal(
            barrier, inc=1, device_id=peer, device_id_type=pl.DeviceIdType.MESH
        )
    pl.semaphore_wait(barrier, len(peers))


def remote(source, target, send, recv, peer):
    return pltpu.make_async_remote_copy(
        src_ref=source,
        dst_ref=target,
        send_sem=send,
        recv_sem=recv,
        device_id=peer,
        device_id_type=pl.DeviceIdType.MESH,
    )


class Spread:
    def __init__(self, own, out, local, send, recv):
        self.own, self.out = own, out
        self.local, self.send, self.recv = local, send, recv
        self.z, self.y, self.core, self.x = place()
        self.to_core = device_at(self.z, self.y, 1 - self.core, self.x)
        self.to_y = device_at(self.z, 1 - self.y, self.core, self.x)
        self.to_z = device_at((self.z + 1) % 4, self.y, self.core, self.x)

    @staticmethod
    def scratch():
        return [
            pltpu.SemaphoreType.DMA((1,)),
            pltpu.SemaphoreType.DMA((15,)),
            pltpu.SemaphoreType.DMA((15,)),
        ]

    def _copy(self, step, y, place_of, peer):
        block = self.out.at[(self.z + 4 - step) % 4, y, self.core]
        source = self.own if step == 0 and self.own is not None and place_of != 11 else block
        at = place_of + step
        return remote(source, block, self.send.at[at], self.recv.at[at], peer)

    def _ring(self, step):
        return self._copy(step - 1, self.y, 0, self.to_z)

    def _across(self, step):
        return self._copy(step, self.y, 3, self.to_y)

    def _core_own(self, step):
        return self._copy(step, self.y, 7, self.to_core)

    def _core_far(self, step):
        return self._copy(step, 1 - self.y, 11, self.to_core)

    def _keep(self):
        return pltpu.make_async_copy(
            self.own, self.out.at[self.z, self.y, self.core], self.local.at[0]
        )

    def begin(self):
        self._ring(1).start()
        self._across(0).start()
        self._core_own(0).start()
        if self.own is not None:
            self._keep().start()

    def step(self, step):
        self._ring(step).wait_recv()
        if step < 3:
            self._ring(step + 1).start()
        self._across(step).start()
        self._core_own(step).start()

    def pass_on(self, step):
        self._across(step).wait_recv()
        self._core_far(step).start()

    def finish(self):
        for step in range(1, 4):
            self._ring(step).wait_send()
        for step in range(4):
            self._across(step).wait_send()
            self._core_own(step).wait()
            self._core_far(step).wait()
        if self.own is not None:
            self._keep().wait()


class SpreadAcross(Spread):
    def _ring(self, step, y=None):
        far = y is not None
        block = self.out.at[(self.z + 5 - step) % 4, 1 - self.y if far else self.y, self.core]
        at = step - 1 + (4 if far else 0)
        source = self.own if step == 1 and not far else block
        return remote(source, block, self.send.at[at], self.recv.at[at], self.to_z)

    def begin(self):
        self._across(0).start()
        self._ring(1).start()
        self._core_own(0).start()
        self._keep().start()

    def pass_on(self, step):
        if step == 0:
            self._across(0).wait_recv()
            self._ring(1, 1).start()
            self._core_far(0).start()

    def step(self, step):
        self._ring(step).wait_recv()
        if step < 3:
            self._ring(step + 1).start()
        self._core_own(step).start()
        self._ring(step, 1).wait_recv()
        if step < 3:
            self._ring(step + 1, 1).start()
        self._core_far(step).start()

    def finish(self):
        self._across(0).wait_send()
        for step in range(1, 4):
            self._ring(step).wait_send()
            self._ring(step, 1).wait_send()
        for step in range(4):
            self._core_own(step).wait()
            self._core_far(step).wait()
        self._keep().wait()


def greet_all():
    z, y, core, x = place()
    greet(
        (
            device_at(z, y, core, 1 - x),
            device_at(z, 1 - y, core, x),
            device_at(z, y, 1 - core, x),
            device_at((z + 1) % 4, y, core, x),
            device_at((z + 3) % 4, y, core, x),
        )
    )


def first_kernel(
    tokens_ref, ids_ref, qkv_ref, vec_ref, all_ref, all_ids_ref, w_ref, vecs_ref,
    block, held, local, x_send, x_recv, *scratch
):
    z, y, core, x = place()
    inner = w_ref.shape[-1] // 3
    to_x = device_at(z, y, core, 1 - x)
    greet_all()
    swaps = [
        remote(tokens_ref, all_ref.at[1], x_send.at[0], x_recv.at[0], to_x),
        remote(ids_ref, all_ids_ref.at[1], x_send.at[1], x_recv.at[1], to_x),
    ]
    for swap in swaps:
        swap.start()
    stage = [
        pltpu.make_async_copy(
            qkv_ref.at[:, pl.ds(pl.multiple_of((2 * part + x) * inner, 128), inner)],
            block.at[:, pl.ds(part * inner, inner)],
            local.at[part],
        )
        for part in range(3)
    ]
    fetch = pltpu.make_async_copy(tokens_ref, held, local.at[3])
    keep = [
        pltpu.make_async_copy(held, all_ref.at[0], local.at[3]),
        pltpu.make_async_copy(ids_ref, all_ids_ref.at[0], local.at[4]),
    ]
    for copy in stage:
        copy.start()
    fetch.start()
    for copy in stage:
        copy.wait()
    spreads = (Spread(block, w_ref, *scratch[:3]), Spread(vec_ref, vecs_ref, *scratch[3:]))
    for each in spreads:
        each.begin()
    fetch.wait()
    for copy in keep:
        copy.start()
    for step in range(1, 4):
        for each in spreads:
            each.step(step)
        for each in spreads:
            each.pass_on(step - 1)
    for each in spreads:
        each.pass_on(3)
    for each in spreads:
        each.finish()
    for copy in swaps + keep:
        copy.wait()


def first_exchange(tokens, ids, qkv_weight, vec):
    anywhere = pl.BlockSpec(memory_space=pl.ANY)
    rows, wide = qkv_weight.shape
    return pl.pallas_call(
        first_kernel,
        in_specs=[anywhere] * 4,
        out_specs=[anywhere] * 4,
        out_shape=[
            jax.ShapeDtypeStruct((2,) + tokens.shape, tokens.dtype),
            jax.ShapeDtypeStruct((2,) + ids.shape, ids.dtype),
            jax.ShapeDtypeStruct((4, 2, 2, rows, wide // 2), qkv_weight.dtype),
            jax.ShapeDtypeStruct((4, 2, 2) + vec.shape, vec.dtype),
        ],
        scratch_shapes=[
            pltpu.VMEM((rows, wide // 2), qkv_weight.dtype),
            pltpu.VMEM(tokens.shape, tokens.dtype),
            pltpu.SemaphoreType.DMA((5,)),
            pltpu.SemaphoreType.DMA((2,)),
            pltpu.SemaphoreType.DMA((2,)),
        ]
        + Spread.scratch()
        + Spread.scratch(),
        compiler_params=pltpu.CompilerParams(collective_id=1, has_side_effects=True),
        cost_estimate=pl.CostEstimate(flops=0, bytes_accessed=120_000_000, transcendentals=0),
    )(tokens, ids, qkv_weight, vec)


class Owner:
    def __init__(self, grad, out, columns, swap, mine, near, across, ring, local, send, recv):
        self.grad, self.out, self.columns, self.swap = grad, out, columns, swap
        self.mine, self.near, self.across, self.ring = mine, near, across, ring
        self.local, self.send, self.recv = local, send, recv
        self.z, self.y, self.core, self.x = place()
        self.to_core = device_at(self.z, self.y, 1 - self.core, self.x)
        self.to_y = device_at(self.z, 1 - self.y, self.core, self.x)
        self.to_z = device_at((self.z + 1) % 4, self.y, self.core, self.x)
        self.to_x = device_at(self.z, self.y, self.core, 1 - self.x)

    @staticmethod
    def pieces(grad):
        columns = grad.shape[-1]
        count = next(n for n in (3, 2, 1) if columns % (n * 128) == 0 and columns // n >= 640 or n == 1)
        return [pl.ds(i * (columns // count), columns // count) for i in range(count)]

    @staticmethod
    def scratch(grad, columns):
        rows, columns = grad.shape[-2], columns.size
        return [
            pltpu.VMEM((4, 2, rows, columns), grad.dtype),
            pltpu.VMEM((4, 2, rows, columns), grad.dtype),
            pltpu.VMEM((4, rows, columns), grad.dtype),
            pltpu.VMEM((3, rows, columns), grad.dtype),
            pltpu.SemaphoreType.DMA((5,)),
            pltpu.SemaphoreType.DMA((12,)),
            pltpu.SemaphoreType.DMA((12,)),
        ]

    def _slot(self, k):
        return (self.z + 3 - k) % 4

    def _core_copy(self, k):
        slot = self._slot(k)
        return remote(
            self.grad.at[slot, :, 1 - self.core, :, self.columns],
            self.near.at[slot],
            self.send.at[k],
            self.recv.at[k],
            self.to_core,
        )

    def _own_copy(self, k):
        slot = self._slot(k)
        return pltpu.make_async_copy(
            self.grad.at[slot, :, self.core, :, self.columns],
            self.mine.at[slot],
            self.local.at[k],
        )

    def _y_copy(self, k):
        slot = self._slot(k)
        return remote(
            self.mine.at[slot, 1 - self.y],
            self.across.at[slot],
            self.send.at[4 + k],
            self.recv.at[4 + k],
            self.to_y,
        )

    def _z_copy(self, k):
        return remote(
            self.across.at[self._slot(k)],
            self.ring.at[k],
            self.send.at[8 + k],
            self.recv.at[8 + k],
            self.to_z,
        )

    def _x_copy(self):
        return remote(
            self.across.at[self.z],
            self.out.at[self.x, :, self.columns],
            self.send.at[11],
            self.recv.at[11],
            self.to_x,
        )

    def _out_copy(self):
        out = self.out.at[self.x] if self.swap else self.out
        return pltpu.make_async_copy(
            self.across.at[self.z], out.at[:, self.columns], self.local.at[4]
        )

    def begin(self):
        for k in range(4):
            self._core_copy(k).start()
            self._own_copy(k).start()

    def core_add(self, k):
        slot = self._slot(k)
        self._core_copy(k).wait_recv()
        self._own_copy(k).wait()
        self.mine[slot] = self.mine[slot] + self.near[slot]
        self._y_copy(k).start()

    def y_add(self, k):
        slot = self._slot(k)
        self._y_copy(k).wait_recv()
        total = self.mine[slot, self.y].astype(f32) + self.across[slot].astype(f32)
        if k > 0:
            self._z_copy(k - 1).wait_recv()
            total = total + self.ring[k - 1].astype(f32)
        self.across[slot] = total.astype(self.across.dtype)
        if k < 3:
            self._z_copy(k).start()
        else:
            if self.swap:
                self._x_copy().start()
            self._out_copy().start()

    def finish(self):
        for k in range(4):
            self._core_copy(k).wait_send()
            self._y_copy(k).wait_send()
        for k in range(3):
            self._z_copy(k).wait_send()
        self._out_copy().wait()
        if self.swap:
            self._x_copy().wait()


def owner_shape(grad, swap):
    shape = grad.shape[-2:]
    return jax.ShapeDtypeStruct((2,) + shape if swap else shape, grad.dtype)


def exchange_kernel(matrices, swaps, swap, *refs):
    refs = list(refs)
    take = lambda n: [refs.pop(0) for _ in range(n)]
    grads, away, outs, here = take(matrices), take(swaps), take(matrices), take(swaps)
    owners = [
        Owner(grad, out, columns, swap, *take(7))
        for grad, out in zip(grads, outs)
        for columns in Owner.pieces(grad)
    ]
    x_send, x_recv = take(2)
    greet_all()
    copies = []
    for i in range(swaps):
        copy = remote(away[i], here[i], x_send.at[i], x_recv.at[i], owners[0].to_x)
        copy.start()
        copies.append(copy)
    for owner in owners:
        owner.begin()
    for k in range(4):
        for owner in owners:
            owner.core_add(k)
    for k in range(4):
        for owner in owners:
            owner.y_add(k)
    for owner in owners:
        owner.finish()
    for copy in copies:
        copy.wait()


def exchange(grads, away, swap, collective_id):
    anywhere = pl.BlockSpec(memory_space=pl.ANY)
    grads = [g.reshape(4, 2, 2, g.shape[0] // 16, g.shape[1]) for g in grads]
    scratch = []
    for grad in grads:
        for columns in Owner.pieces(grad):
            scratch += Owner.scratch(grad, columns)
    scratch += [pltpu.SemaphoreType.DMA((max(1, len(away)),))] * 2
    return pl.pallas_call(
        functools.partial(exchange_kernel, len(grads), len(away), swap),
        in_specs=[anywhere] * (len(grads) + len(away)),
        out_specs=[anywhere] * (len(grads) + len(away)),
        out_shape=[owner_shape(g, swap) for g in grads]
        + [jax.ShapeDtypeStruct(a.shape, a.dtype) for a in away],
        scratch_shapes=scratch,
        compiler_params=pltpu.CompilerParams(
            collective_id=collective_id, has_side_effects=True, vmem_limit_bytes=56 * 2**20
        ),
        cost_estimate=pl.CostEstimate(flops=0, bytes_accessed=120_000_000, transcendentals=0),
    )(*grads, *away)


def finish_kernel(qkv_ref, proj_ref, fc1_ref, fc1_far_ref, fc2_ref, fc2_far_ref, *outs):
    g_qkv, g_proj, g_fc1, g_fc2 = outs
    first = lax.axis_index("seq") == 0
    inner = qkv_ref.shape[2] // 3
    for part in range(3):
        for x in range(2):
            g_qkv[:, pl.ds((2 * part + x) * inner, inner)] = qkv_ref[
                x, :, pl.ds(part * inner, inner)
            ].astype(f32)
    g_proj[...] = proj_ref[0].astype(f32) + proj_ref[1].astype(f32)
    deep = fc2_ref.shape[0]

    def lay(fc1, fc1_far, fc2, fc2_far):
        g_fc2[:deep] = fc2[...].astype(f32)
        g_fc2[deep:] = fc2_far[...].astype(f32)
        columns = fc1.shape[1]
        wide = 4 * deep
        for start in range(0, columns, wide):
            here, far = (a[:, start : start + wide].astype(f32) for a in (fc1, fc1_far))
            cuts = [a[:, i : i + deep] for i in range(0, wide, deep) for a in (here, far)]
            g_fc1[:, 2 * start : 2 * (start + wide)] = jnp.concatenate(cuts, axis=1)

    @pl.when(first)
    def _():
        lay(fc1_ref, fc1_far_ref, fc2_ref, fc2_far_ref)

    @pl.when(jnp.logical_not(first))
    def _():
        lay(fc1_far_ref, fc1_ref, fc2_far_ref, fc2_ref)


def finish(qkv, proj, fc1, fc1_far, fc2, fc2_far):
    rows, width = proj.shape[1:]
    return pl.pallas_call(
        finish_kernel,
        out_shape=[
            jax.ShapeDtypeStruct((rows, 2 * qkv.shape[2]), f32),
            jax.ShapeDtypeStruct((rows, width), f32),
            jax.ShapeDtypeStruct((rows, 2 * fc1.shape[1]), f32),
            jax.ShapeDtypeStruct((2 * fc2.shape[0], width), f32),
        ],
        compiler_params=pltpu.CompilerParams(vmem_limit_bytes=40 * 2**20),
        cost_estimate=pl.CostEstimate(flops=0, bytes_accessed=10_000_000, transcendentals=0),
    )(qkv, proj, fc1, fc1_far, fc2, fc2_far)


class Chain:
    def __init__(self):
        position = lax.axis_index("fsdp")
        self.core = position % 2
        self.y = (position // 2) % 2
        self.z = position // 4
        self.x = lax.axis_index("seq")

    def swap_x(self, values):
        return lax.ppermute(values, "seq", [(0, 1), (1, 0)])

    def first(self, tokens, ids, qkv_weight, vec):
        vec = vec.reshape(-1, 128)
        all_in, all_ids, w_qkv, vecs = first_exchange(tokens, ids, qkv_weight, vec)
        return (
            all_in.reshape(-1, tokens.shape[1]),
            jnp.concatenate([all_ids[0], all_ids[1]], axis=1),
            w_qkv.reshape(-1, w_qkv.shape[-1]),
            vecs.reshape(16, -1),
        )

    def sums(self, terms, tokens, collective_id, swap=False, away=()):
        local = tokens.shape[0] // 2
        sent = []
        for each in terms:
            if each.dtype == f32:
                rows, size = each.shape
                each = jnp.pad(each, ((0, 0), (0, -size % 2048))).reshape(rows * 16, -1)
            sent.append(each)
        sent_away = [tokens[local:].astype(bf16), *away]
        results = exchange(sent, sent_away, swap, collective_id)
        sums, (token_terms, *here) = list(results[: len(sent)]), results[len(sent) :]
        for i, each in enumerate(terms):
            if each.dtype == f32:
                sums[i] = (sums[i][0] + sums[i][1]).reshape(-1)[: each.shape[1]]
        return (*sums, *here, tokens[:local] + token_terms.astype(f32))

    def finish(self, *sums):
        return finish(*sums)

    def far_terms(self, tokens):
        local = tokens.shape[0] // 2
        return tokens[local:].astype(bf16), tokens[:local]

    def near_sum(self, near, kept):
        return kept + near.astype(f32)

    def attend(self, *arguments):
        return attend(*arguments)

    def attend_back(self, rotated, grad_t, *rest):
        return attend_back(rotated, grad_t.reshape(2, -1, grad_t.shape[1]), *rest)


class Plain:
    def __init__(self):
        self.x = lax.axis_index("seq")

    def gather(self, block):
        return lax.all_gather(block, "fsdp", axis=0, tiled=True)

    def sums(self, terms, tokens, collective_id, swap=False, away=()):
        sums = []
        for each in terms:
            if each.dtype == f32:
                each = lax.psum_scatter(each, "fsdp", scatter_dimension=0, tiled=True)
                sums.append(lax.psum(each, "seq")[0])
            else:
                sums.append(self.scatter(each))
        tokens = lax.psum_scatter(tokens, "seq", scatter_dimension=0, tiled=True)
        return (*sums, *away, tokens)

    def finish(self, qkv, proj, fc1, _, fc2, __):
        seq, rows, _ = qkv.shape
        cut = fc2.shape[1]
        qkv = jnp.transpose(qkv.reshape(seq, rows, 3, -1), (1, 2, 0, 3)).reshape(rows, -1)
        fc1 = jnp.transpose(fc1.reshape(seq, rows, -1, cut), (1, 2, 0, 3)).reshape(rows, -1)
        fc2 = fc2.reshape(seq * cut, -1)
        return tuple(a.astype(f32) for a in (qkv, jnp.sum(proj.astype(f32), axis=0), fc1, fc2))

    def attend_back(self, rotated, grad_t, probs, cos_t, sin_t, terms, away):
        grad_t = lax.all_to_all(grad_t, "seq", split_axis=0, concat_axis=1, tiled=True)
        (grad,) = attend_back(rotated, grad_t, probs, cos_t, sin_t)
        return (grad, self.scatter(terms), *away)

    def scatter(self, whole):
        owned = lax.psum_scatter(whole, "fsdp", scatter_dimension=0, tiled=True)
        return lax.all_gather(owned, "seq", axis=0)

    def tokens_to_all(self, values):
        return lax.all_gather(values, "seq", axis=0, tiled=True)

    def first(self, tokens, ids, qkv_weight, vec):
        rows, wide = qkv_weight.shape
        seq = lax.axis_size("seq")
        block = lax.dynamic_index_in_dim(
            qkv_weight.reshape(rows, 3, seq, wide // (3 * seq)), self.x, 2, keepdims=False
        )
        return (
            self.tokens_to_all(tokens),
            lax.all_gather(ids, "seq", axis=1, tiled=True),
            self.gather(block.reshape(rows, wide // seq)),
            lax.all_gather(vec, "fsdp", axis=0),
        )

    def far_terms(self, tokens):
        return tokens, None

    def near_sum(self, near, _):
        return lax.psum_scatter(near, "seq", scatter_dimension=0, tiled=True)

    def attend(self, qkv_t, cos_t, sin_t, blocks, tokens):
        rotated, probs, attended = attend(qkv_t, cos_t, sin_t)
        attended = lax.all_gather(attended, "seq", axis=0, tiled=True)
        whole = [self.gather(block) for block in blocks]
        return (rotated, probs, attended, *whole, self.tokens_to_all(tokens))


def normalize(values):
    centered = values - jnp.mean(values, axis=-1, keepdims=True)
    inv_scale = lax.rsqrt(jnp.mean(centered * centered, axis=-1, keepdims=True) + EPSILON)
    return (centered * inv_scale, inv_scale)


def norm_back(grad_norm, normed, inv_scale):
    return inv_scale * (
        grad_norm
        - jnp.mean(grad_norm, axis=-1, keepdims=True)
        - normed * jnp.mean(grad_norm * normed, axis=-1, keepdims=True)
    )


def joined(vectors):
    size = sum(v.shape[0] for v in vectors)
    size += -size % 2048
    total, start = 0, 0
    for vector in vectors:
        stop = start + vector.shape[0]
        total = total + jnp.pad(vector.astype(f32), (start, size - stop))
        start = stop
    return total.astype(vectors[0].dtype)


def rotary(ids, head_size):
    quarter = head_size // 4
    frequency = jnp.power(10000.0, -2.0 * jnp.arange(quarter, dtype=f32) / (head_size // 2))
    angles = (ids.astype(f32)[:, None, :] * frequency[None, :, None]).reshape(
        2 * quarter, ids.shape[1]
    )
    angles = jnp.concatenate([angles, angles], axis=0)
    return (jnp.cos(angles), jnp.sin(angles))


def body(
    inputs,
    row_ids,
    col_ids,
    norm1_gain,
    norm1_bias,
    qkv_weight,
    qkv_bias,
    proj_weight,
    proj_bias,
    norm2_gain,
    norm2_bias,
    fc1_weight,
    fc1_bias,
    fc2_weight,
    fc2_bias,
    cotangent,
):
    fsdp, seq = lax.axis_size("fsdp"), lax.axis_size("seq")
    move = Chain() if (fsdp, seq) == (16, 2) else Plain()
    x = move.x
    _, local, width = inputs.shape
    heads = HEADS // seq
    head_size = width // HEADS
    inner = heads * head_size
    rows = width // fsdp
    hidden = fc1_weight.shape[1]
    deep = hidden // fsdp
    cut = deep // seq

    own_in = inputs[0]
    own_grad = cotangent[0]

    own_part = lambda a, dim: lax.dynamic_index_in_dim(a, x, dim, keepdims=False)
    fc1_block = own_part(fc1_weight.reshape(rows, fsdp, seq, cut), 2).reshape(rows, fsdp * cut)
    fc2_block = own_part(fc2_weight.reshape(seq, cut, width), 0)

    vectors = (
        norm1_gain,
        norm1_bias,
        proj_bias,
        norm2_gain,
        norm2_bias,
        fc2_bias,
        qkv_bias,
        fc1_bias,
    )
    all_in, ids, w_qkv, packed = move.first(
        own_in, jnp.concatenate([row_ids, col_ids], axis=0), qkv_weight, joined(vectors)
    )
    packed = packed.astype(f32)
    whole_vectors = []
    start = 0
    for vector in vectors:
        whole_vectors.append(packed[:, start : start + vector.shape[0]].reshape(-1))
        start += vector.shape[0]
    gain_one, bias_one, b_proj, gain_two, bias_two, b_down, b_qkv, b_up = whole_vectors
    b_qkv = own_part(b_qkv.reshape(3, seq, inner), 1).reshape(-1)
    b_up = own_part(b_up.reshape(fsdp, seq, cut), 1).reshape(-1)


    cos_t, sin_t = rotary(ids, head_size)
    normed_all, inv_all = normalize(all_in.astype(f32))
    ln_one = (normed_all * gain_one + bias_one).astype(bf16)
    qkv_t = contract(w_qkv, ln_one, 0, 1) + b_qkv[:, None]
    length = qkv_t.shape[1]
    rotated, probs, attended, w_proj, w_up, w_down, all_grad = move.attend(
        qkv_t.reshape(3, inner, length), cos_t, sin_t, (proj_weight, fc1_block, fc2_block), own_grad
    )
    after_all = all_in.astype(f32) + (contract(attended, w_proj, 0, 0) + b_proj)
    own_tokens = (
        (lambda a, dim: lax.slice_in_dim(a, 0, local, axis=dim))
        if isinstance(move, Chain)
        else (lambda a, dim: lax.dynamic_slice_in_dim(a, x * local, local, axis=dim))
    )
    after_attn = own_tokens(after_all, 0)
    normed_two_all, inv_two_all = normalize(after_all)
    ln_two = (normed_two_all * gain_two + bias_two).astype(bf16)
    pre_act = contract(ln_two, w_up, 1, 0) + b_up
    gating = jax.nn.sigmoid(1.702 * pre_act)
    activated = (pre_act * gating).astype(bf16)
    slope = (gating + 1.702 * pre_act * gating * (1.0 - gating)).astype(bf16)

    far_mlp, kept_mlp = move.far_terms(contract(activated, w_down, 1, 0))

    terms_fc2 = contract(activated, all_grad, 0, 0).astype(bf16)
    grad_pre = (contract(all_grad, w_down, 1, 1) * slope.astype(f32)).astype(bf16)
    terms_fc1 = contract(ln_two, grad_pre, 0, 0).astype(bf16)
    terms_ln_two = contract(grad_pre, w_up, 1, 1)
    sum_fc2, grad_ln_two = move.sums([terms_fc2], terms_ln_two, 3)
    normed_two, inv_two = own_tokens(normed_two_all, 0), own_tokens(inv_two_all, 0)
    grad_out = own_grad.astype(f32)
    grad_after = grad_out + norm_back(grad_ln_two * gain_two, normed_two, inv_two)
    grad_proj_in = grad_after.astype(bf16)

    grad_att = contract(w_proj, grad_proj_in, 1, 1).astype(bf16)
    terms_proj = contract(own_tokens(attended, 1), grad_proj_in, 1, 0).astype(bf16)
    grad_qkv_t, sum_fc1, far_fc2, near_mlp = move.attend_back(
        rotated, grad_att, probs, cos_t, sin_t, terms_fc1, (sum_fc2, far_mlp)
    )
    block_out = after_attn + (move.near_sum(near_mlp, kept_mlp) + b_down)
    grad_qkv_t = grad_qkv_t.reshape(3 * inner, length)

    terms_qkv = contract(ln_one, grad_qkv_t, 0, 1).astype(bf16)
    terms_ln_one = contract(grad_qkv_t, w_qkv, 0, 1)

    spread = lambda vector, shape, dim: lax.dynamic_update_index_in_dim(
        jnp.zeros(shape, f32), vector, x, dim
    ).reshape(-1)
    grad_vectors = (
        jnp.sum(terms_ln_one * normed_all, axis=0),
        jnp.sum(terms_ln_one, axis=0),
        jnp.sum(grad_proj_in.astype(f32), axis=0),
        jnp.sum(terms_ln_two * normed_two_all, axis=0),
        jnp.sum(terms_ln_two, axis=0),
        jnp.sum(grad_out, axis=0),
        spread(jnp.sum(grad_qkv_t.astype(f32), axis=1).reshape(3, inner), (3, seq, inner), 1),
        spread(jnp.sum(grad_pre.astype(f32), axis=0).reshape(fsdp, cut), (fsdp, seq, cut), 1),
    )
    qk_vector, v_vector = jnp.split(grad_vectors[6], (2 * width,))
    grad_vectors = grad_vectors[:6] + (qk_vector, v_vector) + grad_vectors[7:]
    terms_vectors = jnp.concatenate([v.reshape(fsdp, -1) for v in grad_vectors], axis=1)

    sum_proj, sum_qkv, sum_vectors, far_fc1, grad_ln_one = move.sums(
        [terms_proj, terms_qkv, terms_vectors], terms_ln_one, 4, True, (sum_fc1,)
    )
    normed_one, inv_one = own_tokens(normed_all, 0), own_tokens(inv_all, 0)
    grad_inputs = grad_after + norm_back(grad_ln_one * gain_one, normed_one, inv_one)
    pieces = []
    start = 0
    for vector in grad_vectors:
        share = vector.shape[0] // fsdp
        pieces.append(lax.slice_in_dim(sum_vectors, start, start + share))
        start += share
    g_gain_one, g_bias_one, g_b_proj, g_gain_two, g_bias_two, g_b_down, g_b_qk, g_b_v, g_b_up = pieces

    g_qkv, g_proj, g_fc1, g_fc2 = move.finish(
        sum_qkv, sum_proj, sum_fc1, far_fc1, sum_fc2, far_fc2
    )

    return (
        block_out.astype(bf16)[None],
        grad_inputs[None],
        g_gain_one,
        g_bias_one,
        g_qkv,
        g_b_qk,
        g_b_v,
        g_proj,
        g_b_proj,
        g_gain_two,
        g_bias_two,
        g_fc1,
        g_b_up,
        g_fc2,
        g_b_down,
    )


def solution(mesh):
    rows = P("fsdp", None)
    vector = P("fsdp")
    tokens = P("fsdp", "seq", None)
    ids = P("fsdp", "seq")
    in_specs = (
        tokens,
        ids,
        ids,
        vector,
        vector,
        rows,
        vector,
        rows,
        vector,
        vector,
        vector,
        rows,
        vector,
        rows,
        vector,
        tokens,
    )
    out_specs = (
        tokens,
        tokens,
        vector,
        vector,
        rows,
        vector,
        vector,
        rows,
        vector,
        vector,
        vector,
        rows,
        vector,
        rows,
        vector,
    )
    return jax.shard_map(body, mesh=mesh, in_specs=in_specs, out_specs=out_specs, check_vma=False)
```

time: 749 us -> 479 us (0.64)
  waiting for transfers between devices: 366 us -> 0 us
  Pallas kernels: 45.2 us -> 297 us
  blocking collectives: 61.3 us -> 0 us
  local copies, waits for them, and re-layouts: 80.9 us -> 30.4 us
  starting transfers between devices: 39.4 us -> 0 us
    ppermute x61 -> x0, waiting for transfers between devices: 366 us -> none  [the longest x48 270 us: _fsdp(): return lax.ppermute(values, 'fsdp', pairs)]
    pallas_call x2 -> x6, Pallas kernels: 45.2 us -> 297 us  [the longest x1 99.4 us: attend(): pl.pallas_call(attend_send_kernel if blocks else attend_kernel, grid=(hea...]
    unnamed x1 -> x0, blocking collectives: 61.3 us -> none
    ppermute x61 -> x0, starting transfers between devices: 39.4 us -> none  [the longest x48 20.9 us: _fsdp(): return lax.ppermute(values, 'fsdp', pairs)]
    dynamic_update_slice x31 -> x0, local copies, waits for them, and re-layouts: 30.4 us -> none  [the longest x16 16.3 us: gather(): lax.dynamic_update_slice(full, part[:, None, None], (0, y, core, 0, 0))]
    convert_element_type x23 -> x1, other arithmetic: 14.7 us -> 1.02 us  [body(): ln_one = (normed_all * gain_one + bias_one).astype(bf16)]
    slice x1 -> x9, local copies, waits for them, and re-layouts: 0.09 us -> 11.6 us  [the longest x2 6.15 us: sums(): sent_away = [tokens[local:].astype(bf16), *away]]
    broadcast_in_dim x10 -> x0, local copies, waits for them, and re-layouts: 10.4 us -> none  [the longest x4 4.62 us: gather(): line = jnp.zeros((4, rows, columns), block.dtype)]
  transfers between devices with their start and end apart: 61 -> 0, of which waited for: 31 -> 0; matrix products, arithmetic and copies ran while one was open for 23% -> 0% of each run, Pallas kernels for 6% -> 0%
where the time goes in v2:
time: 479 us; the launch traced here: 472 us
  Pallas kernels  297 us (62%)
  matrix products  112 us (23%)
  other arithmetic  30.7 us (6%)
  local copies, waits for them, and re-layouts  30.4 us (6%)
    dot_general x12, matrix products, contract(): lax.dot_general(left, right, (((left_dim,), (right_dim,)), ((), ())), pre...  112 us
    pallas_call x1, Pallas kernels, attend(): pl.pallas_call(attend_send_kernel if blocks else attend_kernel, grid=(hea...  99.4 us
    pallas_call x2, Pallas kernels, exchange(): pl.pallas_call(functools.partial(exchange_kernel, len(grads), len(away),...  96.9 us
    pallas_call x1, Pallas kernels, attend_back(): pl.pallas_call(kernel, grid=(heads,), in_specs=in_specs, out_specs=out_sp...  59 us
    pallas_call x1, Pallas kernels, first_exchange(): pl.pallas_call(first_kernel, in_specs=[anywhere] * 4, out_specs=[anywhere...  38.5 us

profile of v2, /device:TPU:0, one launch (start us, length us, event | category | flops | bytes accessed | tf_op | source)
XLA Modules:
  0.0 471.6 jit_solution(5976168799089588942)
XLA Ops:
  7.9 4.0 dynamic-slice_reduce_fusion
  13.6 38.5 %shard_map.271 = (bf16[2,512,1280]{2,1,0:T(8,128)(2,1)}, s32[2,2,512]{2,1,0:T(2,128)}, bf16[4,2,2,80,1920]{4,3,2,1,0:T(8,128)(2,1)}, bf16[4,2,2,16,128]{4,3,2,1,0:T(8,128)(2,1)}) custom-call(bf16[512,1280]{1,0:T(8,128)(2,1)} %bitcast.92, s32[2,512]{1,0:T(2,128)} %pad_add_fusion.ids_ref, bf16[80,3840]{1,0:T(8,128)(2,1)} %qkv_ref.1, ...), custom_call_target="tpu_custom_call" | custom-call | bytes 120000000 | tf_op jit(solution)/shard_map/pallas_call | solution.py:543
  63.7 8.8 %broadcast_add_fusion = f32[1920,1024]{1,0:T(8,128)} fusion(f32[1920]{0:T(1024)S(1)} %add.189, bf16[1280,1920]{1,0:T(8,128)(2,1)S(1)} %bitcast.102, bf16[1024,1280]{1,0:T(8,128)(2,1)S(1)} %bitcast.89), kind=kOutput, calls=%fused_computation.26 | convolution fusion | flops 5035130880 | bytes 15408640 | tf_op jit(solution)/shard_map/dot_general | solution.py:20
  72.5 99.4 %shard_map.272 = (bf16[3,640,1024]{2,1,0:T(8,128)(2,1)}, bf16[8,1024,1024]{2,1,0:T(8,128)(2,1)}, bf16[2,8,80,1024]{3,2,1,0:T(8,128)(2,1)}, bf16[4,2,2,80,1280]{4...) custom-call(f32[3,640,1024]{2,1,0:T(8,128)} %bitcast.103, ...), custom_call_target="tpu_custom_call" | custom-call | flops 13421772800 | bytes 29884416 | tf_op jit(solution)/shard_map/pallas_call | solution.py:162
  171.9 7.0 %fusion.28 = (f32[1024]{0:T(1024)S(1)}, f32[1024,1280]{1,0:T(8,128)S(1)}) fusion(f32[1280]{0:T(1024)S(1)} %add.192, bf16[1280,1024]{1,0:T(8,128)(2,1)} %bitcast.113, bf16[1280,1280]{1,0:T(8,128)(2,1)} %bitcast.111, bf16[2,512,1280]{2,1,0:T(8,128)(2,1)S(1)} %copy-done.9), kind=kOutput, calls=%fused_computation.84 | convolution fusion | flops 3360685056 | bytes 13771776 | tf_op jit(solution)/shard_map/dot_general | solution.py:20
  183.9 10.5 %multiply_convert_fusion.1 = (bf16[1024,2560]{1,0:T(8,128)(2,1)}, f32[1024,2560]{1,0:T(8,128)}) fusion(f32[2560]{0:T(1024)S(1)} %add.200, bf16[1280,2560]{1,0:T(8,128)(2,1)S(1)} %bitcast.106, f32[1024,1280]{1,0:T(8,128)S(1)} %subtract_multiply_fusion, f32[1280]{0:T(1024)S(1)} %add.197, f32[1280]{0:T(1024)S(1)} %mul.166), kind=kOutput, calls=%fused_computation.5 | convolution fusion | flops 6733168640 | bytes 27545600 | tf_op jit(solution)/shard_map/dot_general | solution.py:20
  194.4 15.6 %convert_reduce_fusion = (f32[2560]{0:T(1024)S(1)}, bf16[1024,2560]{1,0:T(8,128)(2,1)}) fusion(f32[1024,2560]{1,0:T(8,128)} %get-tuple-element.103, f32[2560]{0:T(1024)S(1)} %add.200, bf16[1024,1280]{1,0:T(8,128)(2,1)S(1)} %bitcast.115, bf16[2560,1280]{1,0:T(8,128)(2,1)} %bitcast.108), kind=kOutput, calls=%fused_computation.2 | convolution fusion | flops 6750205440 | bytes 24924160 | tf_op jit(solution)/shard_map/dot_general | solution.py:20
  210.0 12.4 %fusion.29 = f32[1024,1280]{1,0:T(8,128)} fusion(bf16[1024,2560]{1,0:T(8,128)(2,1)} %get-tuple-element.102, bf16[2560,1280]{1,0:T(8,128)(2,1)} %bitcast.109), kind=kOutput, calls=%fused_computation.85 | convolution fusion | flops 6710886400 | bytes 17039360 | tf_op jit(solution)/shard_map/dot_general | solution.py:20
  222.4 9.2 %convolution_convert_fusion.1 = bf16[2560,1280]{1,0:T(8,128)(2,1)} fusion(bf16[1024,2560]{1,0:T(8,128)(2,1)S(1)} %copy-done.30, bf16[1024,1280]{1,0:T(8,128)(2,1)S(1)} %bitcast.116), kind=kOutput, calls=%fused_computation.1 | convolution fusion | flops 6714163200 | bytes 14417920 | tf_op jit(solution)/shard_map/dot_general | solution.py:20
  231.6 10.4 %fusion.24 = (f32[1280]{0:T(1024)S(1)}, f32[1280]{0:T(1024)S(1)}, f32[1024,1280]{1,0:T(8,128)}) fusion(f32[1024,1280]{1,0:T(8,128)S(1)} %subtract_multiply_fusion, bf16[1024,2560]{1,0:T(8,128)(2,1)} %get-tuple-element.107, bf16[1280,2560]{1,0:T(8,128)(2,1)S(1)} %bitcast.107), kind=kOutput, calls=%fused_computation.80 | convolution fusion | flops 6714816512 | bytes 22292480 | tf_op jit(solution)/shard_map/dot_general | solution.py:20
  242.4 3.1 slice.222.refs_1_
  245.5 42.8 %shard_map.273 = (bf16[160,1280]{1,0:T(8,128)(2,1)}, bf16[512,1280]{1,0:T(8,128)(2,1)}) custom-call(bf16[4,2,2,160,1280]{4,3,2,1,0:T(8,128)(2,1)} %bitcast.84, bf16[512,1280]{1,0:T(8,128)(2,1)} %slice.222.refs_1_), custom_call_target="tpu_custom_call" | custom-call | bytes 120000000 | tf_op jit(solution)/shard_map/pallas_call | solution.py:733
  291.3 3.0 convert_reduce_fusion.4
  294.4 9.2 %convolution_convert_fusion = bf16[1280,2560]{1,0:T(8,128)(2,1)} fusion(bf16[1024,2560]{1,0:T(8,128)(2,1)S(1)} %bitcast.119, f32[1024,1280]{1,0:T(8,128)S(1)} %bitcast.81, f32[1280]{0:T(1024)S(1)} %add.197, f32[1280]{0:T(1024)S(1)} %mul.166), kind=kOutput, calls=%fused_computation | convolution fusion | flops 6718095360 | bytes 17049600 | tf_op jit(solution)/shard_map/dot_general | solution.py:20
  303.6 3.0 convolution_convert_fusion.4
  306.7 5.1 %convolution_convert_fusion.3 = bf16[1280,1280]{1,0:T(8,128)(2,1)} fusion(bf16[1280,1024]{1,0:T(8,128)(2,1)} %bitcast.114, f32[512,1280]{1,0:T(8,128)S(1)} %get-tuple-element.76), kind=kOutput, calls=%fused_computation.9 | convolution fusion | flops 1680015360 | bytes 7208960 | tf_op jit(solution)/shard_map/dot_general | solution.py:20
  311.8 2.9 slice.221.far_ref
  314.7 59.0 %shard_map.274 = (bf16[3,640,1024]{2,1,0:T(8,128)(2,1)}, bf16[80,2560]{1,0:T(8,128)(2,1)}, bf16[160,1280]{1,0:T(8,128)(2,1)}, bf16[512,1280]{1,0:T(8,128)(2,1)}) custom-call(bf16[3,640,1024]{2,1,0:T(8,128)(2,1)} %get-tuple-element.49.rot_ref, bf16[8,1024,1024]{2,1,0:T(8,128)(2,1)} %get-tuple-element.50.probs_ref, f32[80,1024]{1,0:T(8,128)} %get-tuple-element.80.cos_ref, ...), custom_call_target="tpu_custom_call" | custom-call | flops 21474836480 | bytes 27262976 | tf_op jit(solution)/shard_map/pallas_call | solution.py:321
  373.8 3.8 fusion.12
  378.5 10.2 %convolution_convert_fusion.2 = bf16[1280,1920]{1,0:T(8,128)(2,1)} fusion(bf16[1024,1280]{1,0:T(8,128)(2,1)} %bitcast.90, bf16[1920,1024]{1,0:T(8,128)(2,1)} %bitcast.86), kind=kOutput, calls=%fused_computation.8 | convolution fusion | flops 5035622400 | bytes 11468800 | tf_op jit(solution)/shard_map/dot_general | solution.py:20
  388.7 11.2 %fusion.25 = (f32[1280]{0:T(1024)S(1)}, f32[1280]{0:T(1024)S(1)}, f32[1024,1280]{1,0:T(8,128)}, f32[1024,1280]{1,0:T(8,128)}) fusion(f32[1024]{0:T(1024)S(1)} %bitcast.100, f32[1024]{0:T(1024)S(1)} %bitcast.99, bf16[2,512,1280]{2,1,0:T(8,128)(2,1)S(1)} %copy-done.10, bf16[1920,1024]{1,0:T(8,128)(2,1)S(1)} %bitcast.87, bf16[1280,1920]{1,0:T(8,128)(2,1)} %bitcast.101), kind=kOutput, calls=%fused_computation.81 | convolution fusion | flops 5041027072 | bytes 21972992 | tf_op jit(solution)/shard_map/dot_general | solution.py:20
  400.9 3.1 slice.220.refs_3_
  403.9 54.1 %shard_map.275 = (bf16[2,80,1280]{2,1,0:T(8,128)(2,1)}, bf16[2,80,1920]{2,1,0:T(8,128)(2,1)}, f32[2,16,128]{2,1,0:T(8,128)}, bf16[512,1280]{1,0:T(8,128)(2,1)}, bf16[80,2560]{1,0:T(8,128)(2,1)}) custom-call(bf16[4,2,2,80,1280]{4,3,2,1,0:T(8,128)(2,1)} %bitcast.88, bf16[4,2,2,80,1920]{4,3,2,1,0:T(8,128)(2,1)} %bitcast.85, f32[4,2,2,16,128]{4,3,2,1,0:T(8,128)} %bitcast.93, ...), custom_call_target="tpu_custom_call" | custom-call | bytes 120000000 | tf_op jit(solution)/shard_map/pallas_call | solution.py:733
  463.7 5.0 %add_bitcast_fusion = f32[1,512,1280]{2,1,0:T(8,128)} fusion(f32[512,1280]{1,0:T(8,128)S(1)} %get-tuple-element.76, f32[1024,1280]{1,0:T(8,128)} %get-tuple-element.77, f32[512]{0:T(512)S(1)} %broadcast_multiply_fusion.3, f32[512]{0:T(512)S(1)} %broadcast_multiply_fusion.4, f32[512]{0:T(512)S(1)} %bitcast.98, f32[1280]{0:T(1024)S(1)} %copy-done.19, ...), kind=kLoop, calls=%fused_computation.41 | loop fusion | flops 5242880 | bytes 11807744 | tf_op jit(solution)/shard_map/broadcast_in_dim | solution.py:1088
  (162 shorter events, 39.1 us)
Async XLA Ops:
  52.2 6.7 %copy-start.23 = (s32[2,2,512]{2,1,0:T(2,128)S(1)}, s32[2,2,512]{2,1,0:T(2,128)}, u32[]{:S(2)}) copy-start(s32[2,2,512]{2,1,0:T(2,128)} %get-tuple-element.44) | copy-start | bytes 24580
  52.2 6.7 %copy-start.20 = (bf16[4,2,2,16,128]{4,3,2,1,0:T(8,128)(2,1)S(1)}, bf16[4,2,2,16,128]{4,3,2,1,0:T(8,128)(2,1)}, u32[]{:S(2)}) copy-start(bf16[4,2,2,16,128]{4,3,2,1,0:T(8,128)(2,1)} %get-tuple-element.43) | copy-start | bytes 196612
  52.2 10.5 %copy-start.9 = (bf16[2,512,1280]{2,1,0:T(8,128)(2,1)S(1)}, bf16[2,512,1280]{2,1,0:T(8,128)(2,1)}, u32[]{:S(2)}) copy-start(bf16[2,512,1280]{2,1,0:T(8,128)(2,1)} %get-tuple-element.41) | copy-start | bytes 7864324
  60.1 12.4 %copy-start.18 = (f32[1280]{0:T(1024)}, f32[1280]{0:T(1024)S(1)}, u32[]{:S(2)}) copy-start(f32[1280]{0:T(1024)S(1)} %mul.154) | copy-start | bytes 15364
  63.7 8.8 %copy-start.16 = (bf16[2,512,1280]{2,1,0:T(8,128)(2,1)}, bf16[2,512,1280]{2,1,0:T(8,128)(2,1)S(1)}, u32[]{:S(2)}) copy-start(bf16[2,512,1280]{2,1,0:T(8,128)(2,1)S(1)} %fusion.5) | copy-start | bytes 7864324
  183.9 47.6 %copy-start.11 = (f32[1024,1280]{1,0:T(8,128)}, f32[1024,1280]{1,0:T(8,128)S(1)}, u32[]{:S(2)}) copy-start(f32[1024,1280]{1,0:T(8,128)S(1)} %subtract_multiply_fusion) | copy-start | bytes 15728644
  183.9 10.5 %copy-start.29 = (bf16[2,512,1280]{2,1,0:T(8,128)(2,1)S(1)}, bf16[2,512,1280]{2,1,0:T(8,128)(2,1)}, u32[]{:S(2)}) copy-start(bf16[2,512,1280]{2,1,0:T(8,128)(2,1)} %get-tuple-element.51) | copy-start | bytes 7864324
  210.0 12.4 %copy-start.30 = (bf16[1024,2560]{1,0:T(8,128)(2,1)S(1)}, bf16[1024,2560]{1,0:T(8,128)(2,1)}, u32[]{:S(2)}) copy-start(bf16[1024,2560]{1,0:T(8,128)(2,1)} %get-tuple-element.102) | copy-start | bytes 15728644
  242.4 45.9 %slice-start.2 = ((s8[5242880]{0:T(1024)(128)(4,1)}), s8[4194304]{0:T(1024)(128)(4,1)S(1)}, s32[]{:S(2)}) async-start(s8[5242880]{0:T(1024)(128)(4,1)} %bitcast.80), calls=%async_computation.2 | async-start | bytes 8388608
  245.5 42.8 %slice-start.3 = ((s8[5242880]{0:T(1024)(128)(4,1)}), s8[1048576]{0:T(1024)(128)(4,1)S(1)}, s32[]{:S(2)}) async-start(s8[5242880]{0:T(1024)(128)(4,1)} %bitcast.80), calls=%async_computation.3 | async-start | bytes 2097152
  288.4 6.0 %slice-start.9 = ((s8[5242880]{0:T(1024)(128)(4,1)}), s8[4194304]{0:T(1024)(128)(4,1)S(1)}, s32[]{:S(2)}) async-start(s8[5242880]{0:T(1024)(128)(4,1)} %bitcast.118), calls=%async_computation.9 | async-start | bytes 8388608
  294.4 9.2 %copy-start.28 = (bf16[4,2,2,80,1280]{4,3,2,1,0:T(8,128)(2,1)S(1)}, bf16[4,2,2,80,1280]{4,3,2,1,0:T(8,128)(2,1)}, u32[]{:S(2)}) copy-start(bf16[4,2,2,80,1280]{4,3,2,1,0:T(8,128)(2,1)} %get-tuple-element.46) | copy-start | bytes 9830404
  306.7 67.0 %slice-start = ((s8[5242880]{0:T(1024)(128)(4,1)}), s8[4194304]{0:T(1024)(128)(4,1)S(1)}, s32[]{:S(2)}) async-start(s8[5242880]{0:T(1024)(128)(4,1)} %bitcast.78), calls=%async_computation | async-start | bytes 8388608
  314.7 59.0 %slice-start.1 = ((s8[5242880]{0:T(1024)(128)(4,1)}), s8[1048576]{0:T(1024)(128)(4,1)S(1)}, s32[]{:S(2)}) async-start(s8[5242880]{0:T(1024)(128)(4,1)} %bitcast.78), calls=%async_computation.1 | async-start | bytes 2097152
  314.7 59.0 %copy-start.21 = (f32[1280]{0:T(1024)S(1)}, f32[1280]{0:T(1024)}, u32[]{:S(2)}) copy-start(f32[1280]{0:T(1024)} %add.208) | copy-start | bytes 15364
  378.4 10.2 %copy-start.10 = (bf16[2,512,1280]{2,1,0:T(8,128)(2,1)S(1)}, bf16[2,512,1280]{2,1,0:T(8,128)(2,1)}, u32[]{:S(2)}) copy-start(bf16[2,512,1280]{2,1,0:T(8,128)(2,1)} %get-tuple-element.41) | copy-start | bytes 7864324
  378.4 10.2 %copy-start.15 = (bf16[3,640,1024]{2,1,0:T(8,128)(2,1)S(1)}, bf16[3,640,1024]{2,1,0:T(8,128)(2,1)}, u32[]{:S(2)}) copy-start(bf16[3,640,1024]{2,1,0:T(8,128)(2,1)} %get-tuple-element.55) | copy-start | bytes 11796484
  378.5 10.2 %copy-start.25 = (f32[1,4,2,128]{3,1,2,0:T(4,128)S(1)}, f32[1,4,2,128]{3,1,2,0:T(4,128)}, u32[]{:S(2)}) copy-start(f32[1,4,2,128]{3,1,2,0:T(4,128)} %copy.35) | copy-start | bytes 12292
  378.5 10.2 %copy-start.26 = (f32[1,4,2,128]{3,1,2,0:T(4,128)S(1)}, f32[1,4,2,128]{3,1,2,0:T(4,128)}, u32[]{:S(2)}) copy-start(f32[1,4,2,128]{3,1,2,0:T(4,128)} %copy.36) | copy-start | bytes 12292
  400.9 59.9 %slice-start.4 = ((s8[5242880]{0:T(1024)(128)(4,1)}), s8[4194304]{0:T(1024)(128)(4,1)S(1)}, s32[]{:S(2)}) async-start(s8[5242880]{0:T(1024)(128)(4,1)} %bitcast.82), calls=%async_computation.4 | async-start | bytes 8388608
  403.9 56.8 %slice-start.5 = ((s8[5242880]{0:T(1024)(128)(4,1)}), s8[1048576]{0:T(1024)(128)(4,1)S(1)}, s32[]{:S(2)}) async-start(s8[5242880]{0:T(1024)(128)(4,1)} %bitcast.82), calls=%async_computation.5 | async-start | bytes 2097152
  403.9 56.9 %copy-start.19 = (f32[1280]{0:T(1024)S(1)}, f32[1280]{0:T(1024)}, u32[]{:S(2)}) copy-start(f32[1280]{0:T(1024)} %copy-done.18) | copy-start | bytes 15364
  458.0 5.6 %copy-start.13 = (bf16[512,1280]{1,0:T(8,128)(2,1)S(1)}, bf16[512,1280]{1,0:T(8,128)(2,1)}, u32[]{:S(2)}) copy-start(bf16[512,1280]{1,0:T(8,128)(2,1)} %get-tuple-element.57) | copy-start | bytes 3932164
  463.6 7.9 %copy-start.1 = (bf16[320,1280]{1,0:T(8,128)(2,1)S(1)}, bf16[320,1280]{1,0:T(8,128)(2,1)}, u32[]{:S(2)}) copy-start(bf16[320,1280]{1,0:T(8,128)(2,1)} %param.29) | copy-start | bytes 2457604
  (18 other events, 67.3 us)

commit v3 on v2

--- a/solution.py
+++ b/solution.py
@@ -50,19 +50,18 @@
 
 
 def attend_send_kernel(
-    qkv_ref, cos_ref, sin_ref, proj_ref, fc1_ref, fc2_ref, grad_ref, rot_ref, probs_ref, all_ref,
-    w_proj_ref, w_up_ref, w_down_ref, all_grad_ref, held, local, send, recv, *scratch
+    qkv_ref, cos_ref, sin_ref, proj_ref, fc1_ref, grad_ref, rot_ref, probs_ref, all_ref,
+    w_proj_ref, w_up_ref, all_grad_ref, held, local, send, recv, *scratch
 ):
     z, y, core, x = place()
     to_x = device_at(z, y, core, 1 - x)
     head, heads = pl.program_id(0), pl.num_programs(0)
     local_len = held.shape[2] // 2
-    proj_held, fc1_held, fc2_held, grad_held, fetched, g_local, g_send, g_recv = scratch[:8]
-    proj = SpreadAcross(proj_held, w_proj_ref, *scratch[8:11])
-    fc1 = Spread(fc1_held, w_up_ref, *scratch[11:14])
-    fc2 = Spread(fc2_held, w_down_ref, *scratch[14:17])
-    spreads = (proj, fc1, fc2)
-    sources = (proj_ref, fc1_ref, fc2_ref, grad_ref)
+    proj_held, fc1_held, grad_held, fetched, g_local, g_send, g_recv = scratch[:7]
+    proj = Spread(proj_held, w_proj_ref, *scratch[7:10])
+    fc1 = Spread(fc1_held, w_up_ref, *scratch[10:13])
+    spreads = (proj, fc1)
+    sources = (proj_ref, fc1_ref, grad_ref)
     fetches = [
         pltpu.make_async_copy(source, target, fetched.at[i])
         for i, (source, target) in enumerate(zip(sources, scratch))
@@ -96,15 +95,12 @@
         for each in spreads:
             each.begin()
 
-    @pl.when(head == 3)
-    def _():
-        proj.pass_on(0)
-        proj.step(1)
-
-    @pl.when(head == 6)
-    def _():
-        fc1.step(1)
-        fc1.pass_on(0)
+    for each, k, when in ((proj, 1, 1), (fc1, 1, 5), (proj, 2, 7)):
+
+        @pl.when(head == when)
+        def _(each=each, k=k):
+            each.step(k)
+            each.pass_on(k - 1)
 
     held[head] = attend_head(qkv_ref, cos_ref, sin_ref, rot_ref, probs_ref)
     for copy in parts(head):
@@ -114,13 +110,11 @@
     def _():
         for copy in grads:
             copy.start()
-        fc2.step(1)
-        fc2.pass_on(0)
-        for k in range(2, 4):
-            for each in spreads:
-                each.step(k)
-            for each in spreads:
-                each.pass_on(k - 1)
+        fc1.step(2)
+        fc1.pass_on(1)
+        for each in spreads:
+            each.step(3)
+            each.pass_on(2)
         for each in spreads:
             each.pass_on(3)
         for h in range(held.shape[0]):
@@ -148,7 +142,7 @@
             pltpu.SemaphoreType.DMA((heads, 2)),
         ]
         scratch += [pltpu.VMEM(a.shape, a.dtype) for a in (*blocks, tokens)]
-        scratch += [pltpu.SemaphoreType.DMA((4,))] + [pltpu.SemaphoreType.DMA((1,))] * 3
+        scratch += [pltpu.SemaphoreType.DMA((3,))] + [pltpu.SemaphoreType.DMA((1,))] * 3
         scratch += Spread.scratch() * len(blocks)
         extra = dict(collective_id=5, has_side_effects=True)
     else:
@@ -432,47 +426,6 @@
             self._keep().wait()
 
 
-class SpreadAcross(Spread):
-    def _ring(self, step, y=None):
-        far = y is not None
-        block = self.out.at[(self.z + 5 - step) % 4, 1 - self.y if far else self.y, self.core]
-        at = step - 1 + (4 if far else 0)
-        source = self.own if step == 1 and not far else block
-        return remote(source, block, self.send.at[at], self.recv.at[at], self.to_z)
-
-    def begin(self):
-        self._across(0).start()
-        self._ring(1).start()
-        self._core_own(0).start()
-        self._keep().start()
-
-    def pass_on(self, step):
-        if step == 0:
-            self._across(0).wait_recv()
-            self._ring(1, 1).start()
-            self._core_far(0).start()
-
-    def step(self, step):
-        self._ring(step).wait_recv()
-        if step < 3:
-            self._ring(step + 1).start()
-        self._core_own(step).start()
-        self._ring(step, 1).wait_recv()
-        if step < 3:
-            self._ring(step + 1, 1).start()
-        self._core_far(step).start()
-
-    def finish(self):
-        self._across(0).wait_send()
-        for step in range(1, 4):
-            self._ring(step).wait_send()
-            self._ring(step, 1).wait_send()
-        for step in range(4):
-            self._core_own(step).wait()
-            self._core_far(step).wait()
-        self._keep().wait()
-
-
 def greet_all():
     z, y, core, x = place()
     greet(
@@ -487,8 +440,8 @@
 
 
 def first_kernel(
-    tokens_ref, ids_ref, qkv_ref, vec_ref, all_ref, all_ids_ref, w_ref, vecs_ref,
-    block, held, local, x_send, x_recv, *scratch
+    tokens_ref, ids_ref, qkv_ref, vec_ref, fc1_ref, all_ref, all_ids_ref, w_ref, vecs_ref, fc1_out,
+    block, held, fc1_held, fc1_part, local, x_send, x_recv, *scratch
 ):
     z, y, core, x = place()
     inner = w_ref.shape[-1] // 3
@@ -509,6 +462,8 @@
         for part in range(3)
     ]
     fetch = pltpu.make_async_copy(tokens_ref, held, local.at[3])
+    fetch_fc1 = pltpu.make_async_copy(fc1_ref, fc1_held, local.at[5])
+    keep_fc1 = pltpu.make_async_copy(fc1_part, fc1_out, local.at[5])
     keep = [
         pltpu.make_async_copy(held, all_ref.at[0], local.at[3]),
         pltpu.make_async_copy(ids_ref, all_ids_ref.at[0], local.at[4]),
@@ -516,6 +471,7 @@
     for copy in stage:
         copy.start()
     fetch.start()
+    fetch_fc1.start()
     for copy in stage:
         copy.wait()
     spreads = (Spread(block, w_ref, *scratch[:3]), Spread(vec_ref, vecs_ref, *scratch[3:]))
@@ -524,6 +480,23 @@
     fetch.wait()
     for copy in keep:
         copy.start()
+    fetch_fc1.wait()
+    wide = fc1_held.shape[1]
+    cut = wide // 32
+
+    def take(at):
+        for start in range(0, wide, 8 * cut):
+            whole = fc1_held[:, start : start + 8 * cut]
+            cuts = [whole[:, (2 * i + at) * cut : (2 * i + at + 1) * cut] for i in range(4)]
+            fc1_part[:, start // 2 : start // 2 + 4 * cut] = jnp.concatenate(cuts, axis=1)
+
+    for at in range(2):
+
+        @pl.when(x == at)
+        def _(at=at):
+            take(at)
+
+    keep_fc1.start()
     for step in range(1, 4):
         for each in spreads:
             each.step(step)
@@ -533,27 +506,30 @@
         each.pass_on(3)
     for each in spreads:
         each.finish()
-    for copy in swaps + keep:
+    for copy in swaps + keep + [keep_fc1]:
         copy.wait()
 
 
-def first_exchange(tokens, ids, qkv_weight, vec):
+def first_exchange(tokens, ids, qkv_weight, vec, fc1_weight):
     anywhere = pl.BlockSpec(memory_space=pl.ANY)
     rows, wide = qkv_weight.shape
     return pl.pallas_call(
         first_kernel,
-        in_specs=[anywhere] * 4,
-        out_specs=[anywhere] * 4,
+        in_specs=[anywhere] * 5,
+        out_specs=[anywhere] * 5,
         out_shape=[
             jax.ShapeDtypeStruct((2,) + tokens.shape, tokens.dtype),
             jax.ShapeDtypeStruct((2,) + ids.shape, ids.dtype),
             jax.ShapeDtypeStruct((4, 2, 2, rows, wide // 2), qkv_weight.dtype),
             jax.ShapeDtypeStruct((4, 2, 2) + vec.shape, vec.dtype),
+            jax.ShapeDtypeStruct((rows, fc1_weight.shape[1] // 2), fc1_weight.dtype),
         ],
         scratch_shapes=[
             pltpu.VMEM((rows, wide // 2), qkv_weight.dtype),
             pltpu.VMEM(tokens.shape, tokens.dtype),
-            pltpu.SemaphoreType.DMA((5,)),
+            pltpu.VMEM(fc1_weight.shape, fc1_weight.dtype),
+            pltpu.VMEM((rows, fc1_weight.shape[1] // 2), fc1_weight.dtype),
+            pltpu.SemaphoreType.DMA((6,)),
             pltpu.SemaphoreType.DMA((2,)),
             pltpu.SemaphoreType.DMA((2,)),
         ]
@@ -561,7 +537,7 @@
         + Spread.scratch(),
         compiler_params=pltpu.CompilerParams(collective_id=1, has_side_effects=True),
         cost_estimate=pl.CostEstimate(flops=0, bytes_accessed=120_000_000, transcendentals=0),
-    )(tokens, ids, qkv_weight, vec)
+    )(tokens, ids, qkv_weight, vec, fc1_weight)
 
 
 class Owner:
@@ -744,6 +720,273 @@
     )(*grads, *away)
 
 
+def mlp_kernel(
+    att_ref, proj_ref, in_ref, vec_ref, b_up_ref, up_ref, grad_ref, fc2_ref,
+    after_ref, ln_ref, act_ref, slope_ref, terms_ref, down_ref,
+    fc2_held, fetched, *scratch
+):
+    step = pl.program_id(0)
+    parts, last = ln_ref.shape[0] // in_ref.shape[0], pl.num_programs(0) - 1
+    rows = in_ref.shape[0]
+    fc2 = Spread(fc2_held, down_ref, *scratch)
+    fetch = pltpu.make_async_copy(fc2_ref, fc2_held, fetched.at[0])
+
+    @pl.when(step == 0)
+    def _():
+        fetch.start()
+        greet_all()
+        fetch.wait()
+        fc2.begin()
+
+    for k, when in ((1, parts + 1), (2, parts + 3)):
+
+        @pl.when(step == when)
+        def _(k=k):
+            fc2.step(k)
+            fc2.pass_on(k - 1)
+
+    @pl.when(step < parts)
+    def _():
+        after = in_ref[...].astype(f32) + (
+            contract(att_ref[...], proj_ref[...], 0, 0) + vec_ref[0:1]
+        )
+        normed, _ = normalize(after)
+        here = pl.ds(pl.multiple_of(step * rows, rows), rows)
+        ln_ref[here] = (normed * vec_ref[1:2] + vec_ref[2:3]).astype(bf16)
+
+        @pl.when(step < parts // 2)
+        def _():
+            after_ref[here] = after
+
+    @pl.when(step >= parts)
+    def _():
+        pre_act = contract(ln_ref[...], up_ref[...], 1, 0) + b_up_ref[...]
+        gating = jax.nn.sigmoid(1.702 * pre_act)
+        active = (pre_act * gating).astype(bf16)
+        act_ref[...] = active
+        slope_ref[...] = (gating + 1.702 * pre_act * gating * (1.0 - gating)).astype(bf16)
+        terms_ref[...] = contract(active, grad_ref[...], 0, 0).astype(bf16)
+
+    @pl.when(step == last)
+    def _():
+        fc2.step(3)
+        fc2.pass_on(2)
+        fc2.pass_on(3)
+        fc2.finish()
+
+
+def mlp(attended, w_proj, all_in, vectors, b_up, w_up, all_grad, fc2_block, tile=512, rows=256):
+    length, width = all_in.shape
+    hidden = w_up.shape[1]
+    parts, tiles = length // rows, hidden // tile
+    anywhere = pl.BlockSpec(memory_space=pl.ANY)
+    once = pl.Buffered(1)
+    whole = lambda shape: pl.BlockSpec(shape, lambda s: (0, 0), pipeline_mode=once)
+    early = lambda s: jnp.minimum(s, parts - 1)
+    late = lambda s: jnp.maximum(s - parts, 0)
+    wide = pl.BlockSpec((length, tile), lambda s: (0, late(s)))
+    results = pl.pallas_call(
+        mlp_kernel,
+        grid=(parts + tiles,),
+        in_specs=[
+            pl.BlockSpec((width, rows), lambda s: (0, early(s))),
+            whole((width, width)),
+            pl.BlockSpec((rows, width), lambda s: (early(s), 0)),
+            whole((3, width)),
+            pl.BlockSpec((1, tile), lambda s: (0, late(s))),
+            pl.BlockSpec((width, tile), lambda s: (0, late(s))),
+            whole((length, width)),
+            anywhere,
+        ],
+        out_specs=[
+            whole((length // 2, width)),
+            whole((length, width)),
+            wide,
+            wide,
+            pl.BlockSpec((tile, width), lambda s: (late(s), 0)),
+            anywhere,
+        ],
+        out_shape=[
+            jax.ShapeDtypeStruct((length // 2, width), f32),
+            jax.ShapeDtypeStruct((length, width), bf16),
+            jax.ShapeDtypeStruct((length, hidden), bf16),
+            jax.ShapeDtypeStruct((length, hidden), bf16),
+            jax.ShapeDtypeStruct((hidden, width), bf16),
+            jax.ShapeDtypeStruct((4, 2, 2) + fc2_block.shape, bf16),
+        ],
+        scratch_shapes=[
+            pltpu.VMEM(fc2_block.shape, bf16),
+            pltpu.SemaphoreType.DMA((1,)),
+        ]
+        + Spread.scratch(),
+        compiler_params=pltpu.CompilerParams(
+            collective_id=6, has_side_effects=True, vmem_limit_bytes=60 * 2**20
+        ),
+        cost_estimate=pl.CostEstimate(
+            flops=4 * length * width * hidden, bytes_accessed=60_000_000, transcendentals=0
+        ),
+    )(attended, w_proj, all_in, vectors, b_up, w_up, all_grad, fc2_block)
+    *results, w_down = results
+    return (*results, w_down.reshape(-1, width))
+
+
+def mlp_back_kernel(
+    grad_ref, ln_ref, down_ref, up_ref, slope_ref, act_ref, terms_ref,
+    fc1_ref, bias_ref, out_ref, far_ref, kept_ref, sum_ref,
+    ln_t, grad_pre, far_sum, far_mlp, sent, received, x_send, x_recv, *scratch
+):
+    owners = [
+        Owner(terms_ref, sum_ref, columns, False, *scratch[7 * i : 7 * i + 7])
+        for i, columns in enumerate(Owner.pieces(terms_ref))
+    ]
+    step = pl.program_id(0)
+    tiles, local, tile = grad_pre.shape
+    swap = remote(sent, received, x_send.at[0], x_recv.at[0], owners[0].to_x)
+    columns = ln_ref.shape[1] // tiles
+
+    @pl.when(step == 0)
+    def _():
+        greet_all()
+        for each in owners:
+            each.begin()
+        bias_ref[...] = jnp.zeros_like(bias_ref)
+
+    for first in range(2):
+
+        @pl.when(step == 1 + first)
+        def _(first=first):
+            for k in (2 * first, 2 * first + 1):
+                for each in owners:
+                    each.core_add(k)
+
+    for k, when in ((0, tiles), (1, tiles + 2), (2, tiles + 3)):
+
+        @pl.when(step == when)
+        def _(k=k):
+            for each in owners:
+                each.y_add(k)
+
+    def tile_of(index, tokens):
+        grad = contract(grad_ref[tokens], down_ref[...], 1, 1) * slope_ref[...].astype(f32)
+        part = pl.ds(pl.multiple_of(index * tile, tile), tile)
+        grad = grad.astype(bf16)
+        bias_ref[:, part] += jnp.sum(grad.astype(f32), axis=0, keepdims=True)
+        return grad
+
+    @pl.when(step < tiles)
+    def _():
+        grad = tile_of(step, pl.ds(local, local))
+        grad_pre[step] = grad
+        back = contract(grad, up_ref[...], 1, 1)
+
+        @pl.when(step == 0)
+        def _():
+            far_sum[...] = back
+
+        @pl.when(step > 0)
+        def _():
+            far_sum[...] += back
+
+        part = pl.ds(pl.multiple_of(step * columns, columns), columns)
+        ln_t[part] = ln_ref[:, part].T
+
+    @pl.when(step == tiles - 1)
+    def _():
+        sent[...] = far_sum[...].astype(bf16)
+        swap.start()
+
+    @pl.when(step >= tiles)
+    def _():
+        index = step - tiles
+        grad = tile_of(index, pl.ds(0, local))
+        back = contract(grad, up_ref[...], 1, 1)
+        mlp = contract(act_ref[pl.ds(0, local)], down_ref[...], 1, 0)
+        mlp_far = contract(act_ref[pl.ds(local, local)], down_ref[...], 1, 0)
+        both = jnp.concatenate([grad, grad_pre[index]], axis=0)
+        fc1_ref[...] = contract(ln_t[...], both, 1, 0).astype(bf16)
+
+        @pl.when(index == 0)
+        def _():
+            out_ref[...] = back
+            kept_ref[...] = mlp
+            far_mlp[...] = mlp_far
+
+        @pl.when(index > 0)
+        def _():
+            out_ref[...] += back
+            kept_ref[...] += mlp
+            far_mlp[...] += mlp_far
+
+    @pl.when(step == 2 * tiles - 1)
+    def _():
+        far_ref[...] = far_mlp[...].astype(bf16)
+        for each in owners:
+            each.y_add(3)
+        swap.wait()
+        out_ref[...] += received[...].astype(f32)
+        for each in owners:
+            each.finish()
+
+
+def mlp_back(all_grad, ln_two, w_down, w_up, slope, activated, terms, tile=512):
+    length, width = all_grad.shape
+    local, hidden = length // 2, w_down.shape[0]
+    tiles = hidden // tile
+    terms = terms.reshape(4, 2, 2, terms.shape[0] // 16, terms.shape[1])
+    anywhere = pl.BlockSpec(memory_space=pl.ANY)
+    once = pl.Buffered(1)
+    late = lambda s: jnp.maximum(s - tiles, 0)
+    scratch = [
+        pltpu.VMEM((width, length), bf16),
+        pltpu.VMEM((tiles, local, tile), bf16),
+        pltpu.VMEM((local, width), f32),
+        pltpu.VMEM((local, width), f32),
+        pltpu.VMEM((local, width), bf16),
+        pltpu.VMEM((local, width), bf16),
+        pltpu.SemaphoreType.DMA((1,)),
+        pltpu.SemaphoreType.DMA((1,)),
+    ]
+    for columns in Owner.pieces(terms):
+        scratch += Owner.scratch(terms, columns)
+    whole = lambda shape: pl.BlockSpec(shape, lambda s: (0, 0), pipeline_mode=once)
+    return pl.pallas_call(
+        mlp_back_kernel,
+        grid=(2 * tiles,),
+        in_specs=[
+            whole((length, width)),
+            whole((length, width)),
+            pl.BlockSpec((tile, width), lambda s: (s % tiles, 0)),
+            pl.BlockSpec((width, tile), lambda s: (0, s % tiles)),
+            pl.BlockSpec((local, tile), lambda s: (1 - s // tiles, s % tiles)),
+            pl.BlockSpec((length, tile), lambda s: (0, late(s))),
+            anywhere,
+        ],
+        out_specs=[
+            pl.BlockSpec((width, tile), lambda s: (0, late(s))),
+            whole((1, hidden)),
+            whole((local, width)),
+            whole((local, width)),
+            whole((local, width)),
+            anywhere,
+        ],
+        out_shape=[
+            jax.ShapeDtypeStruct((width, hidden), bf16),
+            jax.ShapeDtypeStruct((1, hidden), f32),
+            jax.ShapeDtypeStruct((local, width), f32),
+            jax.ShapeDtypeStruct((local, width), bf16),
+            jax.ShapeDtypeStruct((local, width), f32),
+            owner_shape(terms, False),
+        ],
+        scratch_shapes=scratch,
+        compiler_params=pltpu.CompilerParams(
+            collective_id=3, has_side_effects=True, vmem_limit_bytes=60 * 2**20
+        ),
+        cost_estimate=pl.CostEstimate(
+            flops=8 * length * width * hidden, bytes_accessed=100_000_000, transcendentals=0
+        ),
+    )(all_grad, ln_two, w_down, w_up, slope, activated, terms)
+
+
 def finish_kernel(qkv_ref, proj_ref, fc1_ref, fc1_far_ref, fc2_ref, fc2_far_ref, *outs):
     g_qkv, g_proj, g_fc1, g_fc2 = outs
     first = lax.axis_index("seq") == 0
@@ -801,14 +1044,15 @@
     def swap_x(self, values):
         return lax.ppermute(values, "seq", [(0, 1), (1, 0)])
 
-    def first(self, tokens, ids, qkv_weight, vec):
+    def first(self, tokens, ids, qkv_weight, vec, fc1_weight):
         vec = vec.reshape(-1, 128)
-        all_in, all_ids, w_qkv, vecs = first_exchange(tokens, ids, qkv_weight, vec)
+        all_in, all_ids, w_qkv, vecs, fc1 = first_exchange(tokens, ids, qkv_weight, vec, fc1_weight)
         return (
             all_in.reshape(-1, tokens.shape[1]),
             jnp.concatenate([all_ids[0], all_ids[1]], axis=1),
             w_qkv.reshape(-1, w_qkv.shape[-1]),
             vecs.reshape(16, -1),
+            fc1,
         )
 
     def sums(self, terms, tokens, collective_id, swap=False, away=()):
@@ -830,9 +1074,11 @@
     def finish(self, *sums):
         return finish(*sums)
 
-    def far_terms(self, tokens):
-        local = tokens.shape[0] // 2
-        return tokens[local:].astype(bf16), tokens[:local]
+    def mlp(self, *arguments):
+        return mlp(*arguments)
+
+    def mlp_back(self, *arguments):
+        return mlp_back(*arguments)
 
     def near_sum(self, near, kept):
         return kept + near.astype(f32)
@@ -882,9 +1128,9 @@
     def tokens_to_all(self, values):
         return lax.all_gather(values, "seq", axis=0, tiled=True)
 
-    def first(self, tokens, ids, qkv_weight, vec):
+    def first(self, tokens, ids, qkv_weight, vec, fc1_weight):
         rows, wide = qkv_weight.shape
-        seq = lax.axis_size("seq")
+        fsdp, seq = lax.axis_size("fsdp"), lax.axis_size("seq")
         block = lax.dynamic_index_in_dim(
             qkv_weight.reshape(rows, 3, seq, wide // (3 * seq)), self.x, 2, keepdims=False
         )
@@ -893,10 +1139,39 @@
             lax.all_gather(ids, "seq", axis=1, tiled=True),
             self.gather(block.reshape(rows, wide // seq)),
             lax.all_gather(vec, "fsdp", axis=0),
-        )
-
-    def far_terms(self, tokens):
-        return tokens, None
+            lax.dynamic_index_in_dim(
+                fc1_weight.reshape(rows, fsdp, seq, -1), self.x, 2, keepdims=False
+            ).reshape(rows, -1),
+        )
+
+    def mlp(self, attended, w_proj, all_in, vectors, b_up, w_up, all_grad, fc2_block):
+        after = all_in.astype(f32) + (contract(attended, w_proj, 0, 0) + vectors[0])
+        normed, _ = normalize(after)
+        ln_two = (normed * vectors[1] + vectors[2]).astype(bf16)
+        pre_act = contract(ln_two, w_up, 1, 0) + b_up
+        gating = jax.nn.sigmoid(1.702 * pre_act)
+        activated = (pre_act * gating).astype(bf16)
+        slope = (gating + 1.702 * pre_act * gating * (1.0 - gating)).astype(bf16)
+        local = after.shape[0] // lax.axis_size("seq")
+        return (
+            lax.dynamic_slice_in_dim(after, self.x * local, local),
+            ln_two,
+            activated,
+            slope,
+            contract(activated, all_grad, 0, 0).astype(bf16),
+            self.gather(fc2_block),
+        )
+
+    def mlp_back(self, all_grad, ln_two, w_down, w_up, slope, activated, terms):
+        grad_pre = (contract(all_grad, w_down, 1, 1) * slope.astype(f32)).astype(bf16)
+        return (
+            contract(ln_two, grad_pre, 0, 0).astype(bf16),
+            jnp.sum(grad_pre.astype(f32), axis=0),
+            self.near_sum(contract(grad_pre, w_up, 1, 1), None),
+            contract(activated, w_down, 1, 0),
+            None,
+            self.scatter(terms),
+        )
 
     def near_sum(self, near, _):
         return lax.psum_scatter(near, "seq", scatter_dimension=0, tiled=True)
@@ -977,7 +1252,6 @@
     own_grad = cotangent[0]
 
     own_part = lambda a, dim: lax.dynamic_index_in_dim(a, x, dim, keepdims=False)
-    fc1_block = own_part(fc1_weight.reshape(rows, fsdp, seq, cut), 2).reshape(rows, fsdp * cut)
     fc2_block = own_part(fc2_weight.reshape(seq, cut, width), 0)
 
     vectors = (
@@ -990,8 +1264,8 @@
         qkv_bias,
         fc1_bias,
     )
-    all_in, ids, w_qkv, packed = move.first(
-        own_in, jnp.concatenate([row_ids, col_ids], axis=0), qkv_weight, joined(vectors)
+    all_in, ids, w_qkv, packed, fc1_block = move.first(
+        own_in, jnp.concatenate([row_ids, col_ids], axis=0), qkv_weight, joined(vectors), fc1_weight
     )
     packed = packed.astype(f32)
     whole_vectors = []
@@ -1009,31 +1283,29 @@
     ln_one = (normed_all * gain_one + bias_one).astype(bf16)
     qkv_t = contract(w_qkv, ln_one, 0, 1) + b_qkv[:, None]
     length = qkv_t.shape[1]
-    rotated, probs, attended, w_proj, w_up, w_down, all_grad = move.attend(
-        qkv_t.reshape(3, inner, length), cos_t, sin_t, (proj_weight, fc1_block, fc2_block), own_grad
-    )
-    after_all = all_in.astype(f32) + (contract(attended, w_proj, 0, 0) + b_proj)
+    rotated, probs, attended, w_proj, w_up, all_grad = move.attend(
+        qkv_t.reshape(3, inner, length), cos_t, sin_t, (proj_weight, fc1_block), own_grad
+    )
+    after_attn, ln_two, activated, slope, terms_fc2, w_down = move.mlp(
+        attended,
+        w_proj,
+        all_in,
+        jnp.stack([b_proj, gain_two, bias_two]),
+        b_up[None],
+        w_up,
+        all_grad,
+        fc2_block,
+    )
     own_tokens = (
         (lambda a, dim: lax.slice_in_dim(a, 0, local, axis=dim))
         if isinstance(move, Chain)
         else (lambda a, dim: lax.dynamic_slice_in_dim(a, x * local, local, axis=dim))
     )
-    after_attn = own_tokens(after_all, 0)
-    normed_two_all, inv_two_all = normalize(after_all)
-    ln_two = (normed_two_all * gain_two + bias_two).astype(bf16)
-    pre_act = contract(ln_two, w_up, 1, 0) + b_up
-    gating = jax.nn.sigmoid(1.702 * pre_act)
-    activated = (pre_act * gating).astype(bf16)
-    slope = (gating + 1.702 * pre_act * gating * (1.0 - gating)).astype(bf16)
-
-    far_mlp, kept_mlp = move.far_terms(contract(activated, w_down, 1, 0))
-
-    terms_fc2 = contract(activated, all_grad, 0, 0).astype(bf16)
-    grad_pre = (contract(all_grad, w_down, 1, 1) * slope.astype(f32)).astype(bf16)
-    terms_fc1 = contract(ln_two, grad_pre, 0, 0).astype(bf16)
-    terms_ln_two = contract(grad_pre, w_up, 1, 1)
-    sum_fc2, grad_ln_two = move.sums([terms_fc2], terms_ln_two, 3)
-    normed_two, inv_two = own_tokens(normed_two_all, 0), own_tokens(inv_two_all, 0)
+
+    terms_fc1, terms_b_up, grad_ln_two, far_mlp, kept_mlp, sum_fc2 = move.mlp_back(
+        all_grad, ln_two, w_down, w_up, slope, activated, terms_fc2
+    )
+    normed_two, inv_two = normalize(after_attn)
     grad_out = own_grad.astype(f32)
     grad_after = grad_out + norm_back(grad_ln_two * gain_two, normed_two, inv_two)
     grad_proj_in = grad_after.astype(bf16)
@@ -1056,11 +1328,11 @@
         jnp.sum(terms_ln_one * normed_all, axis=0),
         jnp.sum(terms_ln_one, axis=0),
         jnp.sum(grad_proj_in.astype(f32), axis=0),
-        jnp.sum(terms_ln_two * normed_two_all, axis=0),
-        jnp.sum(terms_ln_two, axis=0),
+        jnp.sum(grad_ln_two * normed_two, axis=0),
+        jnp.sum(grad_ln_two, axis=0),
         jnp.sum(grad_out, axis=0),
         spread(jnp.sum(grad_qkv_t.astype(f32), axis=1).reshape(3, inner), (3, seq, inner), 1),
-        spread(jnp.sum(grad_pre.astype(f32), axis=0).reshape(fsdp, cut), (fsdp, seq, cut), 1),
+        spread(terms_b_up.reshape(fsdp, cut), (fsdp, seq, cut), 1),
     )
     qk_vector, v_vector = jnp.split(grad_vectors[6], (2 * width,))
     grad_vectors = grad_vectors[:6] + (qk_vector, v_vector) + grad_vectors[7:]

time: 479 us -> 418 us (0.87)
  matrix products: 112 us -> 33.8 us
  Pallas kernels: 297 us -> 333 us
  local copies, waits for them, and re-layouts: 30.4 us -> 15.8 us
    pallas_call x1 -> x3, Pallas kernels: 38.5 us -> 148 us  [the longest x1 59 us: mlp_back(): pl.pallas_call(mlp_back_kernel, grid=(2 * tiles,), in_specs=[whole((lengt...]
    dot_general x12 -> x5, matrix products: 112 us -> 33.8 us  [contract(): lax.dot_general(left, right, (((left_dim,), (right_dim,)), ((), ())), pre...]
    pallas_call x2 -> x1, Pallas kernels: 96.9 us -> 55.3 us  [exchange(): pl.pallas_call(functools.partial(exchange_kernel, len(grads), len(away),...]
    pallas_call x1, Pallas kernels: 99.4 us -> 69.9 us  [attend(): pl.pallas_call(attend_send_kernel if blocks else attend_kernel, grid=(hea...]
where the time goes in v3:
time: 418 us; the launch traced here: 414 us
  Pallas kernels  333 us (80%)
  matrix products  33.8 us (8%)
  other arithmetic  29.9 us (7%)
  local copies, waits for them, and re-layouts  15.8 us (4%)
    pallas_call x1, Pallas kernels, attend(): pl.pallas_call(attend_send_kernel if blocks else attend_kernel, grid=(hea...  69.9 us
    pallas_call x1, Pallas kernels, mlp_back(): pl.pallas_call(mlp_back_kernel, grid=(2 * tiles,), in_specs=[whole((lengt...  59 us
    pallas_call x1, Pallas kernels, attend_back(): pl.pallas_call(kernel, grid=(heads,), in_specs=in_specs, out_specs=out_sp...  56.8 us
    pallas_call x1, Pallas kernels, exchange(): pl.pallas_call(functools.partial(exchange_kernel, len(grads), len(away),...  55.3 us
    pallas_call x1, Pallas kernels, mlp(): pl.pallas_call(mlp_kernel, grid=(parts + tiles,), in_specs=[pl.BlockSpec(...  50.9 us
    pallas_call x1, Pallas kernels, first_exchange(): pl.pallas_call(first_kernel, in_specs=[anywhere] * 5, out_specs=[anywhere...  38.5 us
    dot_general x5, matrix products, contract(): lax.dot_general(left, right, (((left_dim,), (right_dim,)), ((), ())), pre...  33.8 us

profile of v3, /device:TPU:0, one launch (start us, length us, event | category | flops | bytes accessed | tf_op | source)
XLA Modules:
  0.0 414.2 jit_solution(4828846838849726619)
XLA Ops:
  0.7 1.4 pad_add_fusion.ids_ref
  2.0 1.4 fusion.12.vec_ref
  3.5 38.5 %shard_map.271 = (bf16[2,512,1280]{2,1,0:T(8,128)(2,1)}, s32[2,2,512]{2,1,0:T(2,128)}, bf16[4,2,2,80,1920]{4,3,2,1,0:T(8,128)(2,1)}, bf16[4,2,2,16,128]{4,3,2,1,0:T(8,128)(2,1)}, bf16[80,2560]{1,0:T(8,128)(2,1)}) custom-call(bf16[512,1280]{1,0:T(8,128)(2,1)} %bitcast.71, s32[2,512]{1,0:T(2,128)} %pad_add_fusion.ids_ref, bf16[80,3840]{1,0:T(8,128)(2,1)} %qkv_ref.1, ...), custom_call_target="tpu_custom_call" | custom-call | bytes 120000000 | tf_op jit(solution)/shard_map/pallas_call | solution.py:516
  45.0 2.2 convert_reduce_fusion.1
  49.1 2.3 copy-done.23
  51.4 8.4 %broadcast_add_fusion = f32[1920,1024]{1,0:T(8,128)} fusion(f32[1920]{0:T(1024)S(1)} %add.147, bf16[1280,1920]{1,0:T(8,128)(2,1)S(1)} %bitcast.81, bf16[1024,1280]{1,0:T(8,128)(2,1)S(1)} %bitcast.68), kind=kOutput, calls=%fused_computation.13 | convolution fusion | flops 5035130880 | bytes 15408640 | tf_op jit(solution)/shard_map/dot_general | solution.py:20
  60.0 1.9 fusion.10
  62.0 69.9 %shard_map.272 = (bf16[3,640,1024]{2,1,0:T(8,128)(2,1)}, bf16[8,1024,1024]{2,1,0:T(8,128)(2,1)}, bf16[2,8,80,1024]{3,2,1,0:T(8,128)(2,1)}, bf16[4,2,2,80,1280]{4...) custom-call(f32[3,640,1024]{2,1,0:T(8,128)} %bitcast.82, ...), custom_call_target="tpu_custom_call" | custom-call | flops 13421772800 | bytes 29884416 | tf_op jit(solution)/shard_map/pallas_call | solution.py:156
  135.3 50.9 %shard_map.273 = (f32[512,1280]{1,0:T(8,128)}, bf16[1024,1280]{1,0:T(8,128)(2,1)}, bf16[1024,2560]{1,0:T(8,128)(2,1)}, bf16[1024,2560]{1,0:T(8,128)(2,1)}, bf16[...) custom-call(bf16[1280,1024]{1,0:T(8,128)(2,1)} %bitcast.90, bf16[1280,1280]{1,0:T(8,128)(2,1)} %bitcast.88, ...), custom_call_target="tpu_custom_call" | custom-call | flops 13421772800 | bytes 60000000 | tf_op jit(solution)/shard_map/pallas_call | solution.py:788
  186.2 59.0 %shard_map.274 = (bf16[1280,2560]{1,0:T(8,128)(2,1)}, f32[1,2560]{1,0:T(1,128)}, f32[512,1280]{1,0:T(8,128)}, bf16[512,1280]{1,0:T(8,128)(2,1)}, f32[512,1280]{1,0:T(8,128)}, /*index=5*/bf16[160,1280]{1,0:T(8,128)(2,1)}) custom-call(bf16[1024,1280]{1,0:T(8,128)(2,1)} %bitcast.93, bf16[1024,1280]{1,0:T(8,128)(2,1)} %get-tuple-element.61.ln_ref, ...), custom_call_target="tpu_custom_call" | custom-call | flops 26843545600 | bytes 100000000 | tf_op jit(solution)/shard_map/pallas_call | solution.py:952
  245.9 2.9 multiply_reduce_fusion.2
  248.9 1.8 convert_reduce_fusion.3
  250.8 3.0 convolution_convert_fusion.2
  253.8 56.8 %shard_map.275 = (bf16[3,640,1024]{2,1,0:T(8,128)(2,1)}, bf16[80,2560]{1,0:T(8,128)(2,1)}, bf16[160,1280]{1,0:T(8,128)(2,1)}, bf16[512,1280]{1,0:T(8,128)(2,1)}) custom-call(bf16[3,640,1024]{2,1,0:T(8,128)(2,1)} %get-tuple-element.67.rot_ref, bf16[8,1024,1024]{2,1,0:T(8,128)(2,1)} %get-tuple-element.68.probs_ref, f32[80,1024]{1,0:T(8,128)} %get-tuple-element.100.cos_ref, ...), custom_call_target="tpu_custom_call" | custom-call | flops 21474836480 | bytes 27262976 | tf_op jit(solution)/shard_map/pallas_call | solution.py:315
  310.7 3.8 fusion.7
  315.3 11.3 %fusion.17 = (f32[1280]{0:T(1024)S(1)}, f32[1280]{0:T(1024)S(1)}, f32[1024,1280]{1,0:T(8,128)}, f32[1024,1280]{1,0:T(8,128)}) fusion(f32[1024]{0:T(1024)S(1)} %bitcast.78, f32[1024]{0:T(1024)S(1)} %bitcast.79, bf16[2,512,1280]{2,1,0:T(8,128)(2,1)S(1)} %copy-done.10, bf16[1920,1024]{1,0:T(8,128)(2,1)S(1)} %bitcast.65, bf16[1280,1920]{1,0:T(8,128)(2,1)} %bitcast.80), kind=kOutput, calls=%fused_computation.62 | convolution fusion | flops 5041027072 | bytes 21972992 | tf_op jit(solution)/shard_map/dot_general | solution.py:20
  326.5 3.6 convolution_convert_fusion.1
  330.1 7.5 %convolution_convert_fusion = bf16[1280,1920]{1,0:T(8,128)(2,1)} fusion(bf16[1024,1280]{1,0:T(8,128)(2,1)S(1)} %bitcast.69, bf16[1920,1024]{1,0:T(8,128)(2,1)S(1)} %bitcast.66), kind=kOutput, calls=%fused_computation.1 | convolution fusion | flops 5035622400 | bytes 11468800 | tf_op jit(solution)/shard_map/dot_general | solution.py:20
  338.1 2.7 convert_reduce_fusion
  342.3 2.9 slice.158.refs_3_
  345.2 55.3 %shard_map.276 = (bf16[2,80,1280]{2,1,0:T(8,128)(2,1)}, bf16[2,80,1920]{2,1,0:T(8,128)(2,1)}, f32[2,16,128]{2,1,0:T(8,128)}, bf16[512,1280]{1,0:T(8,128)(2,1)}, bf16[80,2560]{1,0:T(8,128)(2,1)}) custom-call(bf16[4,2,2,80,1280]{4,3,2,1,0:T(8,128)(2,1)} %bitcast.67, bf16[4,2,2,80,1920]{4,3,2,1,0:T(8,128)(2,1)} %bitcast.64, f32[4,2,2,16,128]{4,3,2,1,0:T(8,128)} %bitcast.72, ...), custom_call_target="tpu_custom_call" | custom-call | bytes 120000000 | tf_op jit(solution)/shard_map/pallas_call | solution.py:709
  400.5 3.7 fusion.9
  404.3 5.0 %add_bitcast_fusion = f32[1,512,1280]{2,1,0:T(8,128)} fusion(f32[512,1280]{1,0:T(8,128)S(1)} %copy-done.13, f32[1024,1280]{1,0:T(8,128)} %get-tuple-element.97, f32[512]{0:T(512)S(1)} %broadcast_multiply_fusion.2, f32[512]{0:T(512)S(1)} %broadcast_multiply_fusion.3, f32[512]{0:T(512)S(1)} %bitcast.77, f32[1280]{0:T(1024)S(1)} %mul.128, ...), kind=kLoop, calls=%fused_computation.20 | loop fusion | flops 5242880 | bytes 11807744 | tf_op jit(solution)/shard_map/broadcast_in_dim | solution.py:1360
  409.9 2.8 shard_map.277
  (117 shorter events, 13.8 us)
Async XLA Ops:
  0.6 133.8 %copy-start = (bf16[320,1280]{1,0:T(8,128)(2,1)S(1)}, bf16[320,1280]{1,0:T(8,128)(2,1)}, u32[]{:S(2)}) copy-start(bf16[320,1280]{1,0:T(8,128)(2,1)} %param.29) | copy-start | bytes 2457604
  42.0 5.1 %copy-start.9 = (bf16[2,512,1280]{2,1,0:T(8,128)(2,1)S(1)}, bf16[2,512,1280]{2,1,0:T(8,128)(2,1)}, u32[]{:S(2)}) copy-start(bf16[2,512,1280]{2,1,0:T(8,128)(2,1)} %get-tuple-element.52) | copy-start | bytes 7864324
  48.0 3.3 copy-start.23
  49.1 10.7 %copy-start.16 = (bf16[2,512,1280]{2,1,0:T(8,128)(2,1)}, bf16[2,512,1280]{2,1,0:T(8,128)(2,1)S(1)}, u32[]{:S(2)}) copy-start(bf16[2,512,1280]{2,1,0:T(8,128)(2,1)S(1)} %fusion.5) | copy-start | bytes 7864324
  51.4 8.4 %copy-start.22 = (s32[2,2,512]{2,1,0:T(2,128)S(1)}, s32[2,2,512]{2,1,0:T(2,128)}, u32[]{:S(2)}) copy-start(s32[2,2,512]{2,1,0:T(2,128)} %get-tuple-element.54) | copy-start | bytes 24580
  186.2 59.0 %copy-start.8 = (f32[512,1280]{1,0:T(8,128)S(1)}, f32[512,1280]{1,0:T(8,128)}, u32[]{:S(2)}) copy-start(f32[512,1280]{1,0:T(8,128)} %get-tuple-element.60) | copy-start | bytes 7864324
  245.9 3.0 copy-start.11
  245.9 3.0 copy-start.18
  250.7 3.1 copy-start.12
  310.7 3.8 copy-start.10
  310.7 4.6 %copy-start.15 = (bf16[3,640,1024]{2,1,0:T(8,128)(2,1)S(1)}, bf16[3,640,1024]{2,1,0:T(8,128)(2,1)}, u32[]{:S(2)}) copy-start(bf16[3,640,1024]{2,1,0:T(8,128)(2,1)} %get-tuple-element.74) | copy-start | bytes 11796484
  315.3 11.3 %copy-start.13 = (f32[512,1280]{1,0:T(8,128)S(1)}, f32[512,1280]{1,0:T(8,128)}, u32[]{:S(2)}) copy-start(f32[512,1280]{1,0:T(8,128)} %copy-done.12) | copy-start | bytes 7864324
  315.3 11.3 %copy-start.25 = (bf16[2,8,80,1024]{3,2,1,0:T(8,128)(2,1)S(1)}, bf16[2,8,80,1024]{3,2,1,0:T(8,128)(2,1)}, u32[]{:S(2)}) copy-start(bf16[2,8,80,1024]{3,2,1,0:T(8,128)(2,1)} %get-tuple-element.56) | copy-start | bytes 7864324
  326.5 3.6 copy-start.17
  337.7 3.4 copy-start.21
  400.5 3.7 copy-start.14
  404.2 5.0 %copy-start.20 = (f32[2,16,128]{2,1,0:T(8,128)S(1)}, f32[2,16,128]{2,1,0:T(8,128)}, u32[]{:S(2)}) copy-start(f32[2,16,128]{2,1,0:T(8,128)} %get-tuple-element.78) | copy-start | bytes 49156
  404.3 5.6 %copy-start.2 = (bf16[80,2560]{1,0:T(8,128)(2,1)S(1)}, bf16[80,2560]{1,0:T(8,128)(2,1)}, u32[]{:S(2)}) copy-start(bf16[80,2560]{1,0:T(8,128)(2,1)} %get-tuple-element.76.refs_4_.fc1_ref) | copy-start | bytes 1228804
  404.3 5.6 %copy-start.3 = (bf16[2,80,1920]{2,1,0:T(8,128)(2,1)S(1)}, bf16[2,80,1920]{2,1,0:T(8,128)(2,1)}, u32[]{:S(2)}) copy-start(bf16[2,80,1920]{2,1,0:T(8,128)(2,1)} %get-tuple-element.79.qkv_ref) | copy-start | bytes 1843204
  404.3 5.6 %copy-start.4 = (bf16[160,1280]{1,0:T(8,128)(2,1)S(1)}, bf16[160,1280]{1,0:T(8,128)(2,1)}, u32[]{:S(2)}) copy-start(bf16[160,1280]{1,0:T(8,128)(2,1)} %get-tuple-element.71.away_ref.fc2_ref) | copy-start | bytes 1228804
  404.3 5.6 %copy-start.5 = (bf16[160,1280]{1,0:T(8,128)(2,1)S(1)}, bf16[160,1280]{1,0:T(8,128)(2,1)}, u32[]{:S(2)}) copy-start(bf16[160,1280]{1,0:T(8,128)(2,1)} %get-tuple-element.82.fc2_far_ref) | copy-start | bytes 1228804
  404.3 5.6 %copy-start.6 = (bf16[2,80,1280]{2,1,0:T(8,128)(2,1)S(1)}, bf16[2,80,1280]{2,1,0:T(8,128)(2,1)}, u32[]{:S(2)}) copy-start(bf16[2,80,1280]{2,1,0:T(8,128)(2,1)} %get-tuple-element.80.proj_ref) | copy-start | bytes 1228804
  404.3 5.6 %copy-start.7 = (bf16[80,2560]{1,0:T(8,128)(2,1)S(1)}, bf16[80,2560]{1,0:T(8,128)(2,1)}, u32[]{:S(2)}) copy-start(bf16[80,2560]{1,0:T(8,128)(2,1)} %get-tuple-element.81.fc1_far_ref) | copy-start | bytes 1228804
  404.3 9.7 %copy-start.1 = (bf16[320,1280]{1,0:T(8,128)(2,1)S(1)}, bf16[320,1280]{1,0:T(8,128)(2,1)}, u32[]{:S(2)}) copy-start(bf16[320,1280]{1,0:T(8,128)(2,1)} %param.29) | copy-start | bytes 2457604
  (2 other events, 2.6 us)
